TPU v7x, 128 devices: a whole 4x4x4 slice. The times are simulated.
128 devices in a mesh: ctx: 16 (over z, x), tp: 8 (over y, core).
Axes of the slice: x: 4, y: 4, z: 4, core: 2. Of those that a mesh axis runs over, the one named last changes fastest.
Arguments:
- queries: bfloat16 [16384, 8192], P('ctx', 'tp'), may hold values from -6 to 6
- key_proj: bfloat16 [16384, 8192], P('ctx', 'tp'), may hold values from -6 to 6
- values: bfloat16 [16384, 8192], P('ctx', 'tp'), may hold values from -6 to 6
- gate_input: bfloat16 [16384, 8192], P('ctx', 'tp'), may hold values from -8 to 8
- norm_gain: float32 [8192], P('tp'), may hold values from 0.1 to 1.9
- out_weight: bfloat16 [8192, 6144], P('tp'), may hold values from -0.0625 to 0.0625
Outputs:
- layer_out: bfloat16 [16384, 6144], P('ctx', 'tp')
All inputs are finite; a program needn't handle non-finite values.
Results may differ from a plain program's by a relative error of at most 0.02.
Values may be sent and summed in bfloat16 or wider, within the bound.
No kernel may reach another device: no remote copies, remote signals or barrier semaphores. Data moves between devices by JAX's collectives and lax.ppermute only.
A program may use at most 128 MiB of HBM per device.

v0:
```python
import jax
import jax.numpy as jnp
from jax import lax
from jax.sharding import PartitionSpec as P

DH = 128


def carried_in(shard, axis, combine, identity):
    devices, position = (lax.axis_size(axis), lax.axis_index(axis))
    everything = lax.all_gather(shard.astype(jnp.bfloat16), axis)
    start = jnp.broadcast_to(jnp.asarray(identity, shard.dtype), shard.shape)

    def lap(k, before):
        reached = k < position
        new = combine(before, everything[k].astype(shard.dtype))
        return jnp.where(reached, new, before)

    return lax.fori_loop(0, devices, lap, start)


def add_states(earlier, later):
    return earlier + later


def on_device(queries, key_proj, values, gate_input, norm_gain, out_weight):
    tok_rows = queries.shape[0]
    local_width = queries.shape[1]
    head_count = local_width // DH
    qfeat = jax.nn.silu(queries.astype(jnp.float32)).astype(jnp.bfloat16)
    kfeat = jax.nn.silu(key_proj.astype(jnp.float32)).astype(jnp.bfloat16)
    qheads = qfeat.reshape(tok_rows, head_count, DH)
    kheads = kfeat.reshape(tok_rows, head_count, DH)
    vheads = values.reshape(tok_rows, head_count, DH)
    local_state = jnp.einsum("thd,the->hde", kheads, vheads, preferred_element_type=jnp.float32)
    zeros_state = jnp.zeros_like(local_state)
    prefix = carried_in(local_state, "ctx", add_states, zeros_state)
    causal = jnp.arange(tok_rows)[:, None] >= jnp.arange(tok_rows)[None, :]
    scores = jnp.einsum("thd,shd->hts", qheads, kheads, preferred_element_type=jnp.float32)
    scores = jnp.where(causal[None], scores, 0.0).astype(jnp.bfloat16)
    intra = jnp.einsum("hts,she->the", scores, vheads, preferred_element_type=jnp.float32)
    inter = jnp.einsum(
        "thd,hde->the", qheads.astype(jnp.float32), prefix, precision=lax.Precision.HIGHEST
    )
    attn = intra + inter
    meansq = jnp.mean(attn * attn, axis=-1, keepdims=True)
    normed = (attn / jnp.sqrt(meansq + 1e-06)).reshape(tok_rows, local_width)
    hidden = (normed * norm_gain[None, :] * jax.nn.sigmoid(gate_input.astype(jnp.float32))).astype(
        jnp.bfloat16
    )
    partial_value = jnp.dot(hidden, out_weight, preferred_element_type=jnp.float32)
    summed = lax.psum_scatter(
        partial_value.astype(jnp.bfloat16), "tp", scatter_dimension=1, tiled=True
    )
    return summed


def solution(mesh):
    return jax.shard_map(
        on_device,
        mesh=mesh,
        in_specs=(
            P("ctx", "tp"),
            P("ctx", "tp"),
            P("ctx", "tp"),
            P("ctx", "tp"),
            P("tp"),
            P("tp", None),
        ),
        out_specs=P("ctx", "tp"),
        check_vma=False,
    )
```

profile of v0, /device:TPU:0, one launch (start us, length us, event | category | flops | bytes accessed | tf_op | source)
XLA Modules:
  0.0 224.5 jit_solution(17029751467733295346)
XLA Ops:
  6.5 0.0 copy-start
  6.5 0.0 all-gather.3.cloned.1.call-start
  6.5 4.3 %fusion.12 = bf16[1024,1024]{1,0:T(8,128)(2,1)} fusion(bf16[1024,1024]{1,0:T(8,128)(2,1)} %param.9), kind=kLoop, calls=%fused_computation.18 | loop fusion | flops 6291456 | bytes 4194304 | tf_op jit(solution)/shard_map/convert_element_type | solution.py:31
  10.8 3.9 %copy.20 = bf16[1024,1024]{0,1:T(8,128)(2,1)} copy(bf16[1024,1024]{1,0:T(8,128)(2,1)} %fusion.12) | data formatting | bytes 4194304 | tf_op jit(solution)/shard_map/reshape | solution.py:33
  14.7 0.0 copy-done
  14.7 3.1 %fusion.28 = bf16[8,128,128]{2,1,0:T(8,128)(2,1)} fusion(bf16[1024,8,128]{0,2,1:T(8,128)(2,1)} %bitcast.48, bf16[1024,1024]{1,0:T(8,128)(2,1)S(1)} %copy-done), kind=kOutput, calls=%fused_computation.37 | convolution fusion | flops 268566528 | bytes 4456448 | tf_op jit(solution)/shard_map/thd,the->hde/dot_general | solution.py:35
  17.8 0.0 all-gather.3.cloned.1.call-update
  17.8 0.0 reduce-scatter.2.cloned.1.call-start
  17.9 1.3 iota_compare_fusion
  19.2 52.9 %all-gather.3.cloned.1.call-done = bf16[128,128,128]{2,1,0:T(8,128)(2,1)} async-done(((bf16[8,128,128]{2,1,0:T(8,128)(2,1)}), bf16[128,128,128]{2,1,0:T(8,128)(2,1)}) %all-gather.3.cloned.1.call-update) | async-done | bytes 4194320 | tf_op jit(solution)/shard_map/all_gather | solution.py:11
  72.1 20.1 %while.14 = (s32[]{:T(128)}, f32[8,128,128]{2,1,0:T(8,128)S(1)}, s32[]{:T(128)}, bf16[16,8,128,128]{3,2,1,0:T(8,128)(2,1)}, s32[]{:T(128)}, /*index=5*/s32[]{:T(128)}) while((s32[]{:T(128)}, f32[8,128,128]{2,1,0:T(8,128)S(1)}, s32[]{:T(128)}, bf16[16,8,128,128]{3,2,1,0:T(8,128)(2,1)}, s32[]{:T(128)}, /*index=5*/s32[]{:T(128)}) %tuple.40), condition=%wide.region_1.2_spmd.clone, body=%wide.region_0.1_spmd.clone.sunk | while | flops 524292 | bytes 1310821 | solution.py:19
  72.1 1.2 add_select_fusion.2
  73.4 1.2 add_select_fusion.2
  74.6 1.2 add_select_fusion.2
  75.9 1.2 add_select_fusion.2
  77.2 1.2 add_select_fusion.2
  78.4 1.2 add_select_fusion.2
  79.7 1.2 add_select_fusion.2
  80.9 1.2 add_select_fusion.2
  82.2 1.2 add_select_fusion.2
  83.4 1.2 add_select_fusion.2
  84.7 1.2 add_select_fusion.2
  86.0 1.2 add_select_fusion.2
  87.2 1.2 add_select_fusion.2
  88.5 1.2 add_select_fusion.2
  89.7 1.2 add_select_fusion.2
  91.0 1.2 add_select_fusion.2
  92.2 6.3 %fusion.19 = f32[8,128,1024]{2,1,0:T(8,128)} fusion(f32[8,128,128]{2,1,0:T(8,128)S(1)} %get-tuple-element.84, bf16[1024,1024]{1,0:T(8,128)(2,1)} %param.8), kind=kOutput, calls=%fused_computation.28 | convolution fusion | flops 1616904192 | bytes 6815744 | tf_op jit(solution)/shard_map/thd,hde->the/dot_general | solution.py:42
  98.5 14.8 %multiply_reduce_fusion = (f32[1024,8]{0,1:T(8,128)S(1)}, f32[1024,8,128]{0,2,1:T(8,128)}) fusion(f32[8,128,1024]{2,1,0:T(8,128)} %fusion.19, pred[1024,1024]{1,0:T(8,128)(4,1)} %iota_compare_fusion, bf16[1024,8,128]{0,2,1:T(8,128)(2,1)} %bitcast.49, bf16[1024,1024]{1,0:T(8,128)(2,1)S(1)} %copy-done, bf16[1024,1024]{1,0:T(8,128)(2,1)} %param.8), kind=kOutput, calls=%fused_computation.21 | convolution fusion | flops 4321173504 | bytes 15761408 | tf_op jit(solution)/shard_map/hts,she->the/dot_general | solution.py:41
  113.3 5.0 %broadcast_divide_fusion = f32[1024,8,128]{0,2,1:T(8,128)} fusion(f32[1024,8,128]{0,2,1:T(8,128)} %get-tuple-element.109, f32[1024,8]{0,1:T(8,128)S(1)} %add_sqrt_fusion), kind=kLoop, calls=%fused_computation.31 | loop fusion | flops 1048576 | bytes 8421376 | tf_op jit(solution)/shard_map/div | solution.py:47
  118.3 0.0 copy-start.1
  118.3 5.4 %copy.18 = f32[1024,1024]{1,0:T(8,128)} copy(f32[1024,1024]{0,1:T(8,128)} %bitcast.47) | data formatting | bytes 8388608 | tf_op jit(solution)/shard_map/reshape | solution.py:47
  123.7 0.0 copy-done.1
  123.7 21.8 %convolution_convert_fusion = bf16[1024,6144]{1,0:T(8,128)(2,1)} fusion(bf16[1024,6144]{1,0:T(8,128)(2,1)} %param.13, bf16[1024,1024]{1,0:T(8,128)(2,1)} %param.11, f32[1024,1024]{1,0:T(8,128)} %copy.18, f32[1024]{0:T(1024)S(1)} %copy-done.1), kind=kOutput, calls=%fused_computation.5 | convolution fusion | flops 12898533376 | bytes 31461376 | tf_op jit(solution)/shard_map/dot_general | solution.py:51
  145.5 0.0 reduce-scatter.2.cloned.1.call-update
  145.5 72.1 %reduce-scatter.2.cloned.1.call-done = bf16[1024,768]{1,0:T(8,128)(2,1)} async-done(((bf16[1024,6144]{1,0:T(8,128)(2,1)}), bf16[1024,768]{1,0:T(8,128)(2,1)}) %reduce-scatter.2.cloned.1.call-update) | async-done | bytes 1572880 | tf_op jit(solution)/shard_map/reduce_scatter | solution.py:52
  (2 shorter events, 0.0 us)
Async XLA Ops:
  6.5 8.2 %copy-start = (bf16[1024,1024]{1,0:T(8,128)(2,1)S(1)}, bf16[1024,1024]{1,0:T(8,128)(2,1)}, u32[]{:S(2)}) copy-start(bf16[1024,1024]{1,0:T(8,128)(2,1)} %param.10) | copy-start | bytes 6291460
  6.5 65.6 %all-gather.3.cloned.1.call-start = ((), (), s32[]{:S(2)}) async-start(), calls=%async_computation.2 | async-start | bytes 4456448 | tf_op jit(solution)/shard_map/all_gather | solution.py:11
  17.8 199.8 %reduce-scatter.2.cloned.1.call-start = ((), (), s32[]{:S(2)}) async-start(), calls=%async_computation.1 | async-start | bytes 14155776 | tf_op jit(solution)/shard_map/reduce_scatter | solution.py:52
  118.3 5.4 %copy-start.1 = (f32[1024]{0:T(1024)S(1)}, f32[1024]{0:T(1024)}, u32[]{:S(2)}) copy-start(f32[1024]{0:T(1024)} %param.12) | copy-start | bytes 12292
Sparse Core Ops, SparseCore 0:
  18.0 54.1 all-gather.2
  145.6 71.9 reduce-scatter.1
where the time goes:
time: 225 us; the launch traced here: 224 us
  waiting for transfers between devices  125 us (56%)
  matrix products  45.9 us (20%)
  other arithmetic  30.4 us (14%)
  between operations  13.4 us (6%)
  local copies, waits for them, and re-layouts  9.28 us (4%)
    reduce_scatter x1, waiting for transfers between devices, on_device(): lax.psum_scatter(partial_value.astype(jnp.bfloat16), 'tp', scatter_dimens...  72.1 us
    all_gather x1, waiting for transfers between devices, carried_in(): everything = lax.all_gather(shard.astype(jnp.bfloat16), axis)  52.9 us
    dot_general x1, matrix products, on_device(): jnp.dot(hidden, out_weight, preferred_element_type=jnp.float32)  21.8 us
    select_n x16, other arithmetic, lap(): return jnp.where(reached, new, before)  19.8 us
    dot_general x1, matrix products, on_device(): jnp.einsum('hts,she->the', scores, vheads, preferred_element_type=jnp.flo...  14.8 us
    dot_general x1, matrix products, on_device(): jnp.einsum('thd,hde->the', qheads.astype(jnp.float32), prefix, precision=...  6.31 us
    reshape x1, local copies, waits for them, and re-layouts, on_device(): normed = (attn / jnp.sqrt(meansq + 1e-06)).reshape(tok_rows, local_width)  5.36 us
    div x1, other arithmetic, on_device(): normed = (attn / jnp.sqrt(meansq + 1e-06)).reshape(tok_rows, local_width)  5.03 us
  transfers between devices with their start and end apart: 2, of which 2 were waited for; matrix products, arithmetic and copies ran while one was open for 1% of the time, Pallas kernels for 0%

commit v1 on v0

v1 whole, which is shorter than its diff:
```python
import functools

import jax
import jax.numpy as jnp
from jax import lax
from jax.experimental import pallas as pl
from jax.experimental.pallas import tpu as pltpu
from jax.sharding import PartitionSpec as P

DH = 128
N_X = 4
N_Z = 4
N_Y = 4
CHUNK = 256
F32 = jnp.float32
BF16 = jnp.bfloat16
ROW_BLOCK = 128


def shift_x(k):
    return [(z * N_X + x, z * N_X + (x + k) % N_X) for z in range(N_Z) for x in range(N_X)]


def later_z(k):
    return [(z * N_X + x, (z + k) * N_X + x) for z in range(N_Z - k) for x in range(N_X)]


def shift_y(k):
    return [(y * 2 + c, ((y + k) % N_Y) * 2 + c) for y in range(N_Y) for c in range(2)]


OTHER_CORE = [(i, i ^ 1) for i in range(2 * N_Y)]


def sigmoid(x):
    return 0.5 * jnp.tanh(0.5 * x) + 0.5


def feature(x):
    wide = x.astype(F32)
    return (wide * sigmoid(wide)).astype(BF16)


def call(kernel, vmem=24, **kwargs):
    compiler_params = pltpu.CompilerParams(vmem_limit_bytes=vmem << 20)
    cost = pl.CostEstimate(flops=1, bytes_accessed=1, transcendentals=0)
    return pl.pallas_call(kernel, compiler_params=compiler_params, cost_estimate=cost, **kwargs)


def in_hbm(x):
    return pltpu.with_memory_space_constraint(x, pltpu.HBM)


def in_vmem(x):
    return pltpu.with_memory_space_constraint(x, pltpu.VMEM)


def state_kernel(k_ref, v_ref, state_ref):
    for h in range(k_ref.shape[1] // DH):
        cols = slice(h * DH, (h + 1) * DH)
        kf = feature(k_ref[:, cols])
        state = lax.dot_general(kf, v_ref[:, cols], (((0,), (0,)), ((), ())), preferred_element_type=F32)
        state_ref[cols, :] = state.astype(BF16)


def local_states(keys, values):
    rows, width = keys.shape
    block = 2 * DH
    spec = pl.BlockSpec((rows, block), lambda i: (0, i))
    return call(
        state_kernel,
        name="local_states",
        grid=(width // block,),
        in_specs=[spec, spec],
        out_specs=pl.BlockSpec((block, DH), lambda i: (i, 0)),
        out_shape=jax.ShapeDtypeStruct((width, DH), BF16),
    )(in_hbm(keys), in_hbm(values))


def split(x):
    high = x.astype(BF16)
    return high, (x - high.astype(F32)).astype(BF16)


def two_part_dot(q, high, low):
    return jnp.dot(
        jnp.concatenate([q, q], axis=1), jnp.concatenate([high, low], axis=0), preferred_element_type=F32
    )


def intra_kernel(q_ref, k_ref, v_ref, after_ref, intra_ref, qfeat_ref):
    rows = q_ref.shape[0]
    t = lax.broadcasted_iota(jnp.int32, (CHUNK, CHUNK), 0)
    s = lax.broadcasted_iota(jnp.int32, (CHUNK, CHUNK), 1)
    causal = s <= t
    for h in range(q_ref.shape[1] // DH):
        cols = slice(h * DH, (h + 1) * DH)
        state = jnp.zeros((DH, DH), F32)
        for i in range(rows // CHUNK):
            here = slice(i * CHUNK, (i + 1) * CHUNK)
            q, k, v = feature(q_ref[here, cols]), feature(k_ref[here, cols]), v_ref[here, cols]
            qfeat_ref[here, cols] = q
            scores = lax.dot_general(q, k, (((1,), (1,)), ((), ())), preferred_element_type=F32)
            scores = jnp.where(causal, scores, 0.0).astype(BF16)
            out = jnp.dot(scores, v, preferred_element_type=F32)
            if i:
                out += two_part_dot(q, *split(state))
            intra_ref[here, cols] = out
            if (i + 1) * CHUNK < rows:
                state += lax.dot_general(k, v, (((0,), (0,)), ((), ())), preferred_element_type=F32)


def intra_block(queries, keys, values, after):
    rows, width = keys.shape
    block = 2 * DH
    spec = pl.BlockSpec((rows, block), lambda i: (0, i))
    return call(
        intra_kernel,
        name="intra_block",
        grid=(width // block,),
        in_specs=[spec] * 3 + [pl.BlockSpec(memory_space=pl.ANY)],
        out_specs=[spec] * 2,
        out_shape=[
            pltpu.VMEM((rows, width), F32),
            pltpu.VMEM((rows, width), BF16),
        ],
    )(in_hbm(queries), in_hbm(keys), in_hbm(values), *after)


def hidden_kernel(n_parts, *refs):
    intra_ref, qfeat_ref, gate_ref, gain_ref = refs[:4]
    part_refs, hidden_ref, both_ref = refs[4 : 4 + n_parts], refs[-2], refs[-1]
    width = intra_ref.shape[1]

    @pl.when(pl.program_id(0) == 0)
    def _():
        prefix = part_refs[0][...].astype(F32)
        for ref in part_refs[1:]:
            prefix += ref[...].astype(F32)
        high, low = split(prefix)
        for h in range(width // DH):
            both_ref[h, :DH, :] = high[h * DH : (h + 1) * DH]
            both_ref[h, DH:, :] = low[h * DH : (h + 1) * DH]

    for h in range(width // DH):
        cols = slice(h * DH, (h + 1) * DH)
        q = qfeat_ref[:, cols]
        inter = jnp.dot(jnp.concatenate([q, q], axis=1), both_ref[h], preferred_element_type=F32)
        attn = intra_ref[:, cols] + inter
        scale = lax.rsqrt(jnp.mean(attn * attn, axis=-1, keepdims=True) + 1e-06)
        gate = sigmoid(gate_ref[:, cols].astype(F32))
        hidden_ref[:, cols] = (attn * scale * gain_ref[:, cols] * gate).astype(BF16)


def hidden_rows(part, intra, qfeat, gate_input, gain, parts, after):
    rows, width = intra.shape
    steps = rows // 2 // ROW_BLOCK
    spec = pl.BlockSpec((ROW_BLOCK, width), lambda i: (i // (steps // 2) * steps + part * (steps // 2) + i % (steps // 2), 0))
    return call(
        functools.partial(hidden_kernel, len(parts)),
        name="hidden_rows",
        grid=(steps,),
        in_specs=[spec, spec, spec, pl.BlockSpec((1, width), lambda i: (0, 0))]
        + [pl.BlockSpec((width, DH), lambda i: (0, 0))] * len(parts)
        + [pl.BlockSpec(memory_space=pl.ANY)] * len(after),
        out_specs=pl.BlockSpec((ROW_BLOCK, width), lambda i: (i, 0)),
        out_shape=pltpu.VMEM((rows // 2, width), BF16),
        scratch_shapes=[pltpu.VMEM((width // DH, 2 * DH, DH), BF16)],
    )(in_vmem(intra), in_vmem(qfeat), in_vmem(gate_input), gain, *parts, *after)


def project_kernel(plan, n_hidden, n_adds, n_outs, n_after, blocks_ref, *refs):
    own, other = refs[:n_hidden], refs[n_hidden : 2 * n_hidden]
    w_own, w_other = refs[2 * n_hidden : 2 * n_hidden + 2]
    adds = refs[2 * n_hidden + 2 : 2 * n_hidden + 2 + n_adds]
    outs = refs[len(refs) - n_outs :]
    steps = w_own.shape[1]
    for group, pieces in enumerate(plan):

        def work(pieces=pieces):
            cols = pl.ds(pl.multiple_of(lax.rem(pl.program_id(0), 3) * steps, steps), steps)
            for source, first, rows, terms, out, at in pieces:
                here = slice(first, first + rows)
                value = jnp.dot(own[source][here, :], w_own[...], preferred_element_type=F32)
                value += jnp.dot(other[source][here, :], w_other[...], preferred_element_type=F32)
                for term, term_first in terms:
                    value += adds[term][term_first : term_first + rows, cols].astype(F32)
                outs[out][at : at + rows, cols] = value.astype(outs[out].dtype)

        pl.when(pl.program_id(0) // 3 == group)(work)


def project(name, own, other, w_own, w_other, blocks, plan, outs, adds=(), after=()):
    third = w_own.shape[1] // (2 * N_Y) // 3
    depth = w_own.shape[0]
    whole = lambda a: pl.BlockSpec(memory_space=pltpu.VMEM)
    w_spec = pl.BlockSpec((depth, third), lambda i, b: (0, b[i // 3] * 3 + lax.rem(i, 3)))
    return call(
        functools.partial(project_kernel, plan, len(own), len(adds), len(outs), len(after)),
        name=name,
        grid_spec=pltpu.PrefetchScalarGridSpec(
            num_scalar_prefetch=1,
            grid=(3 * len(plan),),
            in_specs=[whole(h) for h in own]
            + [whole(h) for h in other]
            + [w_spec, w_spec]
            + [whole(a) for a in adds]
            + [pl.BlockSpec(memory_space=pl.ANY)] * len(after),
            out_specs=[pl.BlockSpec(memory_space=pltpu.VMEM) for _ in outs],
        ),
        out_shape=[pltpu.VMEM((n, 3 * third), dtype) for n, dtype in outs],
    )(blocks, *map(in_vmem, own + other), in_hbm(w_own), in_hbm(w_other), *map(in_vmem, adds), *after)


def finish_kernel(top_ref, bottom_ref, top_add_ref, bottom_add_ref, out_ref):
    half = top_ref.shape[0]
    out_ref[:half, :] = (top_ref[...] + top_add_ref[...].astype(F32)).astype(BF16)
    out_ref[half:, :] = (bottom_ref[...] + bottom_add_ref[...].astype(F32)).astype(BF16)


def finish(*halves):
    rows, width = halves[0].shape
    block = width // 2
    return call(
        finish_kernel,
        name="finish",
        grid=(2,),
        in_specs=[pl.BlockSpec((rows, block), lambda i: (0, i))] * 4,
        out_specs=pl.BlockSpec((2 * rows, block), lambda i: (0, i)),
        out_shape=jax.ShapeDtypeStruct((2 * rows, width), BF16),
    )(*map(in_vmem, halves))


def on_device(queries, key_proj, values, gate_input, norm_gain, out_weight):
    rows, width = queries.shape
    half, quarter = rows // 2, rows // 4
    x = lax.rem(lax.axis_index("ctx"), N_X)
    y, core = lax.axis_index("tp") // 2, lax.rem(lax.axis_index("tp"), 2)
    gain = norm_gain[None, :]
    blocks = [((y + k) % N_Y * 2 + core).astype(jnp.int32) for k in range(N_Y)]

    other_weight = lax.ppermute(out_weight, "tp", OTHER_CORE)
    state = local_states(key_proj, values)
    along_x = [lax.ppermute(state, "ctx", shift_x(k)) for k in (1, 3, 2)]
    intra, qfeat = intra_block(queries, key_proj, values, [state])
    total = state.astype(F32)
    earlier = jnp.zeros_like(total)
    for k, part in zip((1, 3, 2), along_x):
        wide = part.astype(F32)
        total += wide
        earlier += jnp.where(k <= x, wide, 0.0)
    total = total.astype(BF16)
    along_z = [lax.ppermute(total, "ctx", later_z(k)) for k in (1, 2, 3)]
    parts = [earlier, *along_z]

    swap = lambda a: lax.ppermute(a, "tp", OTHER_CORE)
    up = lambda a: lax.ppermute(a, "tp", shift_y(1))
    down = lambda a: lax.ppermute(a, "tp", shift_y(-1))
    own = [hidden_rows(0, intra, qfeat, gate_input, gain, parts, [])]
    own.append(hidden_rows(1, intra, qfeat, gate_input, gain, parts, own))
    other = [swap(own[0]), swap(own[1])]

    far = (((0, 0, quarter, (), 0, 0), (0, quarter, quarter, (), 1, 0)),)
    far_up, far_down, last = [], [], own[1]
    for i in range(2):
        top, bottom = project(
            "share_far", own[i : i + 1], other[i : i + 1], out_weight, other_weight, blocks[2][None],
            far, [(quarter, BF16)] * 2, after=[last],
        )
        far_up.append(up(top))
        far_down.append(down(bottom))
        last = top

    near_blocks = jnp.stack([blocks[1], blocks[3]])
    near = tuple(
        tuple((i, part * quarter, quarter, (), g, i * quarter) for i in range(2)) for g, part in ((0, 1), (1, 0))
    )
    up_share, down_share = project(
        "share_near", own, other, out_weight, other_weight, near_blocks, near, [(half, BF16)] * 2,
        after=[last, far_up[0], far_down[0]],
    )
    bottom_from_below, top_from_above = up(up_share), down(down_share)

    passing = tuple(
        tuple((i, part * quarter, quarter, ((2 * g + i, 0),), g, i * quarter) for i in range(2))
        for g, part in ((0, 0), (1, 1))
    )
    up_sum, down_sum = project(
        "share_passing", own, other, out_weight, other_weight, near_blocks, passing, [(half, BF16)] * 2,
        adds=[*far_up, *far_down], after=[up_share],
    )
    top_from_below, bottom_from_above = up(up_sum), down(down_sum)

    mine = (
        tuple(
            (i, part * quarter, quarter, ((part, i * quarter),), part, i * quarter) for part in range(2) for i in range(2)
        ),
    )
    top, bottom = project(
        "share_own", own, other, out_weight, other_weight, blocks[0][None], mine, [(half, F32)] * 2,
        adds=[top_from_above, bottom_from_below], after=[up_sum],
    )
    return finish(top, bottom, top_from_below, bottom_from_above)


def solution(mesh):
    return jax.shard_map(
        on_device,
        mesh=mesh,
        in_specs=(
            P("ctx", "tp"),
            P("ctx", "tp"),
            P("ctx", "tp"),
            P("ctx", "tp"),
            P("tp"),
            P("tp", None),
        ),
        out_specs=P("ctx", "tp"),
        check_vma=False,
    )
```

time: 225 us -> 115 us (0.51)
  waiting for transfers between devices: 125 us -> 32.6 us
  Pallas kernels: 0 us -> 53.6 us
  matrix products: 45.9 us -> 0 us
  other arithmetic: 30.4 us -> 0.3 us
  starting transfers between devices: 0.04 us -> 28.1 us
  between operations: 13.4 us -> 0.15 us
  local copies, waits for them, and re-layouts: 9.28 us -> 0.01 us
    reduce_scatter x1 -> x0, waiting for transfers between devices: 72.1 us -> none  [on_device(): lax.psum_scatter(partial_value.astype(jnp.bfloat16), 'tp', scatter_dimens...]
    pallas_call x0 -> x10, Pallas kernels: none -> 53.6 us  [the longest x5 33.9 us: project(): call(functools.partial(project_kernel, plan, len(own), len(adds), len(out...]
    all_gather x1 -> x0, waiting for transfers between devices: 52.9 us -> none  [carried_in(): everything = lax.all_gather(shard.astype(jnp.bfloat16), axis)]
    dot_general x4 -> x0, matrix products: 45.9 us -> none  [the longest x1 21.8 us: on_device(): jnp.dot(hidden, out_weight, preferred_element_type=jnp.float32)]
    ppermute x0 -> x17, waiting for transfers between devices: none -> 32.6 us  [the longest x4 12.8 us: on_device(): up = lambda a: lax.ppermute(a, 'tp', shift_y(1))]
    ppermute x0 -> x17, starting transfers between devices: none -> 28.1 us  [the longest x3 10.8 us: on_device(): along_z = [lax.ppermute(total, 'ctx', later_z(k)) for k in (1, 2, 3)]]
    select_n x16 -> x0, other arithmetic: 19.8 us -> none  [lap(): return jnp.where(reached, new, before)]
    reshape x2 -> x0, local copies, waits for them, and re-layouts: 9.27 us -> none  [the longest x1 5.36 us: on_device(): normed = (attn / jnp.sqrt(meansq + 1e-06)).reshape(tok_rows, local_width)]
  transfers between devices with their start and end apart: 2 -> 17, of which waited for: 2 -> 9; matrix products, arithmetic and copies ran while one was open for 1% -> 0% of each run, Pallas kernels for 0% -> 45%
where the time goes in v1:
time: 115 us
  Pallas kernels  53.6 us (47%)
  waiting for transfers between devices  32.6 us (28%)
  starting transfers between devices  28.1 us (24%)
    pallas_call x5, Pallas kernels, project(): call(functools.partial(project_kernel, plan, len(own), len(adds), len(out...  33.9 us
    ppermute x4, waiting for transfers between devices, on_device(): up = lambda a: lax.ppermute(a, 'tp', shift_y(1))  12.8 us
    ppermute x3, waiting for transfers between devices, on_device(): along_x = [lax.ppermute(state, 'ctx', shift_x(k)) for k in (1, 3, 2)]  11.5 us
    ppermute x3, starting transfers between devices, on_device(): along_z = [lax.ppermute(total, 'ctx', later_z(k)) for k in (1, 2, 3)]  10.8 us
    pallas_call x1, Pallas kernels, intra_block(): call(intra_kernel, name='intra_block', grid=(width // block,), in_specs=[...  9.49 us
    ppermute x4, starting transfers between devices, on_device(): down = lambda a: lax.ppermute(a, 'tp', shift_y(-1))  8.9 us
    ppermute x4, waiting for transfers between devices, on_device(): down = lambda a: lax.ppermute(a, 'tp', shift_y(-1))  8.04 us
    ppermute x3, starting transfers between devices, on_device(): along_x = [lax.ppermute(state, 'ctx', shift_x(k)) for k in (1, 3, 2)]  5.21 us
  transfers between devices with their start and end apart: 17, of which 9 were waited for; matrix products, arithmetic and copies ran while one was open for 0% of the time, Pallas kernels for 45%

profile of v1, /device:TPU:0, one launch (start us, length us, event | category | flops | bytes accessed | tf_op | source)
XLA Modules:
  0.0 114.8 jit_solution(4371893469174501496)
XLA Ops:
  0.0 0.0 collective-permute-start.8
  0.0 3.8 %local_states.1.after_ref = bf16[1024,128]{1,0:T(8,128)(2,1)S(1)} custom-call(bf16[1024,1024]{1,0:T(8,128)(2,1)} %k_ref.3, bf16[1024,1024]{1,0:T(8,128)(2,1)} %v_ref.3), custom_call_target="tpu_custom_call" | custom-call | flops 1 | bytes 1 | tf_op jit(solution)/shard_map/local_states/pallas_call | solution.py:70
  3.8 1.6 %collective-permute-start = (bf16[1024,128]{1,0:T(8,128)(2,1)S(1)}, bf16[1024,128]{1,0:T(8,128)(2,1)S(1)}, u32[]{:S(2)}, u32[]{:S(2)}) collective-permute-start(bf16[1024,128]{1,0:T(8,128)(2,1)S(1)} %local_states.1.after_ref), channel_id=1, source_target_pairs={{0,8},{8,16},{16,24},{24,0},{32,40},{40,48},{48,56},{56,32},{64,72... | collective-permute-start | bytes 786440 | tf_op jit(solution)/shard_map/ppermute | solution.py:244
  5.4 1.7 %collective-permute-start.1 = (bf16[1024,128]{1,0:T(8,128)(2,1)S(1)}, bf16[1024,128]{1,0:T(8,128)(2,1)S(1)}, u32[]{:S(2)}, u32[]{:S(2)}) collective-permute-start(bf16[1024,128]{1,0:T(8,128)(2,1)S(1)} %local_states.1.after_ref), channel_id=1, source_target_pairs={{0,24},{8,0},{16,8},{24,16},{32,56},{40,32},{48,40},{56,48},{64,88... | collective-permute-start | bytes 786440 | tf_op jit(solution)/shard_map/ppermute | solution.py:244
  7.1 1.9 %collective-permute-start.2 = (bf16[1024,128]{1,0:T(8,128)(2,1)S(1)}, bf16[1024,128]{1,0:T(8,128)(2,1)S(1)}, u32[]{:S(2)}, u32[]{:S(2)}) collective-permute-start(bf16[1024,128]{1,0:T(8,128)(2,1)S(1)} %local_states.1.after_ref), channel_id=1, source_target_pairs={{0,16},{8,24},{16,0},{24,8},{32,48},{40,56},{48,32},{56,40},{64,80... | collective-permute-start | bytes 786440 | tf_op jit(solution)/shard_map/ppermute | solution.py:244
  9.0 4.8 %collective-permute-done = bf16[1024,128]{1,0:T(8,128)(2,1)S(1)} collective-permute-done((bf16[1024,128]{1,0:T(8,128)(2,1)S(1)}, bf16[1024,128]{1,0:T(8,128)(2,1)S(1)}, u32[]{:S(2)}, u32[]{:S(2)}) %collective-permute-start) | collective-permute-done | bytes 262176 | tf_op jit(solution)/shard_map/ppermute | solution.py:244
  13.8 0.8 collective-permute-done.1
  14.6 5.9 %collective-permute-done.2 = bf16[1024,128]{1,0:T(8,128)(2,1)S(1)} collective-permute-done((bf16[1024,128]{1,0:T(8,128)(2,1)S(1)}, bf16[1024,128]{1,0:T(8,128)(2,1)S(1)}, u32[]{:S(2)}, u32[]{:S(2)}) %collective-permute-start.2) | collective-permute-done | bytes 262176 | tf_op jit(solution)/shard_map/ppermute | solution.py:244
  20.5 0.2 fusion.2
  20.7 0.0 copy-start
  20.7 0.0 copy-start.1
  20.7 4.0 %collective-permute-start.3 = (bf16[1024,128]{1,0:T(8,128)(2,1)S(1)}, bf16[1024,128]{1,0:T(8,128)(2,1)S(1)}, u32[]{:S(2)}, u32[]{:S(2)}) collective-permute-start(bf16[1024,128]{1,0:T(8,128)(2,1)S(1)} %get-tuple-element.29), channel_id=1, source_target_pairs={{0,32},{8,40},{16,48},{24,56},{32,64},{40,72},{48,80},{56,88},{64,... | collective-permute-start | bytes 786440 | tf_op jit(solution)/shard_map/ppermute | solution.py:253
  24.7 5.5 %collective-permute-start.4 = (bf16[1024,128]{1,0:T(8,128)(2,1)S(1)}, bf16[1024,128]{1,0:T(8,128)(2,1)S(1)}, u32[]{:S(2)}, u32[]{:S(2)}) collective-permute-start(bf16[1024,128]{1,0:T(8,128)(2,1)S(1)} %get-tuple-element.29), channel_id=1, source_target_pairs={{0,64},{8,72},{16,80},{24,88},{32,96},{40,104},{48,112},{56,120},{... | collective-permute-start | bytes 786440 | tf_op jit(solution)/shard_map/ppermute | solution.py:253
  30.2 1.3 %collective-permute-start.5 = (bf16[1024,128]{1,0:T(8,128)(2,1)S(1)}, bf16[1024,128]{1,0:T(8,128)(2,1)S(1)}, u32[]{:S(2)}, u32[]{:S(2)}) collective-permute-start(bf16[1024,128]{1,0:T(8,128)(2,1)S(1)} %get-tuple-element.29), channel_id=1, source_target_pairs={{0,96},{8,104},{16,112},{24,120},{1,97},{9,105},{17,113},{25,121},... | collective-permute-start | bytes 786440 | tf_op jit(solution)/shard_map/ppermute | solution.py:253
  31.5 9.5 %intra_block.1 = (f32[1024,1024]{1,0:T(8,128)S(1)}, bf16[1024,1024]{1,0:T(8,128)(2,1)S(1)}) custom-call(bf16[1024,1024]{1,0:T(8,128)(2,1)} %q_ref.1, bf16[1024,1024]{1,0:T(8,128)(2,1)} %k_ref.3, bf16[1024,1024]{1,0:T(8,128)(2,1)} %v_ref.3, bf16[1024,128]{1,0:T(8,128)(2,1)S(1)} %local_states.1.after_ref), custom_call_target="tpu_custom_call" | custom-call | flops 1 | bytes 1 | tf_op jit(solution)/shard_map/intra_block/pallas_call | solution.py:117
  41.0 0.0 collective-permute-done.3.refs_5_
  41.0 0.0 collective-permute-done.4.refs_6_
  41.0 0.0 collective-permute-done.5.refs_7_
  41.0 0.0 copy-done
  41.1 0.0 copy-done.1
  41.1 2.0 %hidden_rows.2.refs_8_.refs_0_ = bf16[512,1024]{1,0:T(8,128)(2,1)S(1)} custom-call(f32[1024,1024]{1,0:T(8,128)S(1)} %get-tuple-element.17.refs_0_, bf16[1024,1024]{1,0:T(8,128)(2,1)S(1)} %get-tuple-element.18.refs_1_, bf16[1024,1024]{1,0:T(8,128)(2,1)S(1)} %copy-done, f32[1,1024]{1,0:T(1,128)S(1)} %bitcast.5, f32[1024,128]{1,0:T(8,128)S(1)} %get-tuple-element.30.refs_4_, ...), custom_call_target="tpu_custom_call" | custom-call | flops 1 | bytes 1 | tf_op jit(solution)/shard_map/hidden_rows/pallas_call | solution.py:159
  43.1 0.1 collective-permute-start.6
  43.2 2.0 %hidden_rows.3.refs_4_.refs_0_.refs_1_ = bf16[512,1024]{1,0:T(8,128)(2,1)S(1)} custom-call(f32[1024,1024]{1,0:T(8,128)S(1)} %get-tuple-element.17.refs_0_, bf16[1024,1024]{1,0:T(8,128)(2,1)S(1)} %get-tuple-element.18.refs_1_, bf16[1024,1024]{1,0:T(8,128)(2,1)S(1)} %copy-done, f32[1,1024]{1,0:T(1,128)S(1)} %bitcast.6, ...), custom_call_target="tpu_custom_call" | custom-call | flops 1 | bytes 1 | tf_op jit(solution)/shard_map/hidden_rows/pallas_call | solution.py:159
  45.2 0.6 collective-permute-start.7
  45.7 0.2 collective-permute-done.6.refs_1_.refs_2_
  45.9 0.0 collective-permute-done.8.refs_3_.refs_5_
  45.9 5.1 %share_far.2 = (bf16[256,768]{1,0:T(8,128)(2,1)}, bf16[256,768]{1,0:T(8,128)(2,1)}) custom-call(s32[1]{0:T(128)} %bitcast.4.blocks_ref, bf16[512,1024]{1,0:T(8,128)(2,1)S(1)} %hidden_rows.2.refs_8_.refs_0_, bf16[512,1024]{1,0:T(8,128)(2,1)} %collective-permute-done.6.refs_1_.refs_2_, bf16[1024,6144]{1,0:T(8,128)(2,1)} %refs_4_.5, ...), custom_call_target="tpu_custom_call" | custom-call | flops 1 | bytes 1 | tf_op jit(solution)/shard_map/share_far/pallas_call | solution.py:198
  51.1 3.0 %collective-permute-start.10 = (bf16[256,768]{1,0:T(8,128)(2,1)}, bf16[256,768]{1,0:T(8,128)(2,1)S(1)}, u32[]{:S(2)}, u32[]{:S(2)}) collective-permute-start(bf16[256,768]{1,0:T(8,128)(2,1)} %get-tuple-element.21), channel_id=1, source_target_pairs={{0,6},{1,7},{2,0},{3,1},{4,2},{5,3},{6,4},{7,5},{8,14},{9,15},{10,... | collective-permute-start | bytes 1179656 | tf_op jit(solution)/shard_map/ppermute | solution.py:258
  54.1 0.0 collective-permute-start.9
  54.1 0.0 collective-permute-done.7.refs_1_.refs_3_
  54.1 4.8 %share_far.3 = (bf16[256,768]{1,0:T(8,128)(2,1)}, bf16[256,768]{1,0:T(8,128)(2,1)}) custom-call(s32[1]{0:T(128)} %bitcast.4.blocks_ref, bf16[512,1024]{1,0:T(8,128)(2,1)S(1)} %hidden_rows.3.refs_4_.refs_0_.refs_1_, bf16[512,1024]{1,0:T(8,128)(2,1)S(1)} %collective-permute-done.7.refs_1_.refs_3_, bf16[1024,6144]{1,0:T(8,128)(2,1)} %refs_4_.5, ...), custom_call_target="tpu_custom_call" | custom-call | flops 1 | bytes 1 | tf_op jit(solution)/shard_map/share_far/pallas_call | solution.py:198
  58.9 0.6 collective-permute-start.13
  59.4 2.7 %collective-permute-start.14 = (bf16[256,768]{1,0:T(8,128)(2,1)}, bf16[256,768]{1,0:T(8,128)(2,1)}, u32[]{:S(2)}, u32[]{:S(2)}) collective-permute-start(bf16[256,768]{1,0:T(8,128)(2,1)} %get-tuple-element.24), channel_id=1, source_target_pairs={{0,6},{1,7},{2,0},{3,1},{4,2},{5,3},{6,4},{7,5},{8,14},{9,15},{10,... | collective-permute-start | bytes 1179656 | tf_op jit(solution)/shard_map/ppermute | solution.py:258
  62.1 0.1 pad_add_fusion.blocks_ref
  62.2 1.7 %collective-permute-done.10.refs_8_ = bf16[256,768]{1,0:T(8,128)(2,1)S(1)} collective-permute-done((bf16[256,768]{1,0:T(8,128)(2,1)}, bf16[256,768]{1,0:T(8,128)(2,1)S(1)}, u32[]{:S(2)}, u32[]{:S(2)}) %collective-permute-start.10) | collective-permute-done | bytes 393248 | tf_op jit(solution)/shard_map/ppermute | solution.py:258
  63.9 3.7 %collective-permute-done.9.refs_7_.refs_6_ = bf16[256,768]{1,0:T(8,128)(2,1)} collective-permute-done((bf16[256,768]{1,0:T(8,128)(2,1)}, bf16[256,768]{1,0:T(8,128)(2,1)}, u32[]{:S(2)}, u32[]{:S(2)}) %collective-permute-start.9) | collective-permute-done | bytes 393248 | tf_op jit(solution)/shard_map/ppermute | solution.py:257
  67.6 8.8 %share_near.1 = (bf16[512,768]{1,0:T(8,128)(2,1)}, bf16[512,768]{1,0:T(8,128)(2,1)}) custom-call(s32[2]{0:T(128)S(1)} %pad_add_fusion.blocks_ref, bf16[512,1024]{1,0:T(8,128)(2,1)S(1)} %hidden_rows.2.refs_8_.refs_0_, bf16[512,1024]{1,0:T(8,128)(2,1)S(1)} %hidden_rows.3.refs_4_.refs_0_.refs_1_, bf16[512,1024]{1,0:T(8,128)(2,1)} %collective-permute-done.6.refs_1_.refs_2_, ...), custom_call_target="tpu_custom_call" | custom-call | flops 1 | bytes 1 | tf_op jit(solution)/shard_map/share_near/pallas_call | solution.py:198
  76.4 0.0 collective-permute-start.11
  76.4 2.0 %collective-permute-start.12 = (bf16[512,768]{1,0:T(8,128)(2,1)}, bf16[512,768]{1,0:T(8,128)(2,1)}, u32[]{:S(2)}, u32[]{:S(2)}) collective-permute-start(bf16[512,768]{1,0:T(8,128)(2,1)} %get-tuple-element.23.refs_10_), channel_id=1, source_target_pairs={{0,2},{1,3},{2,4},{3,5},{4,6},{5,7},{6,0},{7,1},{8,10},{9,11},{10,... | collective-permute-start | bytes 2359304 | tf_op jit(solution)/shard_map/ppermute | solution.py:257
  78.4 0.0 collective-permute-done.13.refs_7_
  78.5 0.0 collective-permute-done.14.refs_9_
  78.5 9.2 %share_passing.1 = (bf16[512,768]{1,0:T(8,128)(2,1)}, bf16[512,768]{1,0:T(8,128)(2,1)}) custom-call(s32[2]{0:T(128)S(1)} %pad_add_fusion.blocks_ref, bf16[512,1024]{1,0:T(8,128)(2,1)S(1)} %hidden_rows.2.refs_8_.refs_0_, bf16[512,1024]{1,0:T(8,128)(2,1)S(1)} %hidden_rows.3.refs_4_.refs_0_.refs_1_, bf16[512,1024]{1,0:T(8,128)(2,1)} %collective-permute-done.6.refs_1_.refs_2_, ...), custom_call_target="tpu_custom_call" | custom-call | flops 1 | bytes 1 | tf_op jit(solution)/shard_map/share_passing/pallas_call | solution.py:198
  87.6 0.0 collective-permute-start.15
  87.6 3.2 %collective-permute-start.16 = (bf16[512,768]{1,0:T(8,128)(2,1)}, bf16[512,768]{1,0:T(8,128)(2,1)}, u32[]{:S(2)}, u32[]{:S(2)}) collective-permute-start(bf16[512,768]{1,0:T(8,128)(2,1)} %get-tuple-element.28), channel_id=1, source_target_pairs={{0,6},{1,7},{2,0},{3,1},{4,2},{5,3},{6,4},{7,5},{8,14},{9,15},{10,... | collective-permute-start | bytes 2359304 | tf_op jit(solution)/shard_map/ppermute | solution.py:258
  90.9 6.3 %collective-permute-done.11.refs_6_ = bf16[512,768]{1,0:T(8,128)(2,1)} collective-permute-done((bf16[512,768]{1,0:T(8,128)(2,1)}, bf16[512,768]{1,0:T(8,128)(2,1)}, u32[]{:S(2)}, u32[]{:S(2)}) %collective-permute-start.11) | collective-permute-done | bytes 786464 | tf_op jit(solution)/shard_map/ppermute | solution.py:258
  97.2 1.2 %collective-permute-done.12.refs_7_ = bf16[512,768]{1,0:T(8,128)(2,1)} collective-permute-done((bf16[512,768]{1,0:T(8,128)(2,1)}, bf16[512,768]{1,0:T(8,128)(2,1)}, u32[]{:S(2)}, u32[]{:S(2)}) %collective-permute-start.12) | collective-permute-done | bytes 786464 | tf_op jit(solution)/shard_map/ppermute | solution.py:257
  98.4 6.0 %share_own.1 = (f32[512,768]{1,0:T(8,128)S(1)}, f32[512,768]{1,0:T(8,128)S(1)}) custom-call(s32[1]{0:T(128)} %bitcast.blocks_ref, bf16[512,1024]{1,0:T(8,128)(2,1)S(1)} %hidden_rows.2.refs_8_.refs_0_, bf16[512,1024]{1,0:T(8,128)(2,1)S(1)} %hidden_rows.3.refs_4_.refs_0_.refs_1_, bf16[512,1024]{1,0:T(8,128)(2,1)} %collective-permute-done.6.refs_1_.refs_2_, ...), custom_call_target="tpu_custom_call" | custom-call | flops 1 | bytes 1 | tf_op jit(solution)/shard_map/share_own/pallas_call | solution.py:198
  104.4 7.9 %collective-permute-done.15.top_add_ref = bf16[512,768]{1,0:T(8,128)(2,1)} collective-permute-done((bf16[512,768]{1,0:T(8,128)(2,1)}, bf16[512,768]{1,0:T(8,128)(2,1)}, u32[]{:S(2)}, u32[]{:S(2)}) %collective-permute-start.15) | collective-permute-done | bytes 786464 | tf_op jit(solution)/shard_map/ppermute | solution.py:257
  112.3 0.0 collective-permute-done.16.bottom_add_ref
  112.3 2.5 %finish.1 = bf16[1024,768]{1,0:T(8,128)(2,1)} custom-call(f32[512,768]{1,0:T(8,128)S(1)} %get-tuple-element.26.top_ref, f32[512,768]{1,0:T(8,128)S(1)} %get-tuple-element.27.bottom_ref, bf16[512,768]{1,0:T(8,128)(2,1)} %collective-permute-done.15.top_add_ref, bf16[512,768]{1,0:T(8,128)(2,1)} %collective-permute-done.16.bottom_add_ref), custom_call_target="tpu_custom_call" | custom-call | flops 1 | bytes 1 | tf_op jit(solution)/shard_map/finish/pallas_call | solution.py:224
Async XLA Ops:
  0.0 45.9 %collective-permute-start.8 = (bf16[1024,6144]{1,0:T(8,128)(2,1)}, bf16[1024,6144]{1,0:T(8,128)(2,1)}, u32[]{:S(2)}, u32[]{:S(2)}) collective-permute-start(bf16[1024,6144]{1,0:T(8,128)(2,1)} %refs_4_.5), channel_id=1, source_target_pairs={{0,1},{1,0},{2,3},{3,2},{4,5},{5,4},{6,7},{7,6},{8,9},{9,8},{10,11... | collective-permute-start | bytes 37748744 | tf_op jit(solution)/shard_map/ppermute | solution.py:242
  3.8 10.0 %collective-permute-start = (bf16[1024,128]{1,0:T(8,128)(2,1)S(1)}, bf16[1024,128]{1,0:T(8,128)(2,1)S(1)}, u32[]{:S(2)}, u32[]{:S(2)}) collective-permute-start(bf16[1024,128]{1,0:T(8,128)(2,1)S(1)} %local_states.1.after_ref), channel_id=1, source_target_pairs={{0,8},{8,16},{16,24},{24,0},{32,40},{40,48},{48,56},{56,32},{64,72... | collective-permute-start | bytes 786440 | tf_op jit(solution)/shard_map/ppermute | solution.py:244
  5.4 9.1 %collective-permute-start.1 = (bf16[1024,128]{1,0:T(8,128)(2,1)S(1)}, bf16[1024,128]{1,0:T(8,128)(2,1)S(1)}, u32[]{:S(2)}, u32[]{:S(2)}) collective-permute-start(bf16[1024,128]{1,0:T(8,128)(2,1)S(1)} %local_states.1.after_ref), channel_id=1, source_target_pairs={{0,24},{8,0},{16,8},{24,16},{32,56},{40,32},{48,40},{56,48},{64,88... | collective-permute-start | bytes 786440 | tf_op jit(solution)/shard_map/ppermute | solution.py:244
  7.1 13.4 %collective-permute-start.2 = (bf16[1024,128]{1,0:T(8,128)(2,1)S(1)}, bf16[1024,128]{1,0:T(8,128)(2,1)S(1)}, u32[]{:S(2)}, u32[]{:S(2)}) collective-permute-start(bf16[1024,128]{1,0:T(8,128)(2,1)S(1)} %local_states.1.after_ref), channel_id=1, source_target_pairs={{0,16},{8,24},{16,0},{24,8},{32,48},{40,56},{48,32},{56,40},{64,80... | collective-permute-start | bytes 786440 | tf_op jit(solution)/shard_map/ppermute | solution.py:244
  20.7 20.3 %copy-start = (bf16[1024,1024]{1,0:T(8,128)(2,1)S(1)}, bf16[1024,1024]{1,0:T(8,128)(2,1)}, u32[]{:S(2)}) copy-start(bf16[1024,1024]{1,0:T(8,128)(2,1)} %refs_2_.5) | copy-start | bytes 6291460
  20.7 20.3 %copy-start.1 = (f32[1024]{0:T(1024)S(1)}, f32[1024]{0:T(1024)}, u32[]{:S(2)}) copy-start(f32[1024]{0:T(1024)} %param.10) | copy-start | bytes 12292
  20.7 20.3 %collective-permute-start.3 = (bf16[1024,128]{1,0:T(8,128)(2,1)S(1)}, bf16[1024,128]{1,0:T(8,128)(2,1)S(1)}, u32[]{:S(2)}, u32[]{:S(2)}) collective-permute-start(bf16[1024,128]{1,0:T(8,128)(2,1)S(1)} %get-tuple-element.29), channel_id=1, source_target_pairs={{0,32},{8,40},{16,48},{24,56},{32,64},{40,72},{48,80},{56,88},{64,... | collective-permute-start | bytes 786440 | tf_op jit(solution)/shard_map/ppermute | solution.py:253
  24.7 16.3 %collective-permute-start.4 = (bf16[1024,128]{1,0:T(8,128)(2,1)S(1)}, bf16[1024,128]{1,0:T(8,128)(2,1)S(1)}, u32[]{:S(2)}, u32[]{:S(2)}) collective-permute-start(bf16[1024,128]{1,0:T(8,128)(2,1)S(1)} %get-tuple-element.29), channel_id=1, source_target_pairs={{0,64},{8,72},{16,80},{24,88},{32,96},{40,104},{48,112},{56,120},{... | collective-permute-start | bytes 786440 | tf_op jit(solution)/shard_map/ppermute | solution.py:253
  30.2 10.8 %collective-permute-start.5 = (bf16[1024,128]{1,0:T(8,128)(2,1)S(1)}, bf16[1024,128]{1,0:T(8,128)(2,1)S(1)}, u32[]{:S(2)}, u32[]{:S(2)}) collective-permute-start(bf16[1024,128]{1,0:T(8,128)(2,1)S(1)} %get-tuple-element.29), channel_id=1, source_target_pairs={{0,96},{8,104},{16,112},{24,120},{1,97},{9,105},{17,113},{25,121},... | collective-permute-start | bytes 786440 | tf_op jit(solution)/shard_map/ppermute | solution.py:253
  43.1 2.9 %collective-permute-start.6 = (bf16[512,1024]{1,0:T(8,128)(2,1)S(1)}, bf16[512,1024]{1,0:T(8,128)(2,1)}, u32[]{:S(2)}, u32[]{:S(2)}) collective-permute-start(bf16[512,1024]{1,0:T(8,128)(2,1)S(1)} %hidden_rows.2.refs_8_.refs_0_), channel_id=1, source_target_pairs={{0,1},{1,0},{2,3},{3,2},{4,5},{5,4},{6,7},{7,6},{8,9},{9,8},{10,11... | collective-permute-start | bytes 3145736 | tf_op jit(solution)/shard_map/ppermute | solution.py:256
  45.2 8.9 %collective-permute-start.7 = (bf16[512,1024]{1,0:T(8,128)(2,1)S(1)}, bf16[512,1024]{1,0:T(8,128)(2,1)S(1)}, u32[]{:S(2)}, u32[]{:S(2)}) collective-permute-start(bf16[512,1024]{1,0:T(8,128)(2,1)S(1)} %hidden_rows.3.refs_4_.refs_0_.refs_1_), channel_id=1, source_target_pairs={{0,1},{1,0},{2,3},{3,2},{4,5},{5,4},{6,7},{7,6},{8,9},{9,8},{10,11... | collective-permute-start | bytes 3145736 | tf_op jit(solution)/shard_map/ppermute | solution.py:256
  51.1 12.8 %collective-permute-start.10 = (bf16[256,768]{1,0:T(8,128)(2,1)}, bf16[256,768]{1,0:T(8,128)(2,1)S(1)}, u32[]{:S(2)}, u32[]{:S(2)}) collective-permute-start(bf16[256,768]{1,0:T(8,128)(2,1)} %get-tuple-element.21), channel_id=1, source_target_pairs={{0,6},{1,7},{2,0},{3,1},{4,2},{5,3},{6,4},{7,5},{8,14},{9,15},{10,... | collective-permute-start | bytes 1179656 | tf_op jit(solution)/shard_map/ppermute | solution.py:258
  54.1 13.5 %collective-permute-start.9 = (bf16[256,768]{1,0:T(8,128)(2,1)}, bf16[256,768]{1,0:T(8,128)(2,1)}, u32[]{:S(2)}, u32[]{:S(2)}) collective-permute-start(bf16[256,768]{1,0:T(8,128)(2,1)} %get-tuple-element.19.refs_4_), channel_id=1, source_target_pairs={{0,2},{1,3},{2,4},{3,5},{4,6},{5,7},{6,0},{7,1},{8,10},{9,11},{10,... | collective-permute-start | bytes 1179656 | tf_op jit(solution)/shard_map/ppermute | solution.py:257
  58.9 19.6 %collective-permute-start.13 = (bf16[256,768]{1,0:T(8,128)(2,1)}, bf16[256,768]{1,0:T(8,128)(2,1)}, u32[]{:S(2)}, u32[]{:S(2)}) collective-permute-start(bf16[256,768]{1,0:T(8,128)(2,1)} %get-tuple-element.20.refs_6_), channel_id=1, source_target_pairs={{0,2},{1,3},{2,4},{3,5},{4,6},{5,7},{6,0},{7,1},{8,10},{9,11},{10,... | collective-permute-start | bytes 1179656 | tf_op jit(solution)/shard_map/ppermute | solution.py:257
  59.4 19.0 %collective-permute-start.14 = (bf16[256,768]{1,0:T(8,128)(2,1)}, bf16[256,768]{1,0:T(8,128)(2,1)}, u32[]{:S(2)}, u32[]{:S(2)}) collective-permute-start(bf16[256,768]{1,0:T(8,128)(2,1)} %get-tuple-element.24), channel_id=1, source_target_pairs={{0,6},{1,7},{2,0},{3,1},{4,2},{5,3},{6,4},{7,5},{8,14},{9,15},{10,... | collective-permute-start | bytes 1179656 | tf_op jit(solution)/shard_map/ppermute | solution.py:258
  76.4 20.8 %collective-permute-start.11 = (bf16[512,768]{1,0:T(8,128)(2,1)}, bf16[512,768]{1,0:T(8,128)(2,1)}, u32[]{:S(2)}, u32[]{:S(2)}) collective-permute-start(bf16[512,768]{1,0:T(8,128)(2,1)} %get-tuple-element.22), channel_id=1, source_target_pairs={{0,6},{1,7},{2,0},{3,1},{4,2},{5,3},{6,4},{7,5},{8,14},{9,15},{10,... | collective-permute-start | bytes 2359304 | tf_op jit(solution)/shard_map/ppermute | solution.py:258
  76.4 22.0 %collective-permute-start.12 = (bf16[512,768]{1,0:T(8,128)(2,1)}, bf16[512,768]{1,0:T(8,128)(2,1)}, u32[]{:S(2)}, u32[]{:S(2)}) collective-permute-start(bf16[512,768]{1,0:T(8,128)(2,1)} %get-tuple-element.23.refs_10_), channel_id=1, source_target_pairs={{0,2},{1,3},{2,4},{3,5},{4,6},{5,7},{6,0},{7,1},{8,10},{9,11},{10,... | collective-permute-start | bytes 2359304 | tf_op jit(solution)/shard_map/ppermute | solution.py:257
  87.6 24.7 %collective-permute-start.15 = (bf16[512,768]{1,0:T(8,128)(2,1)}, bf16[512,768]{1,0:T(8,128)(2,1)}, u32[]{:S(2)}, u32[]{:S(2)}) collective-permute-start(bf16[512,768]{1,0:T(8,128)(2,1)} %get-tuple-element.25.refs_8_), channel_id=1, source_target_pairs={{0,2},{1,3},{2,4},{3,5},{4,6},{5,7},{6,0},{7,1},{8,10},{9,11},{10,... | collective-permute-start | bytes 2359304 | tf_op jit(solution)/shard_map/ppermute | solution.py:257
  87.6 24.7 %collective-permute-start.16 = (bf16[512,768]{1,0:T(8,128)(2,1)}, bf16[512,768]{1,0:T(8,128)(2,1)}, u32[]{:S(2)}, u32[]{:S(2)}) collective-permute-start(bf16[512,768]{1,0:T(8,128)(2,1)} %get-tuple-element.28), channel_id=1, source_target_pairs={{0,6},{1,7},{2,0},{3,1},{4,2},{5,3},{6,4},{7,5},{8,14},{9,15},{10,... | collective-permute-start | bytes 2359304 | tf_op jit(solution)/shard_map/ppermute | solution.py:258

commit v2 on v1

v2 whole, which is shorter than its diff:
```python
import functools

import jax
import jax.numpy as jnp
from jax import lax
from jax.experimental import pallas as pl
from jax.experimental.pallas import tpu as pltpu
from jax.sharding import PartitionSpec as P

DH = 128
N_X = 4
N_Z = 4
N_Y = 4
CHUNK = 256
F32 = jnp.float32
BF16 = jnp.bfloat16
FAR_ROWS = (256, 256)
PADDING = (0, 0)
BLOCK_ORDER = (2, 1, 3, 0)


def shift_x(k):
    return [(z * N_X + x, z * N_X + (x + k) % N_X) for z in range(N_Z) for x in range(N_X)]


def later_z(k):
    return [(z * N_X + x, (z + k) * N_X + x) for z in range(N_Z - k) for x in range(N_X)]


def shift_y(k):
    return [(y * 2 + c, ((y + k) % N_Y) * 2 + c) for y in range(N_Y) for c in range(2)]


OTHER_CORE = [(i, i ^ 1) for i in range(2 * N_Y)]


def sigmoid(x):
    return 0.5 * jnp.tanh(0.5 * x) + 0.5


def feature(x):
    wide = x.astype(F32)
    return (wide * sigmoid(wide)).astype(BF16)


def call(kernel, vmem=16, flops=1, **kwargs):
    compiler_params = pltpu.CompilerParams(vmem_limit_bytes=vmem << 20)
    cost = pl.CostEstimate(flops=flops, bytes_accessed=1, transcendentals=0)
    return pl.pallas_call(kernel, compiler_params=compiler_params, cost_estimate=cost, **kwargs)


def in_hbm(x):
    return pltpu.with_memory_space_constraint(x, pltpu.HBM)


def in_vmem(x):
    return pltpu.with_memory_space_constraint(x, pltpu.VMEM)


IN_VMEM = pl.BlockSpec(memory_space=pltpu.VMEM)
ANYWHERE = pl.BlockSpec(memory_space=pl.ANY)


def state_kernel(k_ref, v_ref, state_ref):
    for h in range(k_ref.shape[1] // DH):
        cols = slice(h * DH, (h + 1) * DH)
        kf = feature(k_ref[:, cols])
        state = lax.dot_general(kf, v_ref[:, cols], (((0,), (0,)), ((), ())), preferred_element_type=F32)
        state_ref[cols, :] = state.astype(BF16)


def local_states(keys, values):
    rows, width = keys.shape
    block = 2 * DH
    spec = pl.BlockSpec((rows, block), lambda i: (0, i))
    return call(
        state_kernel,
        name="local_states",
        grid=(width // block,),
        in_specs=[spec, spec],
        out_specs=pl.BlockSpec((block, DH), lambda i: (i, 0)),
        out_shape=jax.ShapeDtypeStruct((width, DH), BF16),
    )(in_hbm(keys), in_hbm(values))


def split(x):
    high = x.astype(BF16)
    return high, (x - high.astype(F32)).astype(BF16)


def two_part_dot(q, high, low):
    return jnp.dot(
        jnp.concatenate([q, q], axis=1), jnp.concatenate([high, low], axis=0), preferred_element_type=F32
    )


def intra_kernel(q_ref, k_ref, v_ref, after_ref, intra_ref, qfeat_ref):
    rows, block = q_ref.shape
    t = lax.broadcasted_iota(jnp.int32, (CHUNK, CHUNK), 0)
    s = lax.broadcasted_iota(jnp.int32, (CHUNK, CHUNK), 1)
    causal = s <= t
    for h in range(q_ref.shape[1] // DH):
        cols = slice(h * DH, (h + 1) * DH)
        out_cols = pl.ds(pl.multiple_of(pl.program_id(0) * block + h * DH, DH), DH)
        state = jnp.zeros((DH, DH), F32)
        for i in range(rows // CHUNK):
            here = slice(i * CHUNK, (i + 1) * CHUNK)
            q, k, v = feature(q_ref[here, cols]), feature(k_ref[here, cols]), v_ref[here, cols]
            qfeat_ref[here, out_cols] = q
            scores = lax.dot_general(q, k, (((1,), (1,)), ((), ())), preferred_element_type=F32)
            scores = jnp.where(causal, scores, 0.0).astype(BF16)
            out = jnp.dot(scores, v, preferred_element_type=F32)
            if i:
                out += two_part_dot(q, *split(state))
            intra_ref[here, out_cols] = out
            if (i + 1) * CHUNK < rows:
                state += lax.dot_general(k, v, (((0,), (0,)), ((), ())), preferred_element_type=F32)


def intra_block(queries, keys, values, after):
    rows, width = keys.shape
    block = 2 * DH
    spec = pl.BlockSpec((rows, block), lambda i: (0, i))
    return call(
        intra_kernel,
        name="intra_block",
        flops=10**11,
        grid=(width // block,),
        in_specs=[spec] * 3 + [ANYWHERE],
        out_specs=[IN_VMEM] * 2,
        out_shape=[
            pltpu.VMEM((rows, width), F32),
            pltpu.VMEM((rows, width), BF16),
        ],
    )(in_hbm(queries), in_hbm(keys), in_hbm(values), *after)


def sort_columns_kernel(blocks_ref, weight_ref, after_ref, far_ref, rest_ref, mine_ref):
    step = pl.program_id(0)

    @pl.when(step == 0)
    def _():
        far_ref[0] = weight_ref[...]

    @pl.when((step > 0) & (step < N_Y))
    def _():
        rest_ref[0] = weight_ref[...]

    @pl.when(step >= N_Y)
    def _():
        mine_ref[0] = weight_ref[...]


def sort_columns(weight, theirs, mine, after):
    rows, width = weight.shape
    block = (rows, width // (2 * N_Y))
    return call(
        sort_columns_kernel,
        vmem=24,
        name="sort_columns",
        grid_spec=pltpu.PrefetchScalarGridSpec(
            num_scalar_prefetch=1,
            grid=(2 * N_Y,),
            in_specs=[pl.BlockSpec(block, lambda i, b: (0, b[i])), ANYWHERE],
            out_specs=[
                pl.BlockSpec((1, *block), lambda i, b: (0, 0, 0)),
                pl.BlockSpec((1, *block), lambda i, b: (jnp.clip(i - 1, 0, N_Y - 2), 0, 0)),
                pl.BlockSpec((1, *block), lambda i, b: (jnp.maximum(i - N_Y, 0), 0, 0)),
            ],
        ),
        out_shape=[pltpu.HBM((n, *block), BF16) for n in (1, N_Y - 1, N_Y)],
    )(jnp.stack(theirs + mine), in_hbm(weight), *after)


def pass_kernel(*refs):
    pass


def settled(arrays, after):
    return call(
        pass_kernel,
        name="settled",
        in_specs=[IN_VMEM] * len(arrays) + [ANYWHERE] * len(after),
        out_specs=[IN_VMEM] * len(arrays),
        out_shape=[pltpu.VMEM(a.shape, a.dtype) for a in arrays],
        input_output_aliases={i: i for i in range(len(arrays))},
    )(*map(in_vmem, arrays), *after)


def hidden_kernel(n_parts, first, rows, *refs):
    intra_ref, qfeat_ref, gate_ref, gain_ref = refs[:4]
    part_refs, hidden_ref, both_ref = refs[4 : 4 + n_parts], refs[-2], refs[-1]
    tokens, width = intra_ref.shape

    prefix = part_refs[0][...].astype(F32)
    for ref in part_refs[1:]:
        prefix += ref[...].astype(F32)
    high, low = split(prefix)
    for h in range(width // DH):
        both_ref[h, :DH, :] = high[h * DH : (h + 1) * DH]
        both_ref[h, DH:, :] = low[h * DH : (h + 1) * DH]

    for part in range(2):
        here = slice(part * tokens // 2 + first, part * tokens // 2 + first + rows)
        there = slice(part * rows, (part + 1) * rows)
        for h in range(width // DH):
            cols = slice(h * DH, (h + 1) * DH)
            q = qfeat_ref[here, cols]
            inter = jnp.dot(jnp.concatenate([q, q], axis=1), both_ref[h], preferred_element_type=F32)
            attn = intra_ref[here, cols] + inter
            scale = lax.rsqrt(jnp.mean(attn * attn, axis=-1, keepdims=True) + 1e-06)
            gate = sigmoid(gate_ref[here, cols].astype(F32))
            hidden_ref[there, cols] = (attn * scale * gain_ref[:, cols] * gate).astype(BF16)


def hidden_rows(first, rows, intra, qfeat, gate_input, gain, parts, after):
    width = intra.shape[1]
    return call(
        functools.partial(hidden_kernel, len(parts), first, rows),
        name="hidden_rows",
        in_specs=[IN_VMEM] * (4 + len(parts)) + [ANYWHERE] * len(after),
        out_specs=IN_VMEM,
        out_shape=pltpu.VMEM((2 * rows, width), BF16),
        scratch_shapes=[pltpu.VMEM((width // DH, 2 * DH, DH), BF16)],
    )(*map(in_vmem, [intra, qfeat, gate_input, gain, *parts]), *after)


def project_kernel(blocks, plan, n_hidden, n_adds, n_outs, *refs):
    own, other = refs[:n_hidden], refs[n_hidden : 2 * n_hidden]
    w_own, w_other = refs[2 * n_hidden : 2 * n_hidden + 2]
    adds = refs[2 * n_hidden + 2 :][:n_adds]
    outs = refs[len(refs) - n_outs :]
    step = outs[0].shape[1] // 3
    ends = [max(piece[5] + piece[2] for pieces in plan for piece in pieces if piece[4] == out) for out in range(n_outs)]
    for (mine, theirs), pieces in zip(blocks, plan):
        for source, first, rows, terms, out, at in pieces:

            def third(i, _, mine=mine, theirs=theirs, source=source, first=first, rows=rows, terms=terms, out=out, at=at):
                cols = pl.ds(pl.multiple_of(i * step, step), step)
                here = slice(first, first + rows)
                value = jnp.dot(own[source][here, :], w_own[mine, :, cols], preferred_element_type=F32)
                value += jnp.dot(other[source][here, :], w_other[theirs, :, cols], preferred_element_type=F32)
                for term, term_first in terms:
                    value += adds[term][term_first : term_first + rows, cols].astype(F32)
                outs[out][at : at + rows, cols] = value.astype(outs[out].dtype)
                return 0

            lax.fori_loop(0, 3, third, 0)
    for out, end in zip(outs, ends):
        if end < out.shape[0]:
            out[end:, :] = jnp.zeros((out.shape[0] - end, out.shape[1]), out.dtype)


def project(name, own, other, w_own, w_other, blocks, plan, outs, adds=(), after=(), flops=1):
    width = w_own.shape[2]
    operands = [*own, *other, w_own, w_other, *adds]
    return call(
        functools.partial(project_kernel, blocks, plan, len(own), len(adds), len(outs)),
        name=name,
        flops=flops,
        in_specs=[IN_VMEM] * len(operands) + [ANYWHERE] * len(after),
        out_specs=[IN_VMEM] * len(outs),
        out_shape=[pltpu.VMEM((n, width), dtype) for n, dtype in outs],
    )(*map(in_vmem, operands), *after)


def finish_kernel(*refs):
    values, adds, out_ref = refs[:2], refs[2:4], refs[4]
    rows = out_ref.shape[0]
    step = pl.program_id(0)
    steps = values[0].shape[0] // rows
    here = pl.ds(pl.multiple_of(lax.rem(step, steps) * rows, rows), rows)
    for value, add, half in zip(values, adds, range(2)):

        @pl.when(step // steps == half)
        def _(value=value, add=add):
            out_ref[...] = (value[here, :] + add[here, :].astype(F32)).astype(BF16)


def finish(*halves):
    rows, width = halves[0].shape
    block = rows // 2
    return call(
        finish_kernel,
        name="finish",
        grid=(2 * rows // block,),
        in_specs=[IN_VMEM] * 4,
        out_specs=pl.BlockSpec((block, width), lambda i: (i, 0)),
        out_shape=jax.ShapeDtypeStruct((2 * rows, width), BF16),
    )(*map(in_vmem, halves))


def on_device(queries, key_proj, values, gate_input, norm_gain, out_weight):
    rows, width = queries.shape
    half = rows // 2
    firsts = (0, FAR_ROWS[0])
    x = lax.rem(lax.axis_index("ctx"), N_X)
    y, core = lax.axis_index("tp") // 2, lax.rem(lax.axis_index("tp"), 2)
    gain = norm_gain[None, :]
    mine = [((y + k) % N_Y * 2 + core).astype(jnp.int32) for k in BLOCK_ORDER]
    theirs = [((y + k) % N_Y * 2 + 1 - core).astype(jnp.int32) for k in BLOCK_ORDER]

    state = local_states(key_proj, values)
    along_x = [lax.ppermute(state, "ctx", shift_x(k)) for k in (2, 3, 1)]
    theirs_far, theirs_rest, own_weight = sort_columns(out_weight, theirs, mine, [state])
    swap = lambda a: lax.ppermute(a, "tp", OTHER_CORE)
    other_far, other_rest = swap(theirs_far), swap(theirs_rest)
    state, own_weight = lax.optimization_barrier((state, own_weight))
    intra, qfeat = intra_block(queries, key_proj, values, [state])
    total = state.astype(F32)
    earlier = jnp.zeros_like(total)
    for k, part in zip((2, 3, 1), along_x):
        wide = part.astype(F32)
        total += wide
        earlier += jnp.where(k <= x, wide, 0.0)
    total = total.astype(BF16)
    along_z = [lax.ppermute(total, "ctx", later_z(k)) for k in (2, 3, 1)]
    parts = [earlier, *along_z]

    up = lambda a: lax.ppermute(a, "tp", shift_y(1))
    down = lambda a: lax.ppermute(a, "tp", shift_y(-1))
    own = [hidden_rows(firsts[0], FAR_ROWS[0], intra, qfeat, gate_input, gain, parts, [other_rest])]
    own.append(hidden_rows(firsts[1], FAR_ROWS[1], intra, qfeat, gate_input, gain, parts, own))
    other = [swap(own[0]), swap(own[1])]

    far_up, far_down, last = [], [], own[1]
    for i, n in enumerate(FAR_ROWS):
        far = (((0, 0, n, (), 0, 0), (0, n, n, (), 1, 0)),)
        top, bottom = project(
            "share_far", own[i : i + 1], other[i : i + 1], own_weight, other_far, ((0, 0),),
            far, [(n + PADDING[i], BF16)] * 2, after=[last], flops=(10**11, 1)[i],
        )
        far_up.append(up(top))
        far_down.append(down(bottom))
        last = top

    def both(part, terms, out):
        return tuple((i, part * n, n, terms(i), out, firsts[i]) for i, n in enumerate(FAR_ROWS))

    near_blocks = ((1, 0), (2, 1))
    near = tuple(both(part, lambda i: (), g) for g, part in ((0, 1), (1, 0)))
    up_share, down_share = project(
        "share_near", own, other, own_weight, other_rest, near_blocks, near, [(half, BF16)] * 2,
        after=[last],
    )
    up_share, down_share = settled([up_share, down_share], [far_up[0], far_down[0]])
    bottom_from_below, top_from_above = up(up_share), down(down_share)

    passing = tuple(both(part, lambda i: ((2 * g + i, 0),), g) for g, part in ((0, 0), (1, 1)))
    up_sum, down_sum = project(
        "share_passing", own, other, own_weight, other_rest, near_blocks, passing, [(half, BF16)] * 2,
        adds=[*far_up, *far_down], after=[up_share], flops=10**11,
    )
    top_from_below, bottom_from_above = up(up_sum), down(down_sum)

    home = (both(0, lambda i: ((0, firsts[i]),), 0) + both(1, lambda i: ((1, firsts[i]),), 1),)
    top, bottom = project(
        "share_own", own, other, own_weight, other_rest, ((3, 2),), home, [(half, F32)] * 2,
        adds=[top_from_above, bottom_from_below], after=[up_sum],
    )
    return finish(top, bottom, top_from_below, bottom_from_above)


def solution(mesh):
    return jax.shard_map(
        on_device,
        mesh=mesh,
        in_specs=(
            P("ctx", "tp"),
            P("ctx", "tp"),
            P("ctx", "tp"),
            P("ctx", "tp"),
            P("tp"),
            P("tp", None),
        ),
        out_specs=P("ctx", "tp"),
        check_vma=False,
    )
```

time: 115 us -> 107 us (0.930)
  waiting for transfers between devices: 32.6 us -> 19.7 us
  Pallas kernels: 53.6 us -> 57.8 us
    ppermute x7 -> x6, waiting for transfers between devices: 11.5 us -> 0.02 us  [the longest x3 0.01 us: on_device(): along_x = [lax.ppermute(state, 'ctx', shift_x(k)) for k in (2, 3, 1)]]
    pallas_call x9 -> x11, Pallas kernels: 49.9 us -> 54 us  [the longest x5 29 us: project(): call(functools.partial(project_kernel, blocks, plan, len(own), len(adds),...]
    ppermute x4, waiting for transfers between devices: 12.8 us -> 10.5 us  [on_device(): up = lambda a: lax.ppermute(a, 'tp', shift_y(1))]
    ppermute x4, starting transfers between devices: 8.9 us -> 10.2 us  [on_device(): down = lambda a: lax.ppermute(a, 'tp', shift_y(-1))]
    ppermute x7 -> x6, starting transfers between devices: 16 us -> 15.3 us  [the longest x3 10.1 us: on_device(): along_z = [lax.ppermute(total, 'ctx', later_z(k)) for k in (2, 3, 1)]]
  transfers between devices with their start and end apart: 17 -> 18, of which waited for: 9 -> 7; matrix products, arithmetic and copies ran while one was open for 0% -> 0% of each run, Pallas kernels for 45% -> 49%
where the time goes in v2:
time: 107 us
  Pallas kernels  57.8 us (54%)
  starting transfers between devices  28.5 us (27%)
  waiting for transfers between devices  19.7 us (18%)
    pallas_call x5, Pallas kernels, project(): call(functools.partial(project_kernel, blocks, plan, len(own), len(adds),...  29 us
    pallas_call x1, Pallas kernels, sort_columns(): call(sort_columns_kernel, vmem=24, name='sort_columns', grid_spec=pltpu.P...  11.5 us
    ppermute x4, waiting for transfers between devices, on_device(): up = lambda a: lax.ppermute(a, 'tp', shift_y(1))  10.5 us
    ppermute x4, starting transfers between devices, on_device(): down = lambda a: lax.ppermute(a, 'tp', shift_y(-1))  10.2 us
    ppermute x3, starting transfers between devices, on_device(): along_z = [lax.ppermute(total, 'ctx', later_z(k)) for k in (2, 3, 1)]  10.1 us
    pallas_call x1, Pallas kernels, intra_block(): call(intra_kernel, name='intra_block', flops=10 ** 11, grid=(width // blo...  8.97 us
    ppermute x4, waiting for transfers between devices, on_device(): down = lambda a: lax.ppermute(a, 'tp', shift_y(-1))  8.45 us
    ppermute x3, starting transfers between devices, on_device(): along_x = [lax.ppermute(state, 'ctx', shift_x(k)) for k in (2, 3, 1)]  5.2 us
  transfers between devices with their start and end apart: 18, of which 7 were waited for; matrix products, arithmetic and copies ran while one was open for 0% of the time, Pallas kernels for 49%

profile of v2, /device:TPU:0, one launch (start us, length us, event | category | flops | bytes accessed | tf_op | source)
XLA Modules:
  0.0 106.5 jit_solution(11042517564617383895)
XLA Ops:
  0.0 3.8 %local_states.1.after_ref = bf16[1024,128]{1,0:T(8,128)(2,1)S(1)} custom-call(bf16[1024,1024]{1,0:T(8,128)(2,1)} %k_ref.3, bf16[1024,1024]{1,0:T(8,128)(2,1)} %v_ref.3), custom_call_target="tpu_custom_call" | custom-call | flops 1 | bytes 1 | tf_op jit(solution)/shard_map/local_states/pallas_call | solution.py:76
  3.8 1.6 %collective-permute-start.2 = (bf16[1024,128]{1,0:T(8,128)(2,1)S(1)}, bf16[1024,128]{1,0:T(8,128)(2,1)S(1)}, u32[]{:S(2)}, u32[]{:S(2)}) collective-permute-start(bf16[1024,128]{1,0:T(8,128)(2,1)S(1)} %local_states.1.after_ref), channel_id=1, source_target_pairs={{0,8},{8,16},{16,24},{24,0},{32,40},{40,48},{48,56},{56,32},{64,72... | collective-permute-start | bytes 786440 | tf_op jit(solution)/shard_map/ppermute | solution.py:304
  5.4 1.7 %collective-permute-start.1 = (bf16[1024,128]{1,0:T(8,128)(2,1)S(1)}, bf16[1024,128]{1,0:T(8,128)(2,1)S(1)}, u32[]{:S(2)}, u32[]{:S(2)}) collective-permute-start(bf16[1024,128]{1,0:T(8,128)(2,1)S(1)} %local_states.1.after_ref), channel_id=1, source_target_pairs={{0,24},{8,0},{16,8},{24,16},{32,56},{40,32},{48,40},{56,48},{64,88... | collective-permute-start | bytes 786440 | tf_op jit(solution)/shard_map/ppermute | solution.py:304
  7.1 1.9 %collective-permute-start = (bf16[1024,128]{1,0:T(8,128)(2,1)S(1)}, bf16[1024,128]{1,0:T(8,128)(2,1)S(1)}, u32[]{:S(2)}, u32[]{:S(2)}) collective-permute-start(bf16[1024,128]{1,0:T(8,128)(2,1)S(1)} %local_states.1.after_ref), channel_id=1, source_target_pairs={{0,16},{8,24},{16,0},{24,8},{32,48},{40,56},{48,32},{56,40},{64,80... | collective-permute-start | bytes 786440 | tf_op jit(solution)/shard_map/ppermute | solution.py:304
  9.0 0.1 stack.35.blocks_ref
  9.1 11.5 %sort_columns.1 = (bf16[1,1024,768]{2,1,0:T(8,128)(2,1)}, bf16[3,1024,768]{2,1,0:T(8,128)(2,1)}, bf16[4,1024,768]{2,1,0:T(8,128)(2,1)}) custom-call(s32[8]{0:T(128)S(1)} %stack.35.blocks_ref, bf16[1024,6144]{1,0:T(8,128)(2,1)} %weight_ref.1, bf16[1024,128]{1,0:T(8,128)(2,1)S(1)} %local_states.1.after_ref), custom_call_target="tpu_custom_call" | custom-call | flops 1 | bytes 1 | tf_op jit(solution)/shard_map/sort_columns/pallas_call | solution.py:157
  20.6 0.0 collective-permute-start.9
  20.6 0.5 collective-permute-start.6
  21.1 0.0 collective-permute-done.2
  21.1 0.0 collective-permute-done.1
  21.1 0.0 collective-permute-done
  21.1 0.2 fusion.2
  21.4 0.0 copy-start.1
  21.4 0.0 copy-start.2
  21.4 4.0 %collective-permute-start.5 = (bf16[1024,128]{1,0:T(8,128)(2,1)S(1)}, bf16[1024,128]{1,0:T(8,128)(2,1)S(1)}, u32[]{:S(2)}, u32[]{:S(2)}) collective-permute-start(bf16[1024,128]{1,0:T(8,128)(2,1)S(1)} %get-tuple-element.43), channel_id=1, source_target_pairs={{0,32},{8,40},{16,48},{24,56},{32,64},{40,72},{48,80},{56,88},{64,... | collective-permute-start | bytes 786440 | tf_op jit(solution)/shard_map/ppermute | solution.py:317
  25.4 3.4 %collective-permute-start.4 = (bf16[1024,128]{1,0:T(8,128)(2,1)S(1)}, bf16[1024,128]{1,0:T(8,128)(2,1)S(1)}, u32[]{:S(2)}, u32[]{:S(2)}) collective-permute-start(bf16[1024,128]{1,0:T(8,128)(2,1)S(1)} %get-tuple-element.43), channel_id=1, source_target_pairs={{0,96},{8,104},{16,112},{24,120},{1,97},{9,105},{17,113},{25,121},... | collective-permute-start | bytes 786440 | tf_op jit(solution)/shard_map/ppermute | solution.py:317
  28.8 2.8 %collective-permute-start.3 = (bf16[1024,128]{1,0:T(8,128)(2,1)S(1)}, bf16[1024,128]{1,0:T(8,128)(2,1)S(1)}, u32[]{:S(2)}, u32[]{:S(2)}) collective-permute-start(bf16[1024,128]{1,0:T(8,128)(2,1)S(1)} %get-tuple-element.43), channel_id=1, source_target_pairs={{0,64},{8,72},{16,80},{24,88},{32,96},{40,104},{48,112},{56,120},{... | collective-permute-start | bytes 786440 | tf_op jit(solution)/shard_map/ppermute | solution.py:317
  31.6 9.0 %intra_block.1 = (f32[1024,1024]{1,0:T(8,128)S(1)}, bf16[1024,1024]{1,0:T(8,128)(2,1)S(1)}) custom-call(bf16[1024,1024]{1,0:T(8,128)(2,1)} %q_ref.1, bf16[1024,1024]{1,0:T(8,128)(2,1)} %k_ref.3, bf16[1024,1024]{1,0:T(8,128)(2,1)} %v_ref.3, bf16[1024,128]{1,0:T(8,128)(2,1)S(1)} %local_states.1.after_ref), custom_call_target="tpu_custom_call" | custom-call | flops 99999997952 | bytes 1 | tf_op jit(solution)/shard_map/intra_block/pallas_call | solution.py:124
  40.5 0.0 collective-permute-done.5.refs_7_
  40.5 0.0 collective-permute-done.4.refs_6_
  40.6 0.0 collective-permute-done.3.refs_5_
  40.6 0.0 collective-permute-done.6.refs_8_.refs_5_
  40.6 0.0 copy-done.1
  40.6 0.0 copy-done.2
  40.6 1.4 %hidden_rows.2.refs_8_.refs_0_ = bf16[512,1024]{1,0:T(8,128)(2,1)S(1)} custom-call(f32[1024,1024]{1,0:T(8,128)S(1)} %get-tuple-element.26.refs_0_, bf16[1024,1024]{1,0:T(8,128)(2,1)S(1)} %get-tuple-element.27.refs_1_, bf16[1024,1024]{1,0:T(8,128)(2,1)S(1)} %copy-done.1, f32[1,1024]{1,0:T(1,128)S(1)} %bitcast.9, f32[1024,128]{1,0:T(8,128)S(1)} %get-tuple-element.44.refs_4_, ...), custom_call_target="tpu_custom_call" | custom-call | flops 1 | bytes 1 | tf_op jit(solution)/shard_map/hidden_rows/pallas_call | solution.py:218
  42.0 0.0 copy-start
  42.0 0.1 collective-permute-start.7
  42.1 1.4 %hidden_rows.3.refs_4_.refs_0_.refs_1_ = bf16[512,1024]{1,0:T(8,128)(2,1)S(1)} custom-call(f32[1024,1024]{1,0:T(8,128)S(1)} %get-tuple-element.26.refs_0_, bf16[1024,1024]{1,0:T(8,128)(2,1)S(1)} %get-tuple-element.27.refs_1_, bf16[1024,1024]{1,0:T(8,128)(2,1)S(1)} %copy-done.1, f32[1,1024]{1,0:T(1,128)S(1)} %bitcast.10, ...), custom_call_target="tpu_custom_call" | custom-call | flops 1 | bytes 1 | tf_op jit(solution)/shard_map/hidden_rows/pallas_call | solution.py:218
  43.4 0.6 collective-permute-start.8
  44.0 0.0 collective-permute-done.9.refs_3_
  44.0 0.7 collective-permute-done.7.refs_1_.refs_2_
  44.7 0.0 copy-done
  44.7 2.8 %share_far.2 = (bf16[256,768]{1,0:T(8,128)(2,1)S(1)}, bf16[256,768]{1,0:T(8,128)(2,1)S(1)}) custom-call(bf16[512,1024]{1,0:T(8,128)(2,1)S(1)} %hidden_rows.2.refs_8_.refs_0_, bf16[512,1024]{1,0:T(8,128)(2,1)S(1)} %collective-permute-done.7.refs_1_.refs_2_, bf16[4,1024,768]{2,1,0:T(8,128)(2,1)S(1)} %copy-done, ...), custom_call_target="tpu_custom_call" | custom-call | flops 99999997952 | bytes 1 | tf_op jit(solution)/shard_map/share_far/pallas_call | solution.py:257
  47.5 3.1 %collective-permute-start.11 = (bf16[256,768]{1,0:T(8,128)(2,1)S(1)}, bf16[256,768]{1,0:T(8,128)(2,1)S(1)}, u32[]{:S(2)}, u32[]{:S(2)}) collective-permute-start(bf16[256,768]{1,0:T(8,128)(2,1)S(1)} %get-tuple-element.35), channel_id=1, source_target_pairs={{0,6},{1,7},{2,0},{3,1},{4,2},{5,3},{6,4},{7,5},{8,14},{9,15},{10,... | collective-permute-start | bytes 1179656 | tf_op jit(solution)/shard_map/ppermute | solution.py:321
  50.6 0.0 collective-permute-start.10
  50.6 0.0 collective-permute-done.8.refs_1_.refs_3_
  50.6 2.8 %share_far.3 = (bf16[256,768]{1,0:T(8,128)(2,1)S(1)}, bf16[256,768]{1,0:T(8,128)(2,1)S(1)}) custom-call(bf16[512,1024]{1,0:T(8,128)(2,1)S(1)} %hidden_rows.3.refs_4_.refs_0_.refs_1_, bf16[512,1024]{1,0:T(8,128)(2,1)S(1)} %collective-permute-done.8.refs_1_.refs_3_, bf16[4,1024,768]{2,1,0:T(8,128)(2,1)S(1)} %copy-done, ...), custom_call_target="tpu_custom_call" | custom-call | flops 1 | bytes 1 | tf_op jit(solution)/shard_map/share_far/pallas_call | solution.py:257
  53.3 3.3 %collective-permute-start.15 = (bf16[256,768]{1,0:T(8,128)(2,1)S(1)}, bf16[256,768]{1,0:T(8,128)(2,1)S(1)}, u32[]{:S(2)}, u32[]{:S(2)}) collective-permute-start(bf16[256,768]{1,0:T(8,128)(2,1)S(1)} %get-tuple-element.38), channel_id=1, source_target_pairs={{0,6},{1,7},{2,0},{3,1},{4,2},{5,3},{6,4},{7,5},{8,14},{9,15},{10,... | collective-permute-start | bytes 1179656 | tf_op jit(solution)/shard_map/ppermute | solution.py:321
  56.6 0.0 collective-permute-start.14
  56.7 7.9 %share_near.1 = (bf16[512,768]{1,0:T(8,128)(2,1)S(1)}, bf16[512,768]{1,0:T(8,128)(2,1)S(1)}) custom-call(bf16[512,1024]{1,0:T(8,128)(2,1)S(1)} %hidden_rows.2.refs_8_.refs_0_, bf16[512,1024]{1,0:T(8,128)(2,1)S(1)} %hidden_rows.3.refs_4_.refs_0_.refs_1_, bf16[512,1024]{1,0:T(8,128)(2,1)S(1)} %collective-permute-done.7.refs_1_.refs_2_, ...), custom_call_target="tpu_custom_call" | custom-call | flops 1 | bytes 1 | tf_op jit(solution)/shard_map/share_near/pallas_call | solution.py:257
  64.5 0.0 collective-permute-done.11.refs_3_.refs_8_
  64.5 0.0 collective-permute-done.10.refs_2_.refs_6_
  64.5 3.5 %collective-permute-start.12 = (bf16[512,768]{1,0:T(8,128)(2,1)S(1)}, bf16[512,768]{1,0:T(8,128)(2,1)S(1)}, u32[]{:S(2)}, u32[]{:S(2)}) collective-permute-start(bf16[512,768]{1,0:T(8,128)(2,1)S(1)} %get-tuple-element.36), channel_id=1, source_target_pairs={{0,6},{1,7},{2,0},{3,1},{4,2},{5,3},{6,4},{7,5},{8,14},{9,15},{10,... | collective-permute-start | bytes 2359304 | tf_op jit(solution)/shard_map/ppermute | solution.py:321
  68.0 0.0 collective-permute-start.13
  68.0 0.1 collective-permute-done.15.refs_9_
  68.1 3.4 %collective-permute-done.14.refs_7_ = bf16[256,768]{1,0:T(8,128)(2,1)S(1)} collective-permute-done((bf16[256,768]{1,0:T(8,128)(2,1)S(1)}, bf16[256,768]{1,0:T(8,128)(2,1)S(1)}, u32[]{:S(2)}, u32[]{:S(2)}) %collective-permute-start.14) | collective-permute-done | bytes 393248 | tf_op jit(solution)/shard_map/ppermute | solution.py:320
  71.5 7.8 %share_passing.1 = (bf16[512,768]{1,0:T(8,128)(2,1)S(1)}, bf16[512,768]{1,0:T(8,128)(2,1)S(1)}) custom-call(bf16[512,1024]{1,0:T(8,128)(2,1)S(1)} %hidden_rows.2.refs_8_.refs_0_, bf16[512,1024]{1,0:T(8,128)(2,1)S(1)} %hidden_rows.3.refs_4_.refs_0_.refs_1_, bf16[512,1024]{1,0:T(8,128)(2,1)S(1)} %collective-permute-done.7.refs_1_.refs_2_, ...), custom_call_target="tpu_custom_call" | custom-call | flops 99999997952 | bytes 1 | tf_op jit(solution)/shard_map/share_passing/pallas_call | solution.py:257
  79.4 0.4 collective-permute-start.17
  79.7 1.7 %collective-permute-start.16 = (bf16[512,768]{1,0:T(8,128)(2,1)S(1)}, bf16[512,768]{1,0:T(8,128)(2,1)S(1)}, u32[]{:S(2)}, u32[]{:S(2)}) collective-permute-start(bf16[512,768]{1,0:T(8,128)(2,1)S(1)} %get-tuple-element.39.refs_8_), channel_id=1, source_target_pairs={{0,2},{1,3},{2,4},{3,5},{4,6},{5,7},{6,0},{7,1},{8,10},{9,11},{10,... | collective-permute-start | bytes 2359304 | tf_op jit(solution)/shard_map/ppermute | solution.py:320
  81.5 4.6 %collective-permute-done.12.refs_6_ = bf16[512,768]{1,0:T(8,128)(2,1)S(1)} collective-permute-done((bf16[512,768]{1,0:T(8,128)(2,1)S(1)}, bf16[512,768]{1,0:T(8,128)(2,1)S(1)}, u32[]{:S(2)}, u32[]{:S(2)}) %collective-permute-start.12) | collective-permute-done | bytes 786464 | tf_op jit(solution)/shard_map/ppermute | solution.py:321
  86.0 3.7 %collective-permute-done.13.refs_7_ = bf16[512,768]{1,0:T(8,128)(2,1)S(1)} collective-permute-done((bf16[512,768]{1,0:T(8,128)(2,1)S(1)}, bf16[512,768]{1,0:T(8,128)(2,1)S(1)}, u32[]{:S(2)}, u32[]{:S(2)}) %collective-permute-start.13) | collective-permute-done | bytes 786464 | tf_op jit(solution)/shard_map/ppermute | solution.py:320
  89.7 7.9 %share_own.1 = (f32[512,768]{1,0:T(8,128)S(1)}, f32[512,768]{1,0:T(8,128)S(1)}) custom-call(bf16[512,1024]{1,0:T(8,128)(2,1)S(1)} %hidden_rows.2.refs_8_.refs_0_, bf16[512,1024]{1,0:T(8,128)(2,1)S(1)} %hidden_rows.3.refs_4_.refs_0_.refs_1_, bf16[512,1024]{1,0:T(8,128)(2,1)S(1)} %collective-permute-done.7.refs_1_.refs_2_, ...), custom_call_target="tpu_custom_call" | custom-call | flops 1 | bytes 1 | tf_op jit(solution)/shard_map/share_own/pallas_call | solution.py:257
  97.6 3.8 %collective-permute-done.17.refs_3_ = bf16[512,768]{1,0:T(8,128)(2,1)S(1)} collective-permute-done((bf16[512,768]{1,0:T(8,128)(2,1)S(1)}, bf16[512,768]{1,0:T(8,128)(2,1)S(1)}, u32[]{:S(2)}, u32[]{:S(2)}) %collective-permute-start.17) | collective-permute-done | bytes 786464 | tf_op jit(solution)/shard_map/ppermute | solution.py:321
  101.4 3.4 %collective-permute-done.16.refs_2_ = bf16[512,768]{1,0:T(8,128)(2,1)S(1)} collective-permute-done((bf16[512,768]{1,0:T(8,128)(2,1)S(1)}, bf16[512,768]{1,0:T(8,128)(2,1)S(1)}, u32[]{:S(2)}, u32[]{:S(2)}) %collective-permute-start.16) | collective-permute-done | bytes 786464 | tf_op jit(solution)/shard_map/ppermute | solution.py:320
  104.8 1.8 %finish.1 = bf16[1024,768]{1,0:T(8,128)(2,1)} custom-call(f32[512,768]{1,0:T(8,128)S(1)} %get-tuple-element.40.refs_0_, f32[512,768]{1,0:T(8,128)S(1)} %get-tuple-element.41.refs_1_, bf16[512,768]{1,0:T(8,128)(2,1)S(1)} %collective-permute-done.16.refs_2_, bf16[512,768]{1,0:T(8,128)(2,1)S(1)} %collective-permute-done.17.refs_3_), custom_call_target="tpu_custom_call" | custom-call | flops 1 | bytes 1 | tf_op jit(solution)/shard_map/finish/pallas_call | solution.py:283
  (1 shorter events, 0.0 us)
Async XLA Ops:
  3.8 17.3 %collective-permute-start.2 = (bf16[1024,128]{1,0:T(8,128)(2,1)S(1)}, bf16[1024,128]{1,0:T(8,128)(2,1)S(1)}, u32[]{:S(2)}, u32[]{:S(2)}) collective-permute-start(bf16[1024,128]{1,0:T(8,128)(2,1)S(1)} %local_states.1.after_ref), channel_id=1, source_target_pairs={{0,8},{8,16},{16,24},{24,0},{32,40},{40,48},{48,56},{56,32},{64,72... | collective-permute-start | bytes 786440 | tf_op jit(solution)/shard_map/ppermute | solution.py:304
  5.4 15.7 %collective-permute-start.1 = (bf16[1024,128]{1,0:T(8,128)(2,1)S(1)}, bf16[1024,128]{1,0:T(8,128)(2,1)S(1)}, u32[]{:S(2)}, u32[]{:S(2)}) collective-permute-start(bf16[1024,128]{1,0:T(8,128)(2,1)S(1)} %local_states.1.after_ref), channel_id=1, source_target_pairs={{0,24},{8,0},{16,8},{24,16},{32,56},{40,32},{48,40},{56,48},{64,88... | collective-permute-start | bytes 786440 | tf_op jit(solution)/shard_map/ppermute | solution.py:304
  7.1 14.0 %collective-permute-start = (bf16[1024,128]{1,0:T(8,128)(2,1)S(1)}, bf16[1024,128]{1,0:T(8,128)(2,1)S(1)}, u32[]{:S(2)}, u32[]{:S(2)}) collective-permute-start(bf16[1024,128]{1,0:T(8,128)(2,1)S(1)} %local_states.1.after_ref), channel_id=1, source_target_pairs={{0,16},{8,24},{16,0},{24,8},{32,48},{40,56},{48,32},{56,40},{64,80... | collective-permute-start | bytes 786440 | tf_op jit(solution)/shard_map/ppermute | solution.py:304
  20.6 23.4 %collective-permute-start.9 = (bf16[1,1024,768]{2,1,0:T(8,128)(2,1)}, bf16[1,1024,768]{2,1,0:T(8,128)(2,1)S(1)}, u32[]{:S(2)}, u32[]{:S(2)}) collective-permute-start(bf16[1,1024,768]{2,1,0:T(8,128)(2,1)} %get-tuple-element.30), channel_id=1, source_target_pairs={{0,1},{1,0},{2,3},{3,2},{4,5},{5,4},{6,7},{7,6},{8,9},{9,8},{10,11... | collective-permute-start | bytes 4718600 | tf_op jit(solution)/shard_map/ppermute | solution.py:306
  20.6 20.0 %collective-permute-start.6 = (bf16[3,1024,768]{2,1,0:T(8,128)(2,1)}, bf16[3,1024,768]{2,1,0:T(8,128)(2,1)}, u32[]{:S(2)}, u32[]{:S(2)}) collective-permute-start(bf16[3,1024,768]{2,1,0:T(8,128)(2,1)} %get-tuple-element.28), channel_id=1, source_target_pairs={{0,1},{1,0},{2,3},{3,2},{4,5},{5,4},{6,7},{7,6},{8,9},{9,8},{10,11... | collective-permute-start | bytes 14155784 | tf_op jit(solution)/shard_map/ppermute | solution.py:306
  21.4 19.2 %copy-start.1 = (bf16[1024,1024]{1,0:T(8,128)(2,1)S(1)}, bf16[1024,1024]{1,0:T(8,128)(2,1)}, u32[]{:S(2)}) copy-start(bf16[1024,1024]{1,0:T(8,128)(2,1)} %refs_2_.3) | copy-start | bytes 6291460
  21.4 19.2 %copy-start.2 = (f32[1024]{0:T(1024)S(1)}, f32[1024]{0:T(1024)}, u32[]{:S(2)}) copy-start(f32[1024]{0:T(1024)} %param.10) | copy-start | bytes 12292
  21.4 19.1 %collective-permute-start.5 = (bf16[1024,128]{1,0:T(8,128)(2,1)S(1)}, bf16[1024,128]{1,0:T(8,128)(2,1)S(1)}, u32[]{:S(2)}, u32[]{:S(2)}) collective-permute-start(bf16[1024,128]{1,0:T(8,128)(2,1)S(1)} %get-tuple-element.43), channel_id=1, source_target_pairs={{0,32},{8,40},{16,48},{24,56},{32,64},{40,72},{48,80},{56,88},{64,... | collective-permute-start | bytes 786440 | tf_op jit(solution)/shard_map/ppermute | solution.py:317
  25.4 15.2 %collective-permute-start.4 = (bf16[1024,128]{1,0:T(8,128)(2,1)S(1)}, bf16[1024,128]{1,0:T(8,128)(2,1)S(1)}, u32[]{:S(2)}, u32[]{:S(2)}) collective-permute-start(bf16[1024,128]{1,0:T(8,128)(2,1)S(1)} %get-tuple-element.43), channel_id=1, source_target_pairs={{0,96},{8,104},{16,112},{24,120},{1,97},{9,105},{17,113},{25,121},... | collective-permute-start | bytes 786440 | tf_op jit(solution)/shard_map/ppermute | solution.py:317
  28.8 11.8 %collective-permute-start.3 = (bf16[1024,128]{1,0:T(8,128)(2,1)S(1)}, bf16[1024,128]{1,0:T(8,128)(2,1)S(1)}, u32[]{:S(2)}, u32[]{:S(2)}) collective-permute-start(bf16[1024,128]{1,0:T(8,128)(2,1)S(1)} %get-tuple-element.43), channel_id=1, source_target_pairs={{0,64},{8,72},{16,80},{24,88},{32,96},{40,104},{48,112},{56,120},{... | collective-permute-start | bytes 786440 | tf_op jit(solution)/shard_map/ppermute | solution.py:317
  42.0 2.8 %copy-start = (bf16[4,1024,768]{2,1,0:T(8,128)(2,1)S(1)}, bf16[4,1024,768]{2,1,0:T(8,128)(2,1)}, u32[]{:S(2)}) copy-start(bf16[4,1024,768]{2,1,0:T(8,128)(2,1)} %get-tuple-element.29.refs_2_.refs_4_) | copy-start | bytes 18874372
  42.0 2.7 %collective-permute-start.7 = (bf16[512,1024]{1,0:T(8,128)(2,1)S(1)}, bf16[512,1024]{1,0:T(8,128)(2,1)S(1)}, u32[]{:S(2)}, u32[]{:S(2)}) collective-permute-start(bf16[512,1024]{1,0:T(8,128)(2,1)S(1)} %hidden_rows.2.refs_8_.refs_0_), channel_id=1, source_target_pairs={{0,1},{1,0},{2,3},{3,2},{4,5},{5,4},{6,7},{7,6},{8,9},{9,8},{10,11... | collective-permute-start | bytes 3145736 | tf_op jit(solution)/shard_map/ppermute | solution.py:306
  43.4 7.2 %collective-permute-start.8 = (bf16[512,1024]{1,0:T(8,128)(2,1)S(1)}, bf16[512,1024]{1,0:T(8,128)(2,1)S(1)}, u32[]{:S(2)}, u32[]{:S(2)}) collective-permute-start(bf16[512,1024]{1,0:T(8,128)(2,1)S(1)} %hidden_rows.3.refs_4_.refs_0_.refs_1_), channel_id=1, source_target_pairs={{0,1},{1,0},{2,3},{3,2},{4,5},{5,4},{6,7},{7,6},{8,9},{9,8},{10,11... | collective-permute-start | bytes 3145736 | tf_op jit(solution)/shard_map/ppermute | solution.py:306
  47.5 17.0 %collective-permute-start.11 = (bf16[256,768]{1,0:T(8,128)(2,1)S(1)}, bf16[256,768]{1,0:T(8,128)(2,1)S(1)}, u32[]{:S(2)}, u32[]{:S(2)}) collective-permute-start(bf16[256,768]{1,0:T(8,128)(2,1)S(1)} %get-tuple-element.35), channel_id=1, source_target_pairs={{0,6},{1,7},{2,0},{3,1},{4,2},{5,3},{6,4},{7,5},{8,14},{9,15},{10,... | collective-permute-start | bytes 1179656 | tf_op jit(solution)/shard_map/ppermute | solution.py:321
  50.6 14.0 %collective-permute-start.10 = (bf16[256,768]{1,0:T(8,128)(2,1)S(1)}, bf16[256,768]{1,0:T(8,128)(2,1)S(1)}, u32[]{:S(2)}, u32[]{:S(2)}) collective-permute-start(bf16[256,768]{1,0:T(8,128)(2,1)S(1)} %get-tuple-element.31.refs_4_), channel_id=1, source_target_pairs={{0,2},{1,3},{2,4},{3,5},{4,6},{5,7},{6,0},{7,1},{8,10},{9,11},{10,... | collective-permute-start | bytes 1179656 | tf_op jit(solution)/shard_map/ppermute | solution.py:320
  53.3 14.8 %collective-permute-start.15 = (bf16[256,768]{1,0:T(8,128)(2,1)S(1)}, bf16[256,768]{1,0:T(8,128)(2,1)S(1)}, u32[]{:S(2)}, u32[]{:S(2)}) collective-permute-start(bf16[256,768]{1,0:T(8,128)(2,1)S(1)} %get-tuple-element.38), channel_id=1, source_target_pairs={{0,6},{1,7},{2,0},{3,1},{4,2},{5,3},{6,4},{7,5},{8,14},{9,15},{10,... | collective-permute-start | bytes 1179656 | tf_op jit(solution)/shard_map/ppermute | solution.py:321
  56.6 14.9 %collective-permute-start.14 = (bf16[256,768]{1,0:T(8,128)(2,1)S(1)}, bf16[256,768]{1,0:T(8,128)(2,1)S(1)}, u32[]{:S(2)}, u32[]{:S(2)}) collective-permute-start(bf16[256,768]{1,0:T(8,128)(2,1)S(1)} %get-tuple-element.32.refs_6_), channel_id=1, source_target_pairs={{0,2},{1,3},{2,4},{3,5},{4,6},{5,7},{6,0},{7,1},{8,10},{9,11},{10,... | collective-permute-start | bytes 1179656 | tf_op jit(solution)/shard_map/ppermute | solution.py:320
  64.5 21.5 %collective-permute-start.12 = (bf16[512,768]{1,0:T(8,128)(2,1)S(1)}, bf16[512,768]{1,0:T(8,128)(2,1)S(1)}, u32[]{:S(2)}, u32[]{:S(2)}) collective-permute-start(bf16[512,768]{1,0:T(8,128)(2,1)S(1)} %get-tuple-element.36), channel_id=1, source_target_pairs={{0,6},{1,7},{2,0},{3,1},{4,2},{5,3},{6,4},{7,5},{8,14},{9,15},{10,... | collective-permute-start | bytes 2359304 | tf_op jit(solution)/shard_map/ppermute | solution.py:321
  68.0 21.7 %collective-permute-start.13 = (bf16[512,768]{1,0:T(8,128)(2,1)S(1)}, bf16[512,768]{1,0:T(8,128)(2,1)S(1)}, u32[]{:S(2)}, u32[]{:S(2)}) collective-permute-start(bf16[512,768]{1,0:T(8,128)(2,1)S(1)} %get-tuple-element.37.refs_10_), channel_id=1, source_target_pairs={{0,2},{1,3},{2,4},{3,5},{4,6},{5,7},{6,0},{7,1},{8,10},{9,11},{10,... | collective-permute-start | bytes 2359304 | tf_op jit(solution)/shard_map/ppermute | solution.py:320
  79.4 22.0 %collective-permute-start.17 = (bf16[512,768]{1,0:T(8,128)(2,1)S(1)}, bf16[512,768]{1,0:T(8,128)(2,1)S(1)}, u32[]{:S(2)}, u32[]{:S(2)}) collective-permute-start(bf16[512,768]{1,0:T(8,128)(2,1)S(1)} %get-tuple-element.42), channel_id=1, source_target_pairs={{0,6},{1,7},{2,0},{3,1},{4,2},{5,3},{6,4},{7,5},{8,14},{9,15},{10,... | collective-permute-start | bytes 2359304 | tf_op jit(solution)/shard_map/ppermute | solution.py:321
  79.7 25.0 %collective-permute-start.16 = (bf16[512,768]{1,0:T(8,128)(2,1)S(1)}, bf16[512,768]{1,0:T(8,128)(2,1)S(1)}, u32[]{:S(2)}, u32[]{:S(2)}) collective-permute-start(bf16[512,768]{1,0:T(8,128)(2,1)S(1)} %get-tuple-element.39.refs_8_), channel_id=1, source_target_pairs={{0,2},{1,3},{2,4},{3,5},{4,6},{5,7},{6,0},{7,1},{8,10},{9,11},{10,... | collective-permute-start | bytes 2359304 | tf_op jit(solution)/shard_map/ppermute | solution.py:320

commit v3 on v2

--- a/solution.py
+++ b/solution.py
@@ -99,31 +99,39 @@
     t = lax.broadcasted_iota(jnp.int32, (CHUNK, CHUNK), 0)
     s = lax.broadcasted_iota(jnp.int32, (CHUNK, CHUNK), 1)
     causal = s <= t
-    for h in range(q_ref.shape[1] // DH):
-        cols = slice(h * DH, (h + 1) * DH)
-        out_cols = pl.ds(pl.multiple_of(pl.program_id(0) * block + h * DH, DH), DH)
-        state = jnp.zeros((DH, DH), F32)
-        for i in range(rows // CHUNK):
-            here = slice(i * CHUNK, (i + 1) * CHUNK)
-            q, k, v = feature(q_ref[here, cols]), feature(k_ref[here, cols]), v_ref[here, cols]
-            qfeat_ref[here, out_cols] = q
-            scores = lax.dot_general(q, k, (((1,), (1,)), ((), ())), preferred_element_type=F32)
-            scores = jnp.where(causal, scores, 0.0).astype(BF16)
-            out = jnp.dot(scores, v, preferred_element_type=F32)
-            if i:
-                out += two_part_dot(q, *split(state))
-            intra_ref[here, out_cols] = out
-            if (i + 1) * CHUNK < rows:
-                state += lax.dot_general(k, v, (((0,), (0,)), ((), ())), preferred_element_type=F32)
+    heads = range(block // DH)
+    cols = [slice(h * DH, (h + 1) * DH) for h in heads]
+    out_cols = [pl.ds(pl.multiple_of(pl.program_id(0) * block + h * DH, DH), DH) for h in heads]
+    states = [jnp.zeros((DH, DH), F32) for _ in heads]
+    for i in range(rows // CHUNK):
+        here = slice(i * CHUNK, (i + 1) * CHUNK)
+        q = [feature(q_ref[here, c]) for c in cols]
+        k = [feature(k_ref[here, c]) for c in cols]
+        v = [v_ref[here, c] for c in cols]
+        scores = [
+            lax.dot_general(q[h], k[h], (((1,), (1,)), ((), ())), preferred_element_type=F32) for h in heads
+        ]
+        before = [two_part_dot(q[h], *split(states[h])) for h in heads] if i else None
+        if (i + 1) * CHUNK < rows:
+            states = [
+                states[h] + lax.dot_general(k[h], v[h], (((0,), (0,)), ((), ())), preferred_element_type=F32)
+                for h in heads
+            ]
+        scores = [jnp.where(causal, x, 0.0).astype(BF16) for x in scores]
+        out = [jnp.dot(scores[h], v[h], preferred_element_type=F32) for h in heads]
+        for h in heads:
+            qfeat_ref[here, out_cols[h]] = q[h]
+            intra_ref[here, out_cols[h]] = out[h] + before[h] if i else out[h]
 
 
 def intra_block(queries, keys, values, after):
     rows, width = keys.shape
-    block = 2 * DH
+    block = 4 * DH
     spec = pl.BlockSpec((rows, block), lambda i: (0, i))
     return call(
         intra_kernel,
         name="intra_block",
+        vmem=28,
         flops=10**11,
         grid=(width // block,),
         in_specs=[spec] * 3 + [ANYWHERE],
@@ -264,30 +272,25 @@
     )(*map(in_vmem, operands), *after)
 
 
-def finish_kernel(*refs):
-    values, adds, out_ref = refs[:2], refs[2:4], refs[4]
+def finish_kernel(value_ref, add_ref, *refs):
+    out_ref = refs[-1]
     rows = out_ref.shape[0]
-    step = pl.program_id(0)
-    steps = values[0].shape[0] // rows
-    here = pl.ds(pl.multiple_of(lax.rem(step, steps) * rows, rows), rows)
-    for value, add, half in zip(values, adds, range(2)):
-
-        @pl.when(step // steps == half)
-        def _(value=value, add=add):
-            out_ref[...] = (value[here, :] + add[here, :].astype(F32)).astype(BF16)
-
-
-def finish(*halves):
-    rows, width = halves[0].shape
+    here = pl.ds(pl.multiple_of(pl.program_id(0) * rows, rows), rows)
+    out_ref[...] = (value_ref[here, :] + add_ref[here, :].astype(F32)).astype(BF16)
+
+
+def finish(part, value, add, begun=()):
+    rows, width = value.shape
     block = rows // 2
     return call(
         finish_kernel,
         name="finish",
-        grid=(2 * rows // block,),
-        in_specs=[IN_VMEM] * 4,
-        out_specs=pl.BlockSpec((block, width), lambda i: (i, 0)),
+        grid=(rows // block,),
+        in_specs=[IN_VMEM] * 2 + [ANYWHERE] * len(begun),
+        out_specs=pl.BlockSpec((block, width), lambda i: (part * (rows // block) + i, 0)),
         out_shape=jax.ShapeDtypeStruct((2 * rows, width), BF16),
-    )(*map(in_vmem, halves))
+        input_output_aliases={2: 0} if begun else {},
+    )(in_vmem(value), in_vmem(add), *begun)
 
 
 def on_device(queries, key_proj, values, gate_input, norm_gain, out_weight):
@@ -358,7 +361,8 @@
         "share_own", own, other, own_weight, other_rest, ((3, 2),), home, [(half, F32)] * 2,
         adds=[top_from_above, bottom_from_below], after=[up_sum],
     )
-    return finish(top, bottom, top_from_below, bottom_from_above)
+    out = finish(1, bottom, bottom_from_above)
+    return finish(0, top, top_from_below, [out])
 
 
 def solution(mesh):

time: 107 us -> 106 us (level)
  Pallas kernels: 57.8 us -> 56 us
    pallas_call x2 -> x3, Pallas kernels: 10.7 us -> 8.92 us  [the longest x1 7.03 us: intra_block(): call(intra_kernel, name='intra_block', vmem=28, flops=10 ** 11, grid=(wid...]
    ppermute x3, waiting for transfers between devices: 0.01 us -> 1.51 us  [on_device(): along_z = [lax.ppermute(total, 'ctx', later_z(k)) for k in (2, 3, 1)]]
  transfers between devices with their start and end apart: 18 -> 18, of which waited for: 7 -> 8; matrix products, arithmetic and copies ran while one was open for 0% -> 0% of each run, Pallas kernels for 49% -> 49%
where the time goes in v3:
time: 106 us; the launch traced here: 105 us
  Pallas kernels  56 us (53%)
  starting transfers between devices  28.3 us (27%)
  waiting for transfers between devices  20.4 us (19%)
    pallas_call x5, Pallas kernels, project(): call(functools.partial(project_kernel, blocks, plan, len(own), len(adds),...  29 us
    pallas_call x1, Pallas kernels, sort_columns(): call(sort_columns_kernel, vmem=24, name='sort_columns', grid_spec=pltpu.P...  11.5 us
    ppermute x3, starting transfers between devices, on_device(): along_z = [lax.ppermute(total, 'ctx', later_z(k)) for k in (2, 3, 1)]  10.1 us
    ppermute x4, starting transfers between devices, on_device(): down = lambda a: lax.ppermute(a, 'tp', shift_y(-1))  10.1 us
    ppermute x4, waiting for transfers between devices, on_device(): up = lambda a: lax.ppermute(a, 'tp', shift_y(1))  9.57 us
    ppermute x4, waiting for transfers between devices, on_device(): down = lambda a: lax.ppermute(a, 'tp', shift_y(-1))  8.59 us
    pallas_call x1, Pallas kernels, intra_block(): call(intra_kernel, name='intra_block', vmem=28, flops=10 ** 11, grid=(wid...  7.03 us
    ppermute x3, starting transfers between devices, on_device(): along_x = [lax.ppermute(state, 'ctx', shift_x(k)) for k in (2, 3, 1)]  5.2 us
  transfers between devices with their start and end apart: 18, of which 8 were waited for; matrix products, arithmetic and copies ran while one was open for 0% of the time, Pallas kernels for 49%

profile of v3, /device:TPU:0, one launch (start us, length us, event | category | flops | bytes accessed | tf_op | source)
XLA Modules:
  0.0 105.2 jit_solution(14795103767305125311)
XLA Ops:
  0.0 3.8 %local_states.1.after_ref = bf16[1024,128]{1,0:T(8,128)(2,1)S(1)} custom-call(bf16[1024,1024]{1,0:T(8,128)(2,1)} %k_ref.3, bf16[1024,1024]{1,0:T(8,128)(2,1)} %v_ref.3), custom_call_target="tpu_custom_call" | custom-call | flops 1 | bytes 1 | tf_op jit(solution)/shard_map/local_states/pallas_call | solution.py:76
  3.8 1.6 %collective-permute-start.2 = (bf16[1024,128]{1,0:T(8,128)(2,1)S(1)}, bf16[1024,128]{1,0:T(8,128)(2,1)S(1)}, u32[]{:S(2)}, u32[]{:S(2)}) collective-permute-start(bf16[1024,128]{1,0:T(8,128)(2,1)S(1)} %local_states.1.after_ref), channel_id=1, source_target_pairs={{0,8},{8,16},{16,24},{24,0},{32,40},{40,48},{48,56},{56,32},{64,72... | collective-permute-start | bytes 786440 | tf_op jit(solution)/shard_map/ppermute | solution.py:307
  5.4 1.7 %collective-permute-start.1 = (bf16[1024,128]{1,0:T(8,128)(2,1)S(1)}, bf16[1024,128]{1,0:T(8,128)(2,1)S(1)}, u32[]{:S(2)}, u32[]{:S(2)}) collective-permute-start(bf16[1024,128]{1,0:T(8,128)(2,1)S(1)} %local_states.1.after_ref), channel_id=1, source_target_pairs={{0,24},{8,0},{16,8},{24,16},{32,56},{40,32},{48,40},{56,48},{64,88... | collective-permute-start | bytes 786440 | tf_op jit(solution)/shard_map/ppermute | solution.py:307
  7.1 1.9 %collective-permute-start = (bf16[1024,128]{1,0:T(8,128)(2,1)S(1)}, bf16[1024,128]{1,0:T(8,128)(2,1)S(1)}, u32[]{:S(2)}, u32[]{:S(2)}) collective-permute-start(bf16[1024,128]{1,0:T(8,128)(2,1)S(1)} %local_states.1.after_ref), channel_id=1, source_target_pairs={{0,16},{8,24},{16,0},{24,8},{32,48},{40,56},{48,32},{56,40},{64,80... | collective-permute-start | bytes 786440 | tf_op jit(solution)/shard_map/ppermute | solution.py:307
  9.0 0.1 stack.35.blocks_ref
  9.1 11.5 %sort_columns.1 = (bf16[1,1024,768]{2,1,0:T(8,128)(2,1)}, bf16[3,1024,768]{2,1,0:T(8,128)(2,1)}, bf16[4,1024,768]{2,1,0:T(8,128)(2,1)}) custom-call(s32[8]{0:T(128)S(1)} %stack.35.blocks_ref, bf16[1024,6144]{1,0:T(8,128)(2,1)} %weight_ref.1, bf16[1024,128]{1,0:T(8,128)(2,1)S(1)} %local_states.1.after_ref), custom_call_target="tpu_custom_call" | custom-call | flops 1 | bytes 1 | tf_op jit(solution)/shard_map/sort_columns/pallas_call | solution.py:165
  20.6 0.0 collective-permute-start.9
  20.6 0.5 collective-permute-start.6
  21.1 0.0 collective-permute-done.2
  21.1 0.0 collective-permute-done.1
  21.1 0.0 collective-permute-done
  21.1 0.2 fusion.2
  21.4 0.0 copy-start.1
  21.4 0.0 copy-start.2
  21.4 4.0 %collective-permute-start.5 = (bf16[1024,128]{1,0:T(8,128)(2,1)S(1)}, bf16[1024,128]{1,0:T(8,128)(2,1)S(1)}, u32[]{:S(2)}, u32[]{:S(2)}) collective-permute-start(bf16[1024,128]{1,0:T(8,128)(2,1)S(1)} %get-tuple-element.43), channel_id=1, source_target_pairs={{0,32},{8,40},{16,48},{24,56},{32,64},{40,72},{48,80},{56,88},{64,... | collective-permute-start | bytes 786440 | tf_op jit(solution)/shard_map/ppermute | solution.py:320
  25.4 3.4 %collective-permute-start.4 = (bf16[1024,128]{1,0:T(8,128)(2,1)S(1)}, bf16[1024,128]{1,0:T(8,128)(2,1)S(1)}, u32[]{:S(2)}, u32[]{:S(2)}) collective-permute-start(bf16[1024,128]{1,0:T(8,128)(2,1)S(1)} %get-tuple-element.43), channel_id=1, source_target_pairs={{0,96},{8,104},{16,112},{24,120},{1,97},{9,105},{17,113},{25,121},... | collective-permute-start | bytes 786440 | tf_op jit(solution)/shard_map/ppermute | solution.py:320
  28.8 2.8 %collective-permute-start.3 = (bf16[1024,128]{1,0:T(8,128)(2,1)S(1)}, bf16[1024,128]{1,0:T(8,128)(2,1)S(1)}, u32[]{:S(2)}, u32[]{:S(2)}) collective-permute-start(bf16[1024,128]{1,0:T(8,128)(2,1)S(1)} %get-tuple-element.43), channel_id=1, source_target_pairs={{0,64},{8,72},{16,80},{24,88},{32,96},{40,104},{48,112},{56,120},{... | collective-permute-start | bytes 786440 | tf_op jit(solution)/shard_map/ppermute | solution.py:320
  31.6 7.0 %intra_block.1 = (f32[1024,1024]{1,0:T(8,128)S(1)}, bf16[1024,1024]{1,0:T(8,128)(2,1)S(1)}) custom-call(bf16[1024,1024]{1,0:T(8,128)(2,1)} %q_ref.1, bf16[1024,1024]{1,0:T(8,128)(2,1)} %k_ref.3, bf16[1024,1024]{1,0:T(8,128)(2,1)} %v_ref.3, bf16[1024,128]{1,0:T(8,128)(2,1)S(1)} %local_states.1.after_ref), custom_call_target="tpu_custom_call" | custom-call | flops 99999997952 | bytes 1 | tf_op jit(solution)/shard_map/intra_block/pallas_call | solution.py:131
  38.6 0.0 collective-permute-done.5.refs_7_
  38.6 1.5 %collective-permute-done.4.refs_6_ = bf16[1024,128]{1,0:T(8,128)(2,1)S(1)} collective-permute-done((bf16[1024,128]{1,0:T(8,128)(2,1)S(1)}, bf16[1024,128]{1,0:T(8,128)(2,1)S(1)}, u32[]{:S(2)}, u32[]{:S(2)}) %collective-permute-start.4) | collective-permute-done | bytes 262176 | tf_op jit(solution)/shard_map/ppermute | solution.py:320
  40.1 0.0 collective-permute-done.3.refs_5_
  40.1 0.0 collective-permute-done.6.refs_8_.refs_5_
  40.1 0.0 copy-done.1
  40.1 0.0 copy-done.2
  40.1 1.4 %hidden_rows.2.refs_8_.refs_0_ = bf16[512,1024]{1,0:T(8,128)(2,1)S(1)} custom-call(f32[1024,1024]{1,0:T(8,128)S(1)} %get-tuple-element.26.refs_0_, bf16[1024,1024]{1,0:T(8,128)(2,1)S(1)} %get-tuple-element.27.refs_1_, bf16[1024,1024]{1,0:T(8,128)(2,1)S(1)} %copy-done.1, f32[1,1024]{1,0:T(1,128)S(1)} %bitcast.9, f32[1024,128]{1,0:T(8,128)S(1)} %get-tuple-element.44.refs_4_, ...), custom_call_target="tpu_custom_call" | custom-call | flops 1 | bytes 1 | tf_op jit(solution)/shard_map/hidden_rows/pallas_call | solution.py:226
  41.5 0.0 copy-start
  41.5 0.1 collective-permute-start.7
  41.6 1.4 %hidden_rows.3.refs_4_.refs_0_.refs_1_ = bf16[512,1024]{1,0:T(8,128)(2,1)S(1)} custom-call(f32[1024,1024]{1,0:T(8,128)S(1)} %get-tuple-element.26.refs_0_, bf16[1024,1024]{1,0:T(8,128)(2,1)S(1)} %get-tuple-element.27.refs_1_, bf16[1024,1024]{1,0:T(8,128)(2,1)S(1)} %copy-done.1, f32[1,1024]{1,0:T(1,128)S(1)} %bitcast.10, ...), custom_call_target="tpu_custom_call" | custom-call | flops 1 | bytes 1 | tf_op jit(solution)/shard_map/hidden_rows/pallas_call | solution.py:226
  43.0 0.6 collective-permute-start.8
  43.5 0.0 collective-permute-done.9.refs_3_
  43.5 0.7 collective-permute-done.7.refs_1_.refs_2_
  44.2 0.0 copy-done
  44.3 2.8 %share_far.2 = (bf16[256,768]{1,0:T(8,128)(2,1)S(1)}, bf16[256,768]{1,0:T(8,128)(2,1)S(1)}) custom-call(bf16[512,1024]{1,0:T(8,128)(2,1)S(1)} %hidden_rows.2.refs_8_.refs_0_, bf16[512,1024]{1,0:T(8,128)(2,1)S(1)} %collective-permute-done.7.refs_1_.refs_2_, bf16[4,1024,768]{2,1,0:T(8,128)(2,1)S(1)} %copy-done, ...), custom_call_target="tpu_custom_call" | custom-call | flops 99999997952 | bytes 1 | tf_op jit(solution)/shard_map/share_far/pallas_call | solution.py:265
  47.0 3.1 %collective-permute-start.11 = (bf16[256,768]{1,0:T(8,128)(2,1)S(1)}, bf16[256,768]{1,0:T(8,128)(2,1)S(1)}, u32[]{:S(2)}, u32[]{:S(2)}) collective-permute-start(bf16[256,768]{1,0:T(8,128)(2,1)S(1)} %get-tuple-element.35), channel_id=1, source_target_pairs={{0,6},{1,7},{2,0},{3,1},{4,2},{5,3},{6,4},{7,5},{8,14},{9,15},{10,... | collective-permute-start | bytes 1179656 | tf_op jit(solution)/shard_map/ppermute | solution.py:324
  50.1 0.0 collective-permute-start.10
  50.1 0.0 collective-permute-done.8.refs_1_.refs_3_
  50.1 2.7 %share_far.3 = (bf16[256,768]{1,0:T(8,128)(2,1)S(1)}, bf16[256,768]{1,0:T(8,128)(2,1)S(1)}) custom-call(bf16[512,1024]{1,0:T(8,128)(2,1)S(1)} %hidden_rows.3.refs_4_.refs_0_.refs_1_, bf16[512,1024]{1,0:T(8,128)(2,1)S(1)} %collective-permute-done.8.refs_1_.refs_3_, bf16[4,1024,768]{2,1,0:T(8,128)(2,1)S(1)} %copy-done, ...), custom_call_target="tpu_custom_call" | custom-call | flops 1 | bytes 1 | tf_op jit(solution)/shard_map/share_far/pallas_call | solution.py:265
  52.9 3.3 %collective-permute-start.15 = (bf16[256,768]{1,0:T(8,128)(2,1)S(1)}, bf16[256,768]{1,0:T(8,128)(2,1)S(1)}, u32[]{:S(2)}, u32[]{:S(2)}) collective-permute-start(bf16[256,768]{1,0:T(8,128)(2,1)S(1)} %get-tuple-element.38), channel_id=1, source_target_pairs={{0,6},{1,7},{2,0},{3,1},{4,2},{5,3},{6,4},{7,5},{8,14},{9,15},{10,... | collective-permute-start | bytes 1179656 | tf_op jit(solution)/shard_map/ppermute | solution.py:324
  56.2 0.0 collective-permute-start.14
  56.2 7.9 %share_near.1 = (bf16[512,768]{1,0:T(8,128)(2,1)S(1)}, bf16[512,768]{1,0:T(8,128)(2,1)S(1)}) custom-call(bf16[512,1024]{1,0:T(8,128)(2,1)S(1)} %hidden_rows.2.refs_8_.refs_0_, bf16[512,1024]{1,0:T(8,128)(2,1)S(1)} %hidden_rows.3.refs_4_.refs_0_.refs_1_, bf16[512,1024]{1,0:T(8,128)(2,1)S(1)} %collective-permute-done.7.refs_1_.refs_2_, ...), custom_call_target="tpu_custom_call" | custom-call | flops 1 | bytes 1 | tf_op jit(solution)/shard_map/share_near/pallas_call | solution.py:265
  64.1 0.0 collective-permute-done.11.refs_3_.refs_8_
  64.1 0.0 collective-permute-done.10.refs_2_.refs_6_
  64.1 3.3 %collective-permute-start.12 = (bf16[512,768]{1,0:T(8,128)(2,1)S(1)}, bf16[512,768]{1,0:T(8,128)(2,1)S(1)}, u32[]{:S(2)}, u32[]{:S(2)}) collective-permute-start(bf16[512,768]{1,0:T(8,128)(2,1)S(1)} %get-tuple-element.36), channel_id=1, source_target_pairs={{0,6},{1,7},{2,0},{3,1},{4,2},{5,3},{6,4},{7,5},{8,14},{9,15},{10,... | collective-permute-start | bytes 2359304 | tf_op jit(solution)/shard_map/ppermute | solution.py:324
  67.4 0.0 collective-permute-start.13
  67.4 0.4 collective-permute-done.15.refs_9_
  67.8 3.4 %collective-permute-done.14.refs_7_ = bf16[256,768]{1,0:T(8,128)(2,1)S(1)} collective-permute-done((bf16[256,768]{1,0:T(8,128)(2,1)S(1)}, bf16[256,768]{1,0:T(8,128)(2,1)S(1)}, u32[]{:S(2)}, u32[]{:S(2)}) %collective-permute-start.14) | collective-permute-done | bytes 393248 | tf_op jit(solution)/shard_map/ppermute | solution.py:323
  71.2 7.8 %share_passing.1 = (bf16[512,768]{1,0:T(8,128)(2,1)S(1)}, bf16[512,768]{1,0:T(8,128)(2,1)S(1)}) custom-call(bf16[512,1024]{1,0:T(8,128)(2,1)S(1)} %hidden_rows.2.refs_8_.refs_0_, bf16[512,1024]{1,0:T(8,128)(2,1)S(1)} %hidden_rows.3.refs_4_.refs_0_.refs_1_, bf16[512,1024]{1,0:T(8,128)(2,1)S(1)} %collective-permute-done.7.refs_1_.refs_2_, ...), custom_call_target="tpu_custom_call" | custom-call | flops 99999997952 | bytes 1 | tf_op jit(solution)/shard_map/share_passing/pallas_call | solution.py:265
  79.1 0.4 collective-permute-start.17
  79.4 1.7 %collective-permute-start.16 = (bf16[512,768]{1,0:T(8,128)(2,1)S(1)}, bf16[512,768]{1,0:T(8,128)(2,1)S(1)}, u32[]{:S(2)}, u32[]{:S(2)}) collective-permute-start(bf16[512,768]{1,0:T(8,128)(2,1)S(1)} %get-tuple-element.39.refs_8_), channel_id=1, source_target_pairs={{0,2},{1,3},{2,4},{3,5},{4,6},{5,7},{6,0},{7,1},{8,10},{9,11},{10,... | collective-permute-start | bytes 2359304 | tf_op jit(solution)/shard_map/ppermute | solution.py:323
  81.2 4.2 %collective-permute-done.12.refs_6_ = bf16[512,768]{1,0:T(8,128)(2,1)S(1)} collective-permute-done((bf16[512,768]{1,0:T(8,128)(2,1)S(1)}, bf16[512,768]{1,0:T(8,128)(2,1)S(1)}, u32[]{:S(2)}, u32[]{:S(2)}) %collective-permute-start.12) | collective-permute-done | bytes 786464 | tf_op jit(solution)/shard_map/ppermute | solution.py:324
  85.4 3.7 %collective-permute-done.13.refs_7_ = bf16[512,768]{1,0:T(8,128)(2,1)S(1)} collective-permute-done((bf16[512,768]{1,0:T(8,128)(2,1)S(1)}, bf16[512,768]{1,0:T(8,128)(2,1)S(1)}, u32[]{:S(2)}, u32[]{:S(2)}) %collective-permute-start.13) | collective-permute-done | bytes 786464 | tf_op jit(solution)/shard_map/ppermute | solution.py:323
  89.1 7.9 %share_own.1 = (f32[512,768]{1,0:T(8,128)S(1)}, f32[512,768]{1,0:T(8,128)S(1)}) custom-call(bf16[512,1024]{1,0:T(8,128)(2,1)S(1)} %hidden_rows.2.refs_8_.refs_0_, bf16[512,1024]{1,0:T(8,128)(2,1)S(1)} %hidden_rows.3.refs_4_.refs_0_.refs_1_, bf16[512,1024]{1,0:T(8,128)(2,1)S(1)} %collective-permute-done.7.refs_1_.refs_2_, ...), custom_call_target="tpu_custom_call" | custom-call | flops 1 | bytes 1 | tf_op jit(solution)/shard_map/share_own/pallas_call | solution.py:265
  97.0 3.9 %collective-permute-done.17.add_ref = bf16[512,768]{1,0:T(8,128)(2,1)S(1)} collective-permute-done((bf16[512,768]{1,0:T(8,128)(2,1)S(1)}, bf16[512,768]{1,0:T(8,128)(2,1)S(1)}, u32[]{:S(2)}, u32[]{:S(2)}) %collective-permute-start.17) | collective-permute-done | bytes 786464 | tf_op jit(solution)/shard_map/ppermute | solution.py:324
  100.9 0.9 finish.2.refs_0_
  101.8 2.5 %collective-permute-done.16.add_ref = bf16[512,768]{1,0:T(8,128)(2,1)S(1)} collective-permute-done((bf16[512,768]{1,0:T(8,128)(2,1)S(1)}, bf16[512,768]{1,0:T(8,128)(2,1)S(1)}, u32[]{:S(2)}, u32[]{:S(2)}) %collective-permute-start.16) | collective-permute-done | bytes 786464 | tf_op jit(solution)/shard_map/ppermute | solution.py:323
  104.3 0.9 finish.3
  (1 shorter events, 0.0 us)
Async XLA Ops:
  3.8 17.3 %collective-permute-start.2 = (bf16[1024,128]{1,0:T(8,128)(2,1)S(1)}, bf16[1024,128]{1,0:T(8,128)(2,1)S(1)}, u32[]{:S(2)}, u32[]{:S(2)}) collective-permute-start(bf16[1024,128]{1,0:T(8,128)(2,1)S(1)} %local_states.1.after_ref), channel_id=1, source_target_pairs={{0,8},{8,16},{16,24},{24,0},{32,40},{40,48},{48,56},{56,32},{64,72... | collective-permute-start | bytes 786440 | tf_op jit(solution)/shard_map/ppermute | solution.py:307
  5.4 15.7 %collective-permute-start.1 = (bf16[1024,128]{1,0:T(8,128)(2,1)S(1)}, bf16[1024,128]{1,0:T(8,128)(2,1)S(1)}, u32[]{:S(2)}, u32[]{:S(2)}) collective-permute-start(bf16[1024,128]{1,0:T(8,128)(2,1)S(1)} %local_states.1.after_ref), channel_id=1, source_target_pairs={{0,24},{8,0},{16,8},{24,16},{32,56},{40,32},{48,40},{56,48},{64,88... | collective-permute-start | bytes 786440 | tf_op jit(solution)/shard_map/ppermute | solution.py:307
  7.1 14.0 %collective-permute-start = (bf16[1024,128]{1,0:T(8,128)(2,1)S(1)}, bf16[1024,128]{1,0:T(8,128)(2,1)S(1)}, u32[]{:S(2)}, u32[]{:S(2)}) collective-permute-start(bf16[1024,128]{1,0:T(8,128)(2,1)S(1)} %local_states.1.after_ref), channel_id=1, source_target_pairs={{0,16},{8,24},{16,0},{24,8},{32,48},{40,56},{48,32},{56,40},{64,80... | collective-permute-start | bytes 786440 | tf_op jit(solution)/shard_map/ppermute | solution.py:307
  20.6 22.9 %collective-permute-start.9 = (bf16[1,1024,768]{2,1,0:T(8,128)(2,1)}, bf16[1,1024,768]{2,1,0:T(8,128)(2,1)S(1)}, u32[]{:S(2)}, u32[]{:S(2)}) collective-permute-start(bf16[1,1024,768]{2,1,0:T(8,128)(2,1)} %get-tuple-element.30), channel_id=1, source_target_pairs={{0,1},{1,0},{2,3},{3,2},{4,5},{5,4},{6,7},{7,6},{8,9},{9,8},{10,11... | collective-permute-start | bytes 4718600 | tf_op jit(solution)/shard_map/ppermute | solution.py:309
  20.6 19.5 %collective-permute-start.6 = (bf16[3,1024,768]{2,1,0:T(8,128)(2,1)}, bf16[3,1024,768]{2,1,0:T(8,128)(2,1)}, u32[]{:S(2)}, u32[]{:S(2)}) collective-permute-start(bf16[3,1024,768]{2,1,0:T(8,128)(2,1)} %get-tuple-element.28), channel_id=1, source_target_pairs={{0,1},{1,0},{2,3},{3,2},{4,5},{5,4},{6,7},{7,6},{8,9},{9,8},{10,11... | collective-permute-start | bytes 14155784 | tf_op jit(solution)/shard_map/ppermute | solution.py:309
  21.4 18.8 %copy-start.1 = (bf16[1024,1024]{1,0:T(8,128)(2,1)S(1)}, bf16[1024,1024]{1,0:T(8,128)(2,1)}, u32[]{:S(2)}) copy-start(bf16[1024,1024]{1,0:T(8,128)(2,1)} %refs_2_.3) | copy-start | bytes 6291460
  21.4 18.7 %copy-start.2 = (f32[1024]{0:T(1024)S(1)}, f32[1024]{0:T(1024)}, u32[]{:S(2)}) copy-start(f32[1024]{0:T(1024)} %param.10) | copy-start | bytes 12292
  21.4 17.2 %collective-permute-start.5 = (bf16[1024,128]{1,0:T(8,128)(2,1)S(1)}, bf16[1024,128]{1,0:T(8,128)(2,1)S(1)}, u32[]{:S(2)}, u32[]{:S(2)}) collective-permute-start(bf16[1024,128]{1,0:T(8,128)(2,1)S(1)} %get-tuple-element.43), channel_id=1, source_target_pairs={{0,32},{8,40},{16,48},{24,56},{32,64},{40,72},{48,80},{56,88},{64,... | collective-permute-start | bytes 786440 | tf_op jit(solution)/shard_map/ppermute | solution.py:320
  25.4 14.7 %collective-permute-start.4 = (bf16[1024,128]{1,0:T(8,128)(2,1)S(1)}, bf16[1024,128]{1,0:T(8,128)(2,1)S(1)}, u32[]{:S(2)}, u32[]{:S(2)}) collective-permute-start(bf16[1024,128]{1,0:T(8,128)(2,1)S(1)} %get-tuple-element.43), channel_id=1, source_target_pairs={{0,96},{8,104},{16,112},{24,120},{1,97},{9,105},{17,113},{25,121},... | collective-permute-start | bytes 786440 | tf_op jit(solution)/shard_map/ppermute | solution.py:320
  28.8 11.3 %collective-permute-start.3 = (bf16[1024,128]{1,0:T(8,128)(2,1)S(1)}, bf16[1024,128]{1,0:T(8,128)(2,1)S(1)}, u32[]{:S(2)}, u32[]{:S(2)}) collective-permute-start(bf16[1024,128]{1,0:T(8,128)(2,1)S(1)} %get-tuple-element.43), channel_id=1, source_target_pairs={{0,64},{8,72},{16,80},{24,88},{32,96},{40,104},{48,112},{56,120},{... | collective-permute-start | bytes 786440 | tf_op jit(solution)/shard_map/ppermute | solution.py:320
  41.5 2.8 %copy-start = (bf16[4,1024,768]{2,1,0:T(8,128)(2,1)S(1)}, bf16[4,1024,768]{2,1,0:T(8,128)(2,1)}, u32[]{:S(2)}) copy-start(bf16[4,1024,768]{2,1,0:T(8,128)(2,1)} %get-tuple-element.29.refs_2_.refs_4_) | copy-start | bytes 18874372
  41.5 2.7 %collective-permute-start.7 = (bf16[512,1024]{1,0:T(8,128)(2,1)S(1)}, bf16[512,1024]{1,0:T(8,128)(2,1)S(1)}, u32[]{:S(2)}, u32[]{:S(2)}) collective-permute-start(bf16[512,1024]{1,0:T(8,128)(2,1)S(1)} %hidden_rows.2.refs_8_.refs_0_), channel_id=1, source_target_pairs={{0,1},{1,0},{2,3},{3,2},{4,5},{5,4},{6,7},{7,6},{8,9},{9,8},{10,11... | collective-permute-start | bytes 3145736 | tf_op jit(solution)/shard_map/ppermute | solution.py:309
  43.0 7.2 %collective-permute-start.8 = (bf16[512,1024]{1,0:T(8,128)(2,1)S(1)}, bf16[512,1024]{1,0:T(8,128)(2,1)S(1)}, u32[]{:S(2)}, u32[]{:S(2)}) collective-permute-start(bf16[512,1024]{1,0:T(8,128)(2,1)S(1)} %hidden_rows.3.refs_4_.refs_0_.refs_1_), channel_id=1, source_target_pairs={{0,1},{1,0},{2,3},{3,2},{4,5},{5,4},{6,7},{7,6},{8,9},{9,8},{10,11... | collective-permute-start | bytes 3145736 | tf_op jit(solution)/shard_map/ppermute | solution.py:309
  47.0 17.0 %collective-permute-start.11 = (bf16[256,768]{1,0:T(8,128)(2,1)S(1)}, bf16[256,768]{1,0:T(8,128)(2,1)S(1)}, u32[]{:S(2)}, u32[]{:S(2)}) collective-permute-start(bf16[256,768]{1,0:T(8,128)(2,1)S(1)} %get-tuple-element.35), channel_id=1, source_target_pairs={{0,6},{1,7},{2,0},{3,1},{4,2},{5,3},{6,4},{7,5},{8,14},{9,15},{10,... | collective-permute-start | bytes 1179656 | tf_op jit(solution)/shard_map/ppermute | solution.py:324
  50.1 14.0 %collective-permute-start.10 = (bf16[256,768]{1,0:T(8,128)(2,1)S(1)}, bf16[256,768]{1,0:T(8,128)(2,1)S(1)}, u32[]{:S(2)}, u32[]{:S(2)}) collective-permute-start(bf16[256,768]{1,0:T(8,128)(2,1)S(1)} %get-tuple-element.31.refs_4_), channel_id=1, source_target_pairs={{0,2},{1,3},{2,4},{3,5},{4,6},{5,7},{6,0},{7,1},{8,10},{9,11},{10,... | collective-permute-start | bytes 1179656 | tf_op jit(solution)/shard_map/ppermute | solution.py:323
  52.9 14.9 %collective-permute-start.15 = (bf16[256,768]{1,0:T(8,128)(2,1)S(1)}, bf16[256,768]{1,0:T(8,128)(2,1)S(1)}, u32[]{:S(2)}, u32[]{:S(2)}) collective-permute-start(bf16[256,768]{1,0:T(8,128)(2,1)S(1)} %get-tuple-element.38), channel_id=1, source_target_pairs={{0,6},{1,7},{2,0},{3,1},{4,2},{5,3},{6,4},{7,5},{8,14},{9,15},{10,... | collective-permute-start | bytes 1179656 | tf_op jit(solution)/shard_map/ppermute | solution.py:324
  56.2 15.0 %collective-permute-start.14 = (bf16[256,768]{1,0:T(8,128)(2,1)S(1)}, bf16[256,768]{1,0:T(8,128)(2,1)S(1)}, u32[]{:S(2)}, u32[]{:S(2)}) collective-permute-start(bf16[256,768]{1,0:T(8,128)(2,1)S(1)} %get-tuple-element.32.refs_6_), channel_id=1, source_target_pairs={{0,2},{1,3},{2,4},{3,5},{4,6},{5,7},{6,0},{7,1},{8,10},{9,11},{10,... | collective-permute-start | bytes 1179656 | tf_op jit(solution)/shard_map/ppermute | solution.py:323
  64.1 21.3 %collective-permute-start.12 = (bf16[512,768]{1,0:T(8,128)(2,1)S(1)}, bf16[512,768]{1,0:T(8,128)(2,1)S(1)}, u32[]{:S(2)}, u32[]{:S(2)}) collective-permute-start(bf16[512,768]{1,0:T(8,128)(2,1)S(1)} %get-tuple-element.36), channel_id=1, source_target_pairs={{0,6},{1,7},{2,0},{3,1},{4,2},{5,3},{6,4},{7,5},{8,14},{9,15},{10,... | collective-permute-start | bytes 2359304 | tf_op jit(solution)/shard_map/ppermute | solution.py:324
  67.4 21.7 %collective-permute-start.13 = (bf16[512,768]{1,0:T(8,128)(2,1)S(1)}, bf16[512,768]{1,0:T(8,128)(2,1)S(1)}, u32[]{:S(2)}, u32[]{:S(2)}) collective-permute-start(bf16[512,768]{1,0:T(8,128)(2,1)S(1)} %get-tuple-element.37.refs_10_), channel_id=1, source_target_pairs={{0,2},{1,3},{2,4},{3,5},{4,6},{5,7},{6,0},{7,1},{8,10},{9,11},{10,... | collective-permute-start | bytes 2359304 | tf_op jit(solution)/shard_map/ppermute | solution.py:323
  79.1 21.8 %collective-permute-start.17 = (bf16[512,768]{1,0:T(8,128)(2,1)S(1)}, bf16[512,768]{1,0:T(8,128)(2,1)S(1)}, u32[]{:S(2)}, u32[]{:S(2)}) collective-permute-start(bf16[512,768]{1,0:T(8,128)(2,1)S(1)} %get-tuple-element.42), channel_id=1, source_target_pairs={{0,6},{1,7},{2,0},{3,1},{4,2},{5,3},{6,4},{7,5},{8,14},{9,15},{10,... | collective-permute-start | bytes 2359304 | tf_op jit(solution)/shard_map/ppermute | solution.py:324
  79.4 24.9 %collective-permute-start.16 = (bf16[512,768]{1,0:T(8,128)(2,1)S(1)}, bf16[512,768]{1,0:T(8,128)(2,1)S(1)}, u32[]{:S(2)}, u32[]{:S(2)}) collective-permute-start(bf16[512,768]{1,0:T(8,128)(2,1)S(1)} %get-tuple-element.39.refs_8_), channel_id=1, source_target_pairs={{0,2},{1,3},{2,4},{3,5},{4,6},{5,7},{6,0},{7,1},{8,10},{9,11},{10,... | collective-permute-start | bytes 2359304 | tf_op jit(solution)/shard_map/ppermute | solution.py:323

commit v4 on v3

--- a/solution.py
+++ b/solution.py
@@ -281,7 +281,7 @@
 
 def finish(part, value, add, begun=()):
     rows, width = value.shape
-    block = rows // 2
+    block = rows // 4
     return call(
         finish_kernel,
         name="finish",
@@ -317,7 +317,7 @@
         total += wide
         earlier += jnp.where(k <= x, wide, 0.0)
     total = total.astype(BF16)
-    along_z = [lax.ppermute(total, "ctx", later_z(k)) for k in (2, 3, 1)]
+    along_z = [lax.ppermute(total, "ctx", later_z(k)) for k in (3, 2, 1)]
     parts = [earlier, *along_z]
 
     up = lambda a: lax.ppermute(a, "tp", shift_y(1))

time: 106 us -> 106 us (level)
  Pallas kernels: 56 us -> 57.1 us
    pallas_call x2, Pallas kernels: 1.88 us -> 2.97 us  [finish(): call(finish_kernel, name='finish', grid=(rows // block,), in_specs=[IN_VM...]
where the time goes in v4:
time: 106 us
  Pallas kernels  57.1 us (54%)
  starting transfers between devices  29 us (27%)
  waiting for transfers between devices  19.5 us (18%)
    pallas_call x5, Pallas kernels, project(): call(functools.partial(project_kernel, blocks, plan, len(own), len(adds),...  29 us
    pallas_call x1, Pallas kernels, sort_columns(): call(sort_columns_kernel, vmem=24, name='sort_columns', grid_spec=pltpu.P...  11.5 us
    ppermute x3, starting transfers between devices, on_device(): along_z = [lax.ppermute(total, 'ctx', later_z(k)) for k in (3, 2, 1)]  10.8 us
    ppermute x4, starting transfers between devices, on_device(): down = lambda a: lax.ppermute(a, 'tp', shift_y(-1))  10.1 us
    ppermute x4, waiting for transfers between devices, on_device(): up = lambda a: lax.ppermute(a, 'tp', shift_y(1))  9.03 us
    ppermute x4, waiting for transfers between devices, on_device(): down = lambda a: lax.ppermute(a, 'tp', shift_y(-1))  8.6 us
    pallas_call x1, Pallas kernels, intra_block(): call(intra_kernel, name='intra_block', vmem=28, flops=10 ** 11, grid=(wid...  7.04 us
    ppermute x3, starting transfers between devices, on_device(): along_x = [lax.ppermute(state, 'ctx', shift_x(k)) for k in (2, 3, 1)]  5.2 us
  transfers between devices with their start and end apart: 18, of which 8 were waited for; matrix products, arithmetic and copies ran while one was open for 0% of the time, Pallas kernels for 49%

profile of v4, /device:TPU:0, one launch (start us, length us, event | category | flops | bytes accessed | tf_op | source)
XLA Modules:
  0.0 106.1 jit_solution(13272054453045878492)
XLA Ops:
  0.0 3.8 %local_states.1.after_ref = bf16[1024,128]{1,0:T(8,128)(2,1)S(1)} custom-call(bf16[1024,1024]{1,0:T(8,128)(2,1)} %k_ref.3, bf16[1024,1024]{1,0:T(8,128)(2,1)} %v_ref.3), custom_call_target="tpu_custom_call" | custom-call | flops 1 | bytes 1 | tf_op jit(solution)/shard_map/local_states/pallas_call | solution.py:76
  3.8 1.6 %collective-permute-start.2 = (bf16[1024,128]{1,0:T(8,128)(2,1)S(1)}, bf16[1024,128]{1,0:T(8,128)(2,1)S(1)}, u32[]{:S(2)}, u32[]{:S(2)}) collective-permute-start(bf16[1024,128]{1,0:T(8,128)(2,1)S(1)} %local_states.1.after_ref), channel_id=1, source_target_pairs={{0,8},{8,16},{16,24},{24,0},{32,40},{40,48},{48,56},{56,32},{64,72... | collective-permute-start | bytes 786440 | tf_op jit(solution)/shard_map/ppermute | solution.py:307
  5.4 1.7 %collective-permute-start.1 = (bf16[1024,128]{1,0:T(8,128)(2,1)S(1)}, bf16[1024,128]{1,0:T(8,128)(2,1)S(1)}, u32[]{:S(2)}, u32[]{:S(2)}) collective-permute-start(bf16[1024,128]{1,0:T(8,128)(2,1)S(1)} %local_states.1.after_ref), channel_id=1, source_target_pairs={{0,24},{8,0},{16,8},{24,16},{32,56},{40,32},{48,40},{56,48},{64,88... | collective-permute-start | bytes 786440 | tf_op jit(solution)/shard_map/ppermute | solution.py:307
  7.1 1.9 %collective-permute-start = (bf16[1024,128]{1,0:T(8,128)(2,1)S(1)}, bf16[1024,128]{1,0:T(8,128)(2,1)S(1)}, u32[]{:S(2)}, u32[]{:S(2)}) collective-permute-start(bf16[1024,128]{1,0:T(8,128)(2,1)S(1)} %local_states.1.after_ref), channel_id=1, source_target_pairs={{0,16},{8,24},{16,0},{24,8},{32,48},{40,56},{48,32},{56,40},{64,80... | collective-permute-start | bytes 786440 | tf_op jit(solution)/shard_map/ppermute | solution.py:307
  9.0 0.1 stack.35.blocks_ref
  9.1 11.5 %sort_columns.1 = (bf16[1,1024,768]{2,1,0:T(8,128)(2,1)}, bf16[3,1024,768]{2,1,0:T(8,128)(2,1)}, bf16[4,1024,768]{2,1,0:T(8,128)(2,1)}) custom-call(s32[8]{0:T(128)S(1)} %stack.35.blocks_ref, bf16[1024,6144]{1,0:T(8,128)(2,1)} %weight_ref.1, bf16[1024,128]{1,0:T(8,128)(2,1)S(1)} %local_states.1.after_ref), custom_call_target="tpu_custom_call" | custom-call | flops 1 | bytes 1 | tf_op jit(solution)/shard_map/sort_columns/pallas_call | solution.py:165
  20.6 0.0 collective-permute-start.9
  20.6 0.5 collective-permute-start.6
  21.1 0.0 collective-permute-done.2
  21.1 0.0 collective-permute-done.1
  21.1 0.0 collective-permute-done
  21.1 0.2 fusion.2
  21.4 0.0 copy-start.1
  21.4 0.0 copy-start.2
  21.4 4.0 %collective-permute-start.5 = (bf16[1024,128]{1,0:T(8,128)(2,1)S(1)}, bf16[1024,128]{1,0:T(8,128)(2,1)S(1)}, u32[]{:S(2)}, u32[]{:S(2)}) collective-permute-start(bf16[1024,128]{1,0:T(8,128)(2,1)S(1)} %get-tuple-element.43), channel_id=1, source_target_pairs={{0,32},{8,40},{16,48},{24,56},{32,64},{40,72},{48,80},{56,88},{64,... | collective-permute-start | bytes 786440 | tf_op jit(solution)/shard_map/ppermute | solution.py:320
  25.4 5.5 %collective-permute-start.4 = (bf16[1024,128]{1,0:T(8,128)(2,1)S(1)}, bf16[1024,128]{1,0:T(8,128)(2,1)S(1)}, u32[]{:S(2)}, u32[]{:S(2)}) collective-permute-start(bf16[1024,128]{1,0:T(8,128)(2,1)S(1)} %get-tuple-element.43), channel_id=1, source_target_pairs={{0,64},{8,72},{16,80},{24,88},{32,96},{40,104},{48,112},{56,120},{... | collective-permute-start | bytes 786440 | tf_op jit(solution)/shard_map/ppermute | solution.py:320
  30.9 1.3 %collective-permute-start.3 = (bf16[1024,128]{1,0:T(8,128)(2,1)S(1)}, bf16[1024,128]{1,0:T(8,128)(2,1)S(1)}, u32[]{:S(2)}, u32[]{:S(2)}) collective-permute-start(bf16[1024,128]{1,0:T(8,128)(2,1)S(1)} %get-tuple-element.43), channel_id=1, source_target_pairs={{0,96},{8,104},{16,112},{24,120},{1,97},{9,105},{17,113},{25,121},... | collective-permute-start | bytes 786440 | tf_op jit(solution)/shard_map/ppermute | solution.py:320
  32.2 7.0 %intra_block.1 = (f32[1024,1024]{1,0:T(8,128)S(1)}, bf16[1024,1024]{1,0:T(8,128)(2,1)S(1)}) custom-call(bf16[1024,1024]{1,0:T(8,128)(2,1)} %q_ref.1, bf16[1024,1024]{1,0:T(8,128)(2,1)} %k_ref.3, bf16[1024,1024]{1,0:T(8,128)(2,1)} %v_ref.3, bf16[1024,128]{1,0:T(8,128)(2,1)S(1)} %local_states.1.after_ref), custom_call_target="tpu_custom_call" | custom-call | flops 99999997952 | bytes 1 | tf_op jit(solution)/shard_map/intra_block/pallas_call | solution.py:131
  39.2 0.0 collective-permute-done.5.refs_7_
  39.2 0.0 collective-permute-done.4.refs_6_
  39.2 1.2 %collective-permute-done.3.refs_5_ = bf16[1024,128]{1,0:T(8,128)(2,1)S(1)} collective-permute-done((bf16[1024,128]{1,0:T(8,128)(2,1)S(1)}, bf16[1024,128]{1,0:T(8,128)(2,1)S(1)}, u32[]{:S(2)}, u32[]{:S(2)}) %collective-permute-start.3) | collective-permute-done | bytes 262176 | tf_op jit(solution)/shard_map/ppermute | solution.py:320
  40.4 0.0 collective-permute-done.6.refs_8_.refs_5_
  40.4 0.0 copy-done.1
  40.4 0.0 copy-done.2
  40.4 1.4 %hidden_rows.2.refs_8_.refs_0_ = bf16[512,1024]{1,0:T(8,128)(2,1)S(1)} custom-call(f32[1024,1024]{1,0:T(8,128)S(1)} %get-tuple-element.26.refs_0_, bf16[1024,1024]{1,0:T(8,128)(2,1)S(1)} %get-tuple-element.27.refs_1_, bf16[1024,1024]{1,0:T(8,128)(2,1)S(1)} %copy-done.1, f32[1,1024]{1,0:T(1,128)S(1)} %bitcast.9, f32[1024,128]{1,0:T(8,128)S(1)} %get-tuple-element.44.refs_4_, ...), custom_call_target="tpu_custom_call" | custom-call | flops 1 | bytes 1 | tf_op jit(solution)/shard_map/hidden_rows/pallas_call | solution.py:226
  41.8 0.0 copy-start
  41.8 0.1 collective-permute-start.7
  41.9 1.4 %hidden_rows.3.refs_4_.refs_0_.refs_1_ = bf16[512,1024]{1,0:T(8,128)(2,1)S(1)} custom-call(f32[1024,1024]{1,0:T(8,128)S(1)} %get-tuple-element.26.refs_0_, bf16[1024,1024]{1,0:T(8,128)(2,1)S(1)} %get-tuple-element.27.refs_1_, bf16[1024,1024]{1,0:T(8,128)(2,1)S(1)} %copy-done.1, f32[1,1024]{1,0:T(1,128)S(1)} %bitcast.10, ...), custom_call_target="tpu_custom_call" | custom-call | flops 1 | bytes 1 | tf_op jit(solution)/shard_map/hidden_rows/pallas_call | solution.py:226
  43.2 0.6 collective-permute-start.8
  43.8 0.0 collective-permute-done.9.refs_3_
  43.8 0.7 collective-permute-done.7.refs_1_.refs_2_
  44.5 0.0 copy-done
  44.6 2.7 %share_far.2 = (bf16[256,768]{1,0:T(8,128)(2,1)S(1)}, bf16[256,768]{1,0:T(8,128)(2,1)S(1)}) custom-call(bf16[512,1024]{1,0:T(8,128)(2,1)S(1)} %hidden_rows.2.refs_8_.refs_0_, bf16[512,1024]{1,0:T(8,128)(2,1)S(1)} %collective-permute-done.7.refs_1_.refs_2_, bf16[4,1024,768]{2,1,0:T(8,128)(2,1)S(1)} %copy-done, ...), custom_call_target="tpu_custom_call" | custom-call | flops 99999997952 | bytes 1 | tf_op jit(solution)/shard_map/share_far/pallas_call | solution.py:265
  47.3 3.1 %collective-permute-start.11 = (bf16[256,768]{1,0:T(8,128)(2,1)S(1)}, bf16[256,768]{1,0:T(8,128)(2,1)S(1)}, u32[]{:S(2)}, u32[]{:S(2)}) collective-permute-start(bf16[256,768]{1,0:T(8,128)(2,1)S(1)} %get-tuple-element.35), channel_id=1, source_target_pairs={{0,6},{1,7},{2,0},{3,1},{4,2},{5,3},{6,4},{7,5},{8,14},{9,15},{10,... | collective-permute-start | bytes 1179656 | tf_op jit(solution)/shard_map/ppermute | solution.py:324
  50.4 0.0 collective-permute-start.10
  50.4 0.0 collective-permute-done.8.refs_1_.refs_3_
  50.4 2.7 %share_far.3 = (bf16[256,768]{1,0:T(8,128)(2,1)S(1)}, bf16[256,768]{1,0:T(8,128)(2,1)S(1)}) custom-call(bf16[512,1024]{1,0:T(8,128)(2,1)S(1)} %hidden_rows.3.refs_4_.refs_0_.refs_1_, bf16[512,1024]{1,0:T(8,128)(2,1)S(1)} %collective-permute-done.8.refs_1_.refs_3_, bf16[4,1024,768]{2,1,0:T(8,128)(2,1)S(1)} %copy-done, ...), custom_call_target="tpu_custom_call" | custom-call | flops 1 | bytes 1 | tf_op jit(solution)/shard_map/share_far/pallas_call | solution.py:265
  53.2 3.3 %collective-permute-start.15 = (bf16[256,768]{1,0:T(8,128)(2,1)S(1)}, bf16[256,768]{1,0:T(8,128)(2,1)S(1)}, u32[]{:S(2)}, u32[]{:S(2)}) collective-permute-start(bf16[256,768]{1,0:T(8,128)(2,1)S(1)} %get-tuple-element.38), channel_id=1, source_target_pairs={{0,6},{1,7},{2,0},{3,1},{4,2},{5,3},{6,4},{7,5},{8,14},{9,15},{10,... | collective-permute-start | bytes 1179656 | tf_op jit(solution)/shard_map/ppermute | solution.py:324
  56.5 0.0 collective-permute-start.14
  56.5 7.9 %share_near.1 = (bf16[512,768]{1,0:T(8,128)(2,1)S(1)}, bf16[512,768]{1,0:T(8,128)(2,1)S(1)}) custom-call(bf16[512,1024]{1,0:T(8,128)(2,1)S(1)} %hidden_rows.2.refs_8_.refs_0_, bf16[512,1024]{1,0:T(8,128)(2,1)S(1)} %hidden_rows.3.refs_4_.refs_0_.refs_1_, bf16[512,1024]{1,0:T(8,128)(2,1)S(1)} %collective-permute-done.7.refs_1_.refs_2_, ...), custom_call_target="tpu_custom_call" | custom-call | flops 1 | bytes 1 | tf_op jit(solution)/shard_map/share_near/pallas_call | solution.py:265
  64.3 0.0 collective-permute-done.11.refs_3_.refs_8_
  64.4 0.0 collective-permute-done.10.refs_2_.refs_6_
  64.4 3.3 %collective-permute-start.12 = (bf16[512,768]{1,0:T(8,128)(2,1)S(1)}, bf16[512,768]{1,0:T(8,128)(2,1)S(1)}, u32[]{:S(2)}, u32[]{:S(2)}) collective-permute-start(bf16[512,768]{1,0:T(8,128)(2,1)S(1)} %get-tuple-element.36), channel_id=1, source_target_pairs={{0,6},{1,7},{2,0},{3,1},{4,2},{5,3},{6,4},{7,5},{8,14},{9,15},{10,... | collective-permute-start | bytes 2359304 | tf_op jit(solution)/shard_map/ppermute | solution.py:324
  67.7 0.0 collective-permute-start.13
  67.7 0.4 collective-permute-done.15.refs_9_
  68.1 3.4 %collective-permute-done.14.refs_7_ = bf16[256,768]{1,0:T(8,128)(2,1)S(1)} collective-permute-done((bf16[256,768]{1,0:T(8,128)(2,1)S(1)}, bf16[256,768]{1,0:T(8,128)(2,1)S(1)}, u32[]{:S(2)}, u32[]{:S(2)}) %collective-permute-start.14) | collective-permute-done | bytes 393248 | tf_op jit(solution)/shard_map/ppermute | solution.py:323
  71.5 7.8 %share_passing.1 = (bf16[512,768]{1,0:T(8,128)(2,1)S(1)}, bf16[512,768]{1,0:T(8,128)(2,1)S(1)}) custom-call(bf16[512,1024]{1,0:T(8,128)(2,1)S(1)} %hidden_rows.2.refs_8_.refs_0_, bf16[512,1024]{1,0:T(8,128)(2,1)S(1)} %hidden_rows.3.refs_4_.refs_0_.refs_1_, bf16[512,1024]{1,0:T(8,128)(2,1)S(1)} %collective-permute-done.7.refs_1_.refs_2_, ...), custom_call_target="tpu_custom_call" | custom-call | flops 99999997952 | bytes 1 | tf_op jit(solution)/shard_map/share_passing/pallas_call | solution.py:265
  79.3 0.4 collective-permute-start.17
  79.7 1.7 %collective-permute-start.16 = (bf16[512,768]{1,0:T(8,128)(2,1)S(1)}, bf16[512,768]{1,0:T(8,128)(2,1)S(1)}, u32[]{:S(2)}, u32[]{:S(2)}) collective-permute-start(bf16[512,768]{1,0:T(8,128)(2,1)S(1)} %get-tuple-element.39.refs_8_), channel_id=1, source_target_pairs={{0,2},{1,3},{2,4},{3,5},{4,6},{5,7},{6,0},{7,1},{8,10},{9,11},{10,... | collective-permute-start | bytes 2359304 | tf_op jit(solution)/shard_map/ppermute | solution.py:323
  81.4 4.2 %collective-permute-done.12.refs_6_ = bf16[512,768]{1,0:T(8,128)(2,1)S(1)} collective-permute-done((bf16[512,768]{1,0:T(8,128)(2,1)S(1)}, bf16[512,768]{1,0:T(8,128)(2,1)S(1)}, u32[]{:S(2)}, u32[]{:S(2)}) %collective-permute-start.12) | collective-permute-done | bytes 786464 | tf_op jit(solution)/shard_map/ppermute | solution.py:324
  85.7 3.7 %collective-permute-done.13.refs_7_ = bf16[512,768]{1,0:T(8,128)(2,1)S(1)} collective-permute-done((bf16[512,768]{1,0:T(8,128)(2,1)S(1)}, bf16[512,768]{1,0:T(8,128)(2,1)S(1)}, u32[]{:S(2)}, u32[]{:S(2)}) %collective-permute-start.13) | collective-permute-done | bytes 786464 | tf_op jit(solution)/shard_map/ppermute | solution.py:323
  89.4 7.8 %share_own.1 = (f32[512,768]{1,0:T(8,128)S(1)}, f32[512,768]{1,0:T(8,128)S(1)}) custom-call(bf16[512,1024]{1,0:T(8,128)(2,1)S(1)} %hidden_rows.2.refs_8_.refs_0_, bf16[512,1024]{1,0:T(8,128)(2,1)S(1)} %hidden_rows.3.refs_4_.refs_0_.refs_1_, bf16[512,1024]{1,0:T(8,128)(2,1)S(1)} %collective-permute-done.7.refs_1_.refs_2_, ...), custom_call_target="tpu_custom_call" | custom-call | flops 1 | bytes 1 | tf_op jit(solution)/shard_map/share_own/pallas_call | solution.py:265
  97.2 3.9 %collective-permute-done.17.add_ref = bf16[512,768]{1,0:T(8,128)(2,1)S(1)} collective-permute-done((bf16[512,768]{1,0:T(8,128)(2,1)S(1)}, bf16[512,768]{1,0:T(8,128)(2,1)S(1)}, u32[]{:S(2)}, u32[]{:S(2)}) %collective-permute-start.17) | collective-permute-done | bytes 786464 | tf_op jit(solution)/shard_map/ppermute | solution.py:324
  101.2 1.5 %finish.2.refs_0_ = bf16[1024,768]{1,0:T(8,128)(2,1)} custom-call(f32[512,768]{1,0:T(8,128)S(1)} %get-tuple-element.41.value_ref, bf16[512,768]{1,0:T(8,128)(2,1)S(1)} %collective-permute-done.17.add_ref), custom_call_target="tpu_custom_call" | custom-call | flops 1 | bytes 1 | tf_op jit(solution)/shard_map/finish/pallas_call | solution.py:285
  102.7 1.9 %collective-permute-done.16.add_ref = bf16[512,768]{1,0:T(8,128)(2,1)S(1)} collective-permute-done((bf16[512,768]{1,0:T(8,128)(2,1)S(1)}, bf16[512,768]{1,0:T(8,128)(2,1)S(1)}, u32[]{:S(2)}, u32[]{:S(2)}) %collective-permute-start.16) | collective-permute-done | bytes 786464 | tf_op jit(solution)/shard_map/ppermute | solution.py:323
  104.6 1.5 %finish.3 = bf16[1024,768]{1,0:T(8,128)(2,1)} custom-call(f32[512,768]{1,0:T(8,128)S(1)} %get-tuple-element.40.value_ref, bf16[512,768]{1,0:T(8,128)(2,1)S(1)} %collective-permute-done.16.add_ref, bf16[1024,768]{1,0:T(8,128)(2,1)} %finish.2.refs_0_), custom_call_target="tpu_custom_call", output_to_operand_aliasing={{}: (2, {})} | custom-call | flops 1 | bytes 1 | tf_op jit(solution)/shard_map/finish/pallas_call | solution.py:285
  (1 shorter events, 0.0 us)
Async XLA Ops:
  3.8 17.3 %collective-permute-start.2 = (bf16[1024,128]{1,0:T(8,128)(2,1)S(1)}, bf16[1024,128]{1,0:T(8,128)(2,1)S(1)}, u32[]{:S(2)}, u32[]{:S(2)}) collective-permute-start(bf16[1024,128]{1,0:T(8,128)(2,1)S(1)} %local_states.1.after_ref), channel_id=1, source_target_pairs={{0,8},{8,16},{16,24},{24,0},{32,40},{40,48},{48,56},{56,32},{64,72... | collective-permute-start | bytes 786440 | tf_op jit(solution)/shard_map/ppermute | solution.py:307
  5.4 15.7 %collective-permute-start.1 = (bf16[1024,128]{1,0:T(8,128)(2,1)S(1)}, bf16[1024,128]{1,0:T(8,128)(2,1)S(1)}, u32[]{:S(2)}, u32[]{:S(2)}) collective-permute-start(bf16[1024,128]{1,0:T(8,128)(2,1)S(1)} %local_states.1.after_ref), channel_id=1, source_target_pairs={{0,24},{8,0},{16,8},{24,16},{32,56},{40,32},{48,40},{56,48},{64,88... | collective-permute-start | bytes 786440 | tf_op jit(solution)/shard_map/ppermute | solution.py:307
  7.1 14.0 %collective-permute-start = (bf16[1024,128]{1,0:T(8,128)(2,1)S(1)}, bf16[1024,128]{1,0:T(8,128)(2,1)S(1)}, u32[]{:S(2)}, u32[]{:S(2)}) collective-permute-start(bf16[1024,128]{1,0:T(8,128)(2,1)S(1)} %local_states.1.after_ref), channel_id=1, source_target_pairs={{0,16},{8,24},{16,0},{24,8},{32,48},{40,56},{48,32},{56,40},{64,80... | collective-permute-start | bytes 786440 | tf_op jit(solution)/shard_map/ppermute | solution.py:307
  20.6 23.2 %collective-permute-start.9 = (bf16[1,1024,768]{2,1,0:T(8,128)(2,1)}, bf16[1,1024,768]{2,1,0:T(8,128)(2,1)S(1)}, u32[]{:S(2)}, u32[]{:S(2)}) collective-permute-start(bf16[1,1024,768]{2,1,0:T(8,128)(2,1)} %get-tuple-element.30), channel_id=1, source_target_pairs={{0,1},{1,0},{2,3},{3,2},{4,5},{5,4},{6,7},{7,6},{8,9},{9,8},{10,11... | collective-permute-start | bytes 4718600 | tf_op jit(solution)/shard_map/ppermute | solution.py:309
  20.6 19.8 %collective-permute-start.6 = (bf16[3,1024,768]{2,1,0:T(8,128)(2,1)}, bf16[3,1024,768]{2,1,0:T(8,128)(2,1)}, u32[]{:S(2)}, u32[]{:S(2)}) collective-permute-start(bf16[3,1024,768]{2,1,0:T(8,128)(2,1)} %get-tuple-element.28), channel_id=1, source_target_pairs={{0,1},{1,0},{2,3},{3,2},{4,5},{5,4},{6,7},{7,6},{8,9},{9,8},{10,11... | collective-permute-start | bytes 14155784 | tf_op jit(solution)/shard_map/ppermute | solution.py:309
  21.4 19.0 %copy-start.1 = (bf16[1024,1024]{1,0:T(8,128)(2,1)S(1)}, bf16[1024,1024]{1,0:T(8,128)(2,1)}, u32[]{:S(2)}) copy-start(bf16[1024,1024]{1,0:T(8,128)(2,1)} %refs_2_.3) | copy-start | bytes 6291460
  21.4 19.0 %copy-start.2 = (f32[1024]{0:T(1024)S(1)}, f32[1024]{0:T(1024)}, u32[]{:S(2)}) copy-start(f32[1024]{0:T(1024)} %param.10) | copy-start | bytes 12292
  21.4 17.8 %collective-permute-start.5 = (bf16[1024,128]{1,0:T(8,128)(2,1)S(1)}, bf16[1024,128]{1,0:T(8,128)(2,1)S(1)}, u32[]{:S(2)}, u32[]{:S(2)}) collective-permute-start(bf16[1024,128]{1,0:T(8,128)(2,1)S(1)} %get-tuple-element.43), channel_id=1, source_target_pairs={{0,32},{8,40},{16,48},{24,56},{32,64},{40,72},{48,80},{56,88},{64,... | collective-permute-start | bytes 786440 | tf_op jit(solution)/shard_map/ppermute | solution.py:320
  25.4 13.9 %collective-permute-start.4 = (bf16[1024,128]{1,0:T(8,128)(2,1)S(1)}, bf16[1024,128]{1,0:T(8,128)(2,1)S(1)}, u32[]{:S(2)}, u32[]{:S(2)}) collective-permute-start(bf16[1024,128]{1,0:T(8,128)(2,1)S(1)} %get-tuple-element.43), channel_id=1, source_target_pairs={{0,64},{8,72},{16,80},{24,88},{32,96},{40,104},{48,112},{56,120},{... | collective-permute-start | bytes 786440 | tf_op jit(solution)/shard_map/ppermute | solution.py:320
  30.9 9.5 %collective-permute-start.3 = (bf16[1024,128]{1,0:T(8,128)(2,1)S(1)}, bf16[1024,128]{1,0:T(8,128)(2,1)S(1)}, u32[]{:S(2)}, u32[]{:S(2)}) collective-permute-start(bf16[1024,128]{1,0:T(8,128)(2,1)S(1)} %get-tuple-element.43), channel_id=1, source_target_pairs={{0,96},{8,104},{16,112},{24,120},{1,97},{9,105},{17,113},{25,121},... | collective-permute-start | bytes 786440 | tf_op jit(solution)/shard_map/ppermute | solution.py:320
  41.8 2.8 %copy-start = (bf16[4,1024,768]{2,1,0:T(8,128)(2,1)S(1)}, bf16[4,1024,768]{2,1,0:T(8,128)(2,1)}, u32[]{:S(2)}) copy-start(bf16[4,1024,768]{2,1,0:T(8,128)(2,1)} %get-tuple-element.29.refs_2_.refs_4_) | copy-start | bytes 18874372
  41.8 2.7 %collective-permute-start.7 = (bf16[512,1024]{1,0:T(8,128)(2,1)S(1)}, bf16[512,1024]{1,0:T(8,128)(2,1)S(1)}, u32[]{:S(2)}, u32[]{:S(2)}) collective-permute-start(bf16[512,1024]{1,0:T(8,128)(2,1)S(1)} %hidden_rows.2.refs_8_.refs_0_), channel_id=1, source_target_pairs={{0,1},{1,0},{2,3},{3,2},{4,5},{5,4},{6,7},{7,6},{8,9},{9,8},{10,11... | collective-permute-start | bytes 3145736 | tf_op jit(solution)/shard_map/ppermute | solution.py:309
  43.2 7.2 %collective-permute-start.8 = (bf16[512,1024]{1,0:T(8,128)(2,1)S(1)}, bf16[512,1024]{1,0:T(8,128)(2,1)S(1)}, u32[]{:S(2)}, u32[]{:S(2)}) collective-permute-start(bf16[512,1024]{1,0:T(8,128)(2,1)S(1)} %hidden_rows.3.refs_4_.refs_0_.refs_1_), channel_id=1, source_target_pairs={{0,1},{1,0},{2,3},{3,2},{4,5},{5,4},{6,7},{7,6},{8,9},{9,8},{10,11... | collective-permute-start | bytes 3145736 | tf_op jit(solution)/shard_map/ppermute | solution.py:309
  47.3 17.0 %collective-permute-start.11 = (bf16[256,768]{1,0:T(8,128)(2,1)S(1)}, bf16[256,768]{1,0:T(8,128)(2,1)S(1)}, u32[]{:S(2)}, u32[]{:S(2)}) collective-permute-start(bf16[256,768]{1,0:T(8,128)(2,1)S(1)} %get-tuple-element.35), channel_id=1, source_target_pairs={{0,6},{1,7},{2,0},{3,1},{4,2},{5,3},{6,4},{7,5},{8,14},{9,15},{10,... | collective-permute-start | bytes 1179656 | tf_op jit(solution)/shard_map/ppermute | solution.py:324
  50.4 14.0 %collective-permute-start.10 = (bf16[256,768]{1,0:T(8,128)(2,1)S(1)}, bf16[256,768]{1,0:T(8,128)(2,1)S(1)}, u32[]{:S(2)}, u32[]{:S(2)}) collective-permute-start(bf16[256,768]{1,0:T(8,128)(2,1)S(1)} %get-tuple-element.31.refs_4_), channel_id=1, source_target_pairs={{0,2},{1,3},{2,4},{3,5},{4,6},{5,7},{6,0},{7,1},{8,10},{9,11},{10,... | collective-permute-start | bytes 1179656 | tf_op jit(solution)/shard_map/ppermute | solution.py:323
  53.2 14.9 %collective-permute-start.15 = (bf16[256,768]{1,0:T(8,128)(2,1)S(1)}, bf16[256,768]{1,0:T(8,128)(2,1)S(1)}, u32[]{:S(2)}, u32[]{:S(2)}) collective-permute-start(bf16[256,768]{1,0:T(8,128)(2,1)S(1)} %get-tuple-element.38), channel_id=1, source_target_pairs={{0,6},{1,7},{2,0},{3,1},{4,2},{5,3},{6,4},{7,5},{8,14},{9,15},{10,... | collective-permute-start | bytes 1179656 | tf_op jit(solution)/shard_map/ppermute | solution.py:324
  56.5 15.0 %collective-permute-start.14 = (bf16[256,768]{1,0:T(8,128)(2,1)S(1)}, bf16[256,768]{1,0:T(8,128)(2,1)S(1)}, u32[]{:S(2)}, u32[]{:S(2)}) collective-permute-start(bf16[256,768]{1,0:T(8,128)(2,1)S(1)} %get-tuple-element.32.refs_6_), channel_id=1, source_target_pairs={{0,2},{1,3},{2,4},{3,5},{4,6},{5,7},{6,0},{7,1},{8,10},{9,11},{10,... | collective-permute-start | bytes 1179656 | tf_op jit(solution)/shard_map/ppermute | solution.py:323
  64.4 21.3 %collective-permute-start.12 = (bf16[512,768]{1,0:T(8,128)(2,1)S(1)}, bf16[512,768]{1,0:T(8,128)(2,1)S(1)}, u32[]{:S(2)}, u32[]{:S(2)}) collective-permute-start(bf16[512,768]{1,0:T(8,128)(2,1)S(1)} %get-tuple-element.36), channel_id=1, source_target_pairs={{0,6},{1,7},{2,0},{3,1},{4,2},{5,3},{6,4},{7,5},{8,14},{9,15},{10,... | collective-permute-start | bytes 2359304 | tf_op jit(solution)/shard_map/ppermute | solution.py:324
  67.7 21.7 %collective-permute-start.13 = (bf16[512,768]{1,0:T(8,128)(2,1)S(1)}, bf16[512,768]{1,0:T(8,128)(2,1)S(1)}, u32[]{:S(2)}, u32[]{:S(2)}) collective-permute-start(bf16[512,768]{1,0:T(8,128)(2,1)S(1)} %get-tuple-element.37.refs_10_), channel_id=1, source_target_pairs={{0,2},{1,3},{2,4},{3,5},{4,6},{5,7},{6,0},{7,1},{8,10},{9,11},{10,... | collective-permute-start | bytes 2359304 | tf_op jit(solution)/shard_map/ppermute | solution.py:323
  79.3 21.8 %collective-permute-start.17 = (bf16[512,768]{1,0:T(8,128)(2,1)S(1)}, bf16[512,768]{1,0:T(8,128)(2,1)S(1)}, u32[]{:S(2)}, u32[]{:S(2)}) collective-permute-start(bf16[512,768]{1,0:T(8,128)(2,1)S(1)} %get-tuple-element.42), channel_id=1, source_target_pairs={{0,6},{1,7},{2,0},{3,1},{4,2},{5,3},{6,4},{7,5},{8,14},{9,15},{10,... | collective-permute-start | bytes 2359304 | tf_op jit(solution)/shard_map/ppermute | solution.py:324
  79.7 24.9 %collective-permute-start.16 = (bf16[512,768]{1,0:T(8,128)(2,1)S(1)}, bf16[512,768]{1,0:T(8,128)(2,1)S(1)}, u32[]{:S(2)}, u32[]{:S(2)}) collective-permute-start(bf16[512,768]{1,0:T(8,128)(2,1)S(1)} %get-tuple-element.39.refs_8_), channel_id=1, source_target_pairs={{0,2},{1,3},{2,4},{3,5},{4,6},{5,7},{6,0},{7,1},{8,10},{9,11},{10,... | collective-permute-start | bytes 2359304 | tf_op jit(solution)/shard_map/ppermute | solution.py:323

commit v5 on v3

--- a/solution.py
+++ b/solution.py
@@ -281,7 +281,7 @@
 
 def finish(part, value, add, begun=()):
     rows, width = value.shape
-    block = rows // 2
+    block = rows
     return call(
         finish_kernel,
         name="finish",

time: 106 us -> 106 us (level)
  no operation moved by 1% of the time
where the time goes in v5:
time: 106 us; the launch traced here: 105 us
  Pallas kernels  56.1 us (53%)
  starting transfers between devices  28.3 us (27%)
  waiting for transfers between devices  20.3 us (19%)
    pallas_call x5, Pallas kernels, project(): call(functools.partial(project_kernel, blocks, plan, len(own), len(adds),...  29 us
    pallas_call x1, Pallas kernels, sort_columns(): call(sort_columns_kernel, vmem=24, name='sort_columns', grid_spec=pltpu.P...  11.5 us
    ppermute x3, starting transfers between devices, on_device(): along_z = [lax.ppermute(total, 'ctx', later_z(k)) for k in (2, 3, 1)]  10.1 us
    ppermute x4, starting transfers between devices, on_device(): down = lambda a: lax.ppermute(a, 'tp', shift_y(-1))  10.1 us
    ppermute x4, waiting for transfers between devices, on_device(): up = lambda a: lax.ppermute(a, 'tp', shift_y(1))  9.51 us
    ppermute x4, waiting for transfers between devices, on_device(): down = lambda a: lax.ppermute(a, 'tp', shift_y(-1))  8.59 us
    pallas_call x1, Pallas kernels, intra_block(): call(intra_kernel, name='intra_block', vmem=28, flops=10 ** 11, grid=(wid...  7.03 us
    ppermute x3, starting transfers between devices, on_device(): along_x = [lax.ppermute(state, 'ctx', shift_x(k)) for k in (2, 3, 1)]  5.2 us
  transfers between devices with their start and end apart: 18, of which 8 were waited for; matrix products, arithmetic and copies ran while one was open for 0% of the time, Pallas kernels for 49%

profile of v5, /device:TPU:0, one launch (start us, length us, event | category | flops | bytes accessed | tf_op | source)
XLA Modules:
  0.0 105.3 jit_solution(9099285422768835116)
XLA Ops:
  0.0 3.8 %local_states.1.after_ref = bf16[1024,128]{1,0:T(8,128)(2,1)S(1)} custom-call(bf16[1024,1024]{1,0:T(8,128)(2,1)} %k_ref.3, bf16[1024,1024]{1,0:T(8,128)(2,1)} %v_ref.3), custom_call_target="tpu_custom_call" | custom-call | flops 1 | bytes 1 | tf_op jit(solution)/shard_map/local_states/pallas_call | solution.py:76
  3.8 1.6 %collective-permute-start.2 = (bf16[1024,128]{1,0:T(8,128)(2,1)S(1)}, bf16[1024,128]{1,0:T(8,128)(2,1)S(1)}, u32[]{:S(2)}, u32[]{:S(2)}) collective-permute-start(bf16[1024,128]{1,0:T(8,128)(2,1)S(1)} %local_states.1.after_ref), channel_id=1, source_target_pairs={{0,8},{8,16},{16,24},{24,0},{32,40},{40,48},{48,56},{56,32},{64,72... | collective-permute-start | bytes 786440 | tf_op jit(solution)/shard_map/ppermute | solution.py:307
  5.4 1.7 %collective-permute-start.1 = (bf16[1024,128]{1,0:T(8,128)(2,1)S(1)}, bf16[1024,128]{1,0:T(8,128)(2,1)S(1)}, u32[]{:S(2)}, u32[]{:S(2)}) collective-permute-start(bf16[1024,128]{1,0:T(8,128)(2,1)S(1)} %local_states.1.after_ref), channel_id=1, source_target_pairs={{0,24},{8,0},{16,8},{24,16},{32,56},{40,32},{48,40},{56,48},{64,88... | collective-permute-start | bytes 786440 | tf_op jit(solution)/shard_map/ppermute | solution.py:307
  7.1 1.9 %collective-permute-start = (bf16[1024,128]{1,0:T(8,128)(2,1)S(1)}, bf16[1024,128]{1,0:T(8,128)(2,1)S(1)}, u32[]{:S(2)}, u32[]{:S(2)}) collective-permute-start(bf16[1024,128]{1,0:T(8,128)(2,1)S(1)} %local_states.1.after_ref), channel_id=1, source_target_pairs={{0,16},{8,24},{16,0},{24,8},{32,48},{40,56},{48,32},{56,40},{64,80... | collective-permute-start | bytes 786440 | tf_op jit(solution)/shard_map/ppermute | solution.py:307
  9.0 0.1 stack.35.blocks_ref
  9.1 11.5 %sort_columns.1 = (bf16[1,1024,768]{2,1,0:T(8,128)(2,1)}, bf16[3,1024,768]{2,1,0:T(8,128)(2,1)}, bf16[4,1024,768]{2,1,0:T(8,128)(2,1)}) custom-call(s32[8]{0:T(128)S(1)} %stack.35.blocks_ref, bf16[1024,6144]{1,0:T(8,128)(2,1)} %weight_ref.1, bf16[1024,128]{1,0:T(8,128)(2,1)S(1)} %local_states.1.after_ref), custom_call_target="tpu_custom_call" | custom-call | flops 1 | bytes 1 | tf_op jit(solution)/shard_map/sort_columns/pallas_call | solution.py:165
  20.6 0.0 collective-permute-start.9
  20.6 0.5 collective-permute-start.6
  21.1 0.0 collective-permute-done.2
  21.1 0.0 collective-permute-done.1
  21.1 0.0 collective-permute-done
  21.1 0.2 fusion.2
  21.4 0.0 copy-start.1
  21.4 0.0 copy-start.2
  21.4 4.0 %collective-permute-start.5 = (bf16[1024,128]{1,0:T(8,128)(2,1)S(1)}, bf16[1024,128]{1,0:T(8,128)(2,1)S(1)}, u32[]{:S(2)}, u32[]{:S(2)}) collective-permute-start(bf16[1024,128]{1,0:T(8,128)(2,1)S(1)} %get-tuple-element.43), channel_id=1, source_target_pairs={{0,32},{8,40},{16,48},{24,56},{32,64},{40,72},{48,80},{56,88},{64,... | collective-permute-start | bytes 786440 | tf_op jit(solution)/shard_map/ppermute | solution.py:320
  25.4 3.4 %collective-permute-start.4 = (bf16[1024,128]{1,0:T(8,128)(2,1)S(1)}, bf16[1024,128]{1,0:T(8,128)(2,1)S(1)}, u32[]{:S(2)}, u32[]{:S(2)}) collective-permute-start(bf16[1024,128]{1,0:T(8,128)(2,1)S(1)} %get-tuple-element.43), channel_id=1, source_target_pairs={{0,96},{8,104},{16,112},{24,120},{1,97},{9,105},{17,113},{25,121},... | collective-permute-start | bytes 786440 | tf_op jit(solution)/shard_map/ppermute | solution.py:320
  28.8 2.8 %collective-permute-start.3 = (bf16[1024,128]{1,0:T(8,128)(2,1)S(1)}, bf16[1024,128]{1,0:T(8,128)(2,1)S(1)}, u32[]{:S(2)}, u32[]{:S(2)}) collective-permute-start(bf16[1024,128]{1,0:T(8,128)(2,1)S(1)} %get-tuple-element.43), channel_id=1, source_target_pairs={{0,64},{8,72},{16,80},{24,88},{32,96},{40,104},{48,112},{56,120},{... | collective-permute-start | bytes 786440 | tf_op jit(solution)/shard_map/ppermute | solution.py:320
  31.6 7.0 %intra_block.1 = (f32[1024,1024]{1,0:T(8,128)S(1)}, bf16[1024,1024]{1,0:T(8,128)(2,1)S(1)}) custom-call(bf16[1024,1024]{1,0:T(8,128)(2,1)} %q_ref.1, bf16[1024,1024]{1,0:T(8,128)(2,1)} %k_ref.3, bf16[1024,1024]{1,0:T(8,128)(2,1)} %v_ref.3, bf16[1024,128]{1,0:T(8,128)(2,1)S(1)} %local_states.1.after_ref), custom_call_target="tpu_custom_call" | custom-call | flops 99999997952 | bytes 1 | tf_op jit(solution)/shard_map/intra_block/pallas_call | solution.py:131
  38.6 0.0 collective-permute-done.5.refs_7_
  38.6 1.5 %collective-permute-done.4.refs_6_ = bf16[1024,128]{1,0:T(8,128)(2,1)S(1)} collective-permute-done((bf16[1024,128]{1,0:T(8,128)(2,1)S(1)}, bf16[1024,128]{1,0:T(8,128)(2,1)S(1)}, u32[]{:S(2)}, u32[]{:S(2)}) %collective-permute-start.4) | collective-permute-done | bytes 262176 | tf_op jit(solution)/shard_map/ppermute | solution.py:320
  40.1 0.0 collective-permute-done.3.refs_5_
  40.1 0.0 collective-permute-done.6.refs_8_.refs_5_
  40.1 0.0 copy-done.1
  40.1 0.0 copy-done.2
  40.1 1.4 %hidden_rows.2.refs_8_.refs_0_ = bf16[512,1024]{1,0:T(8,128)(2,1)S(1)} custom-call(f32[1024,1024]{1,0:T(8,128)S(1)} %get-tuple-element.26.refs_0_, bf16[1024,1024]{1,0:T(8,128)(2,1)S(1)} %get-tuple-element.27.refs_1_, bf16[1024,1024]{1,0:T(8,128)(2,1)S(1)} %copy-done.1, f32[1,1024]{1,0:T(1,128)S(1)} %bitcast.9, f32[1024,128]{1,0:T(8,128)S(1)} %get-tuple-element.44.refs_4_, ...), custom_call_target="tpu_custom_call" | custom-call | flops 1 | bytes 1 | tf_op jit(solution)/shard_map/hidden_rows/pallas_call | solution.py:226
  41.5 0.0 copy-start
  41.5 0.1 collective-permute-start.7
  41.6 1.4 %hidden_rows.3.refs_4_.refs_0_.refs_1_ = bf16[512,1024]{1,0:T(8,128)(2,1)S(1)} custom-call(f32[1024,1024]{1,0:T(8,128)S(1)} %get-tuple-element.26.refs_0_, bf16[1024,1024]{1,0:T(8,128)(2,1)S(1)} %get-tuple-element.27.refs_1_, bf16[1024,1024]{1,0:T(8,128)(2,1)S(1)} %copy-done.1, f32[1,1024]{1,0:T(1,128)S(1)} %bitcast.10, ...), custom_call_target="tpu_custom_call" | custom-call | flops 1 | bytes 1 | tf_op jit(solution)/shard_map/hidden_rows/pallas_call | solution.py:226
  43.0 0.6 collective-permute-start.8
  43.5 0.0 collective-permute-done.9.refs_3_
  43.5 0.7 collective-permute-done.7.refs_1_.refs_2_
  44.2 0.0 copy-done
  44.3 2.8 %share_far.2 = (bf16[256,768]{1,0:T(8,128)(2,1)S(1)}, bf16[256,768]{1,0:T(8,128)(2,1)S(1)}) custom-call(bf16[512,1024]{1,0:T(8,128)(2,1)S(1)} %hidden_rows.2.refs_8_.refs_0_, bf16[512,1024]{1,0:T(8,128)(2,1)S(1)} %collective-permute-done.7.refs_1_.refs_2_, bf16[4,1024,768]{2,1,0:T(8,128)(2,1)S(1)} %copy-done, ...), custom_call_target="tpu_custom_call" | custom-call | flops 99999997952 | bytes 1 | tf_op jit(solution)/shard_map/share_far/pallas_call | solution.py:265
  47.0 3.1 %collective-permute-start.11 = (bf16[256,768]{1,0:T(8,128)(2,1)S(1)}, bf16[256,768]{1,0:T(8,128)(2,1)S(1)}, u32[]{:S(2)}, u32[]{:S(2)}) collective-permute-start(bf16[256,768]{1,0:T(8,128)(2,1)S(1)} %get-tuple-element.35), channel_id=1, source_target_pairs={{0,6},{1,7},{2,0},{3,1},{4,2},{5,3},{6,4},{7,5},{8,14},{9,15},{10,... | collective-permute-start | bytes 1179656 | tf_op jit(solution)/shard_map/ppermute | solution.py:324
  50.1 0.0 collective-permute-start.10
  50.1 0.0 collective-permute-done.8.refs_1_.refs_3_
  50.1 2.7 %share_far.3 = (bf16[256,768]{1,0:T(8,128)(2,1)S(1)}, bf16[256,768]{1,0:T(8,128)(2,1)S(1)}) custom-call(bf16[512,1024]{1,0:T(8,128)(2,1)S(1)} %hidden_rows.3.refs_4_.refs_0_.refs_1_, bf16[512,1024]{1,0:T(8,128)(2,1)S(1)} %collective-permute-done.8.refs_1_.refs_3_, bf16[4,1024,768]{2,1,0:T(8,128)(2,1)S(1)} %copy-done, ...), custom_call_target="tpu_custom_call" | custom-call | flops 1 | bytes 1 | tf_op jit(solution)/shard_map/share_far/pallas_call | solution.py:265
  52.9 3.3 %collective-permute-start.15 = (bf16[256,768]{1,0:T(8,128)(2,1)S(1)}, bf16[256,768]{1,0:T(8,128)(2,1)S(1)}, u32[]{:S(2)}, u32[]{:S(2)}) collective-permute-start(bf16[256,768]{1,0:T(8,128)(2,1)S(1)} %get-tuple-element.38), channel_id=1, source_target_pairs={{0,6},{1,7},{2,0},{3,1},{4,2},{5,3},{6,4},{7,5},{8,14},{9,15},{10,... | collective-permute-start | bytes 1179656 | tf_op jit(solution)/shard_map/ppermute | solution.py:324
  56.2 0.0 collective-permute-start.14
  56.2 7.9 %share_near.1 = (bf16[512,768]{1,0:T(8,128)(2,1)S(1)}, bf16[512,768]{1,0:T(8,128)(2,1)S(1)}) custom-call(bf16[512,1024]{1,0:T(8,128)(2,1)S(1)} %hidden_rows.2.refs_8_.refs_0_, bf16[512,1024]{1,0:T(8,128)(2,1)S(1)} %hidden_rows.3.refs_4_.refs_0_.refs_1_, bf16[512,1024]{1,0:T(8,128)(2,1)S(1)} %collective-permute-done.7.refs_1_.refs_2_, ...), custom_call_target="tpu_custom_call" | custom-call | flops 1 | bytes 1 | tf_op jit(solution)/shard_map/share_near/pallas_call | solution.py:265
  64.1 0.0 collective-permute-done.11.refs_3_.refs_8_
  64.1 0.0 collective-permute-done.10.refs_2_.refs_6_
  64.1 3.3 %collective-permute-start.12 = (bf16[512,768]{1,0:T(8,128)(2,1)S(1)}, bf16[512,768]{1,0:T(8,128)(2,1)S(1)}, u32[]{:S(2)}, u32[]{:S(2)}) collective-permute-start(bf16[512,768]{1,0:T(8,128)(2,1)S(1)} %get-tuple-element.36), channel_id=1, source_target_pairs={{0,6},{1,7},{2,0},{3,1},{4,2},{5,3},{6,4},{7,5},{8,14},{9,15},{10,... | collective-permute-start | bytes 2359304 | tf_op jit(solution)/shard_map/ppermute | solution.py:324
  67.4 0.0 collective-permute-start.13
  67.4 0.4 collective-permute-done.15.refs_9_
  67.8 3.4 %collective-permute-done.14.refs_7_ = bf16[256,768]{1,0:T(8,128)(2,1)S(1)} collective-permute-done((bf16[256,768]{1,0:T(8,128)(2,1)S(1)}, bf16[256,768]{1,0:T(8,128)(2,1)S(1)}, u32[]{:S(2)}, u32[]{:S(2)}) %collective-permute-start.14) | collective-permute-done | bytes 393248 | tf_op jit(solution)/shard_map/ppermute | solution.py:323
  71.2 7.8 %share_passing.1 = (bf16[512,768]{1,0:T(8,128)(2,1)S(1)}, bf16[512,768]{1,0:T(8,128)(2,1)S(1)}) custom-call(bf16[512,1024]{1,0:T(8,128)(2,1)S(1)} %hidden_rows.2.refs_8_.refs_0_, bf16[512,1024]{1,0:T(8,128)(2,1)S(1)} %hidden_rows.3.refs_4_.refs_0_.refs_1_, bf16[512,1024]{1,0:T(8,128)(2,1)S(1)} %collective-permute-done.7.refs_1_.refs_2_, ...), custom_call_target="tpu_custom_call" | custom-call | flops 99999997952 | bytes 1 | tf_op jit(solution)/shard_map/share_passing/pallas_call | solution.py:265
  79.1 0.4 collective-permute-start.17
  79.4 1.7 %collective-permute-start.16 = (bf16[512,768]{1,0:T(8,128)(2,1)S(1)}, bf16[512,768]{1,0:T(8,128)(2,1)S(1)}, u32[]{:S(2)}, u32[]{:S(2)}) collective-permute-start(bf16[512,768]{1,0:T(8,128)(2,1)S(1)} %get-tuple-element.39.refs_8_), channel_id=1, source_target_pairs={{0,2},{1,3},{2,4},{3,5},{4,6},{5,7},{6,0},{7,1},{8,10},{9,11},{10,... | collective-permute-start | bytes 2359304 | tf_op jit(solution)/shard_map/ppermute | solution.py:323
  81.2 4.2 %collective-permute-done.12.refs_6_ = bf16[512,768]{1,0:T(8,128)(2,1)S(1)} collective-permute-done((bf16[512,768]{1,0:T(8,128)(2,1)S(1)}, bf16[512,768]{1,0:T(8,128)(2,1)S(1)}, u32[]{:S(2)}, u32[]{:S(2)}) %collective-permute-start.12) | collective-permute-done | bytes 786464 | tf_op jit(solution)/shard_map/ppermute | solution.py:324
  85.4 3.7 %collective-permute-done.13.refs_7_ = bf16[512,768]{1,0:T(8,128)(2,1)S(1)} collective-permute-done((bf16[512,768]{1,0:T(8,128)(2,1)S(1)}, bf16[512,768]{1,0:T(8,128)(2,1)S(1)}, u32[]{:S(2)}, u32[]{:S(2)}) %collective-permute-start.13) | collective-permute-done | bytes 786464 | tf_op jit(solution)/shard_map/ppermute | solution.py:323
  89.1 7.9 %share_own.1 = (f32[512,768]{1,0:T(8,128)S(1)}, f32[512,768]{1,0:T(8,128)S(1)}) custom-call(bf16[512,1024]{1,0:T(8,128)(2,1)S(1)} %hidden_rows.2.refs_8_.refs_0_, bf16[512,1024]{1,0:T(8,128)(2,1)S(1)} %hidden_rows.3.refs_4_.refs_0_.refs_1_, bf16[512,1024]{1,0:T(8,128)(2,1)S(1)} %collective-permute-done.7.refs_1_.refs_2_, ...), custom_call_target="tpu_custom_call" | custom-call | flops 1 | bytes 1 | tf_op jit(solution)/shard_map/share_own/pallas_call | solution.py:265
  97.0 3.9 %collective-permute-done.17.add_ref = bf16[512,768]{1,0:T(8,128)(2,1)S(1)} collective-permute-done((bf16[512,768]{1,0:T(8,128)(2,1)S(1)}, bf16[512,768]{1,0:T(8,128)(2,1)S(1)}, u32[]{:S(2)}, u32[]{:S(2)}) %collective-permute-start.17) | collective-permute-done | bytes 786464 | tf_op jit(solution)/shard_map/ppermute | solution.py:324
  100.9 1.0 finish.2.refs_0_
  101.9 2.4 %collective-permute-done.16.add_ref = bf16[512,768]{1,0:T(8,128)(2,1)S(1)} collective-permute-done((bf16[512,768]{1,0:T(8,128)(2,1)S(1)}, bf16[512,768]{1,0:T(8,128)(2,1)S(1)}, u32[]{:S(2)}, u32[]{:S(2)}) %collective-permute-start.16) | collective-permute-done | bytes 786464 | tf_op jit(solution)/shard_map/ppermute | solution.py:323
  104.3 1.0 finish.3
  (1 shorter events, 0.0 us)
Async XLA Ops:
  3.8 17.3 %collective-permute-start.2 = (bf16[1024,128]{1,0:T(8,128)(2,1)S(1)}, bf16[1024,128]{1,0:T(8,128)(2,1)S(1)}, u32[]{:S(2)}, u32[]{:S(2)}) collective-permute-start(bf16[1024,128]{1,0:T(8,128)(2,1)S(1)} %local_states.1.after_ref), channel_id=1, source_target_pairs={{0,8},{8,16},{16,24},{24,0},{32,40},{40,48},{48,56},{56,32},{64,72... | collective-permute-start | bytes 786440 | tf_op jit(solution)/shard_map/ppermute | solution.py:307
  5.4 15.7 %collective-permute-start.1 = (bf16[1024,128]{1,0:T(8,128)(2,1)S(1)}, bf16[1024,128]{1,0:T(8,128)(2,1)S(1)}, u32[]{:S(2)}, u32[]{:S(2)}) collective-permute-start(bf16[1024,128]{1,0:T(8,128)(2,1)S(1)} %local_states.1.after_ref), channel_id=1, source_target_pairs={{0,24},{8,0},{16,8},{24,16},{32,56},{40,32},{48,40},{56,48},{64,88... | collective-permute-start | bytes 786440 | tf_op jit(solution)/shard_map/ppermute | solution.py:307
  7.1 14.0 %collective-permute-start = (bf16[1024,128]{1,0:T(8,128)(2,1)S(1)}, bf16[1024,128]{1,0:T(8,128)(2,1)S(1)}, u32[]{:S(2)}, u32[]{:S(2)}) collective-permute-start(bf16[1024,128]{1,0:T(8,128)(2,1)S(1)} %local_states.1.after_ref), channel_id=1, source_target_pairs={{0,16},{8,24},{16,0},{24,8},{32,48},{40,56},{48,32},{56,40},{64,80... | collective-permute-start | bytes 786440 | tf_op jit(solution)/shard_map/ppermute | solution.py:307
  20.6 22.9 %collective-permute-start.9 = (bf16[1,1024,768]{2,1,0:T(8,128)(2,1)}, bf16[1,1024,768]{2,1,0:T(8,128)(2,1)S(1)}, u32[]{:S(2)}, u32[]{:S(2)}) collective-permute-start(bf16[1,1024,768]{2,1,0:T(8,128)(2,1)} %get-tuple-element.30), channel_id=1, source_target_pairs={{0,1},{1,0},{2,3},{3,2},{4,5},{5,4},{6,7},{7,6},{8,9},{9,8},{10,11... | collective-permute-start | bytes 4718600 | tf_op jit(solution)/shard_map/ppermute | solution.py:309
  20.6 19.5 %collective-permute-start.6 = (bf16[3,1024,768]{2,1,0:T(8,128)(2,1)}, bf16[3,1024,768]{2,1,0:T(8,128)(2,1)}, u32[]{:S(2)}, u32[]{:S(2)}) collective-permute-start(bf16[3,1024,768]{2,1,0:T(8,128)(2,1)} %get-tuple-element.28), channel_id=1, source_target_pairs={{0,1},{1,0},{2,3},{3,2},{4,5},{5,4},{6,7},{7,6},{8,9},{9,8},{10,11... | collective-permute-start | bytes 14155784 | tf_op jit(solution)/shard_map/ppermute | solution.py:309
  21.4 18.8 %copy-start.1 = (bf16[1024,1024]{1,0:T(8,128)(2,1)S(1)}, bf16[1024,1024]{1,0:T(8,128)(2,1)}, u32[]{:S(2)}) copy-start(bf16[1024,1024]{1,0:T(8,128)(2,1)} %refs_2_.3) | copy-start | bytes 6291460
  21.4 18.7 %copy-start.2 = (f32[1024]{0:T(1024)S(1)}, f32[1024]{0:T(1024)}, u32[]{:S(2)}) copy-start(f32[1024]{0:T(1024)} %param.10) | copy-start | bytes 12292
  21.4 17.2 %collective-permute-start.5 = (bf16[1024,128]{1,0:T(8,128)(2,1)S(1)}, bf16[1024,128]{1,0:T(8,128)(2,1)S(1)}, u32[]{:S(2)}, u32[]{:S(2)}) collective-permute-start(bf16[1024,128]{1,0:T(8,128)(2,1)S(1)} %get-tuple-element.43), channel_id=1, source_target_pairs={{0,32},{8,40},{16,48},{24,56},{32,64},{40,72},{48,80},{56,88},{64,... | collective-permute-start | bytes 786440 | tf_op jit(solution)/shard_map/ppermute | solution.py:320
  25.4 14.7 %collective-permute-start.4 = (bf16[1024,128]{1,0:T(8,128)(2,1)S(1)}, bf16[1024,128]{1,0:T(8,128)(2,1)S(1)}, u32[]{:S(2)}, u32[]{:S(2)}) collective-permute-start(bf16[1024,128]{1,0:T(8,128)(2,1)S(1)} %get-tuple-element.43), channel_id=1, source_target_pairs={{0,96},{8,104},{16,112},{24,120},{1,97},{9,105},{17,113},{25,121},... | collective-permute-start | bytes 786440 | tf_op jit(solution)/shard_map/ppermute | solution.py:320
  28.8 11.3 %collective-permute-start.3 = (bf16[1024,128]{1,0:T(8,128)(2,1)S(1)}, bf16[1024,128]{1,0:T(8,128)(2,1)S(1)}, u32[]{:S(2)}, u32[]{:S(2)}) collective-permute-start(bf16[1024,128]{1,0:T(8,128)(2,1)S(1)} %get-tuple-element.43), channel_id=1, source_target_pairs={{0,64},{8,72},{16,80},{24,88},{32,96},{40,104},{48,112},{56,120},{... | collective-permute-start | bytes 786440 | tf_op jit(solution)/shard_map/ppermute | solution.py:320
  41.5 2.8 %copy-start = (bf16[4,1024,768]{2,1,0:T(8,128)(2,1)S(1)}, bf16[4,1024,768]{2,1,0:T(8,128)(2,1)}, u32[]{:S(2)}) copy-start(bf16[4,1024,768]{2,1,0:T(8,128)(2,1)} %get-tuple-element.29.refs_2_.refs_4_) | copy-start | bytes 18874372
  41.5 2.7 %collective-permute-start.7 = (bf16[512,1024]{1,0:T(8,128)(2,1)S(1)}, bf16[512,1024]{1,0:T(8,128)(2,1)S(1)}, u32[]{:S(2)}, u32[]{:S(2)}) collective-permute-start(bf16[512,1024]{1,0:T(8,128)(2,1)S(1)} %hidden_rows.2.refs_8_.refs_0_), channel_id=1, source_target_pairs={{0,1},{1,0},{2,3},{3,2},{4,5},{5,4},{6,7},{7,6},{8,9},{9,8},{10,11... | collective-permute-start | bytes 3145736 | tf_op jit(solution)/shard_map/ppermute | solution.py:309
  43.0 7.2 %collective-permute-start.8 = (bf16[512,1024]{1,0:T(8,128)(2,1)S(1)}, bf16[512,1024]{1,0:T(8,128)(2,1)S(1)}, u32[]{:S(2)}, u32[]{:S(2)}) collective-permute-start(bf16[512,1024]{1,0:T(8,128)(2,1)S(1)} %hidden_rows.3.refs_4_.refs_0_.refs_1_), channel_id=1, source_target_pairs={{0,1},{1,0},{2,3},{3,2},{4,5},{5,4},{6,7},{7,6},{8,9},{9,8},{10,11... | collective-permute-start | bytes 3145736 | tf_op jit(solution)/shard_map/ppermute | solution.py:309
  47.0 17.0 %collective-permute-start.11 = (bf16[256,768]{1,0:T(8,128)(2,1)S(1)}, bf16[256,768]{1,0:T(8,128)(2,1)S(1)}, u32[]{:S(2)}, u32[]{:S(2)}) collective-permute-start(bf16[256,768]{1,0:T(8,128)(2,1)S(1)} %get-tuple-element.35), channel_id=1, source_target_pairs={{0,6},{1,7},{2,0},{3,1},{4,2},{5,3},{6,4},{7,5},{8,14},{9,15},{10,... | collective-permute-start | bytes 1179656 | tf_op jit(solution)/shard_map/ppermute | solution.py:324
  50.1 14.0 %collective-permute-start.10 = (bf16[256,768]{1,0:T(8,128)(2,1)S(1)}, bf16[256,768]{1,0:T(8,128)(2,1)S(1)}, u32[]{:S(2)}, u32[]{:S(2)}) collective-permute-start(bf16[256,768]{1,0:T(8,128)(2,1)S(1)} %get-tuple-element.31.refs_4_), channel_id=1, source_target_pairs={{0,2},{1,3},{2,4},{3,5},{4,6},{5,7},{6,0},{7,1},{8,10},{9,11},{10,... | collective-permute-start | bytes 1179656 | tf_op jit(solution)/shard_map/ppermute | solution.py:323
  52.9 14.9 %collective-permute-start.15 = (bf16[256,768]{1,0:T(8,128)(2,1)S(1)}, bf16[256,768]{1,0:T(8,128)(2,1)S(1)}, u32[]{:S(2)}, u32[]{:S(2)}) collective-permute-start(bf16[256,768]{1,0:T(8,128)(2,1)S(1)} %get-tuple-element.38), channel_id=1, source_target_pairs={{0,6},{1,7},{2,0},{3,1},{4,2},{5,3},{6,4},{7,5},{8,14},{9,15},{10,... | collective-permute-start | bytes 1179656 | tf_op jit(solution)/shard_map/ppermute | solution.py:324
  56.2 15.0 %collective-permute-start.14 = (bf16[256,768]{1,0:T(8,128)(2,1)S(1)}, bf16[256,768]{1,0:T(8,128)(2,1)S(1)}, u32[]{:S(2)}, u32[]{:S(2)}) collective-permute-start(bf16[256,768]{1,0:T(8,128)(2,1)S(1)} %get-tuple-element.32.refs_6_), channel_id=1, source_target_pairs={{0,2},{1,3},{2,4},{3,5},{4,6},{5,7},{6,0},{7,1},{8,10},{9,11},{10,... | collective-permute-start | bytes 1179656 | tf_op jit(solution)/shard_map/ppermute | solution.py:323
  64.1 21.3 %collective-permute-start.12 = (bf16[512,768]{1,0:T(8,128)(2,1)S(1)}, bf16[512,768]{1,0:T(8,128)(2,1)S(1)}, u32[]{:S(2)}, u32[]{:S(2)}) collective-permute-start(bf16[512,768]{1,0:T(8,128)(2,1)S(1)} %get-tuple-element.36), channel_id=1, source_target_pairs={{0,6},{1,7},{2,0},{3,1},{4,2},{5,3},{6,4},{7,5},{8,14},{9,15},{10,... | collective-permute-start | bytes 2359304 | tf_op jit(solution)/shard_map/ppermute | solution.py:324
  67.4 21.7 %collective-permute-start.13 = (bf16[512,768]{1,0:T(8,128)(2,1)S(1)}, bf16[512,768]{1,0:T(8,128)(2,1)S(1)}, u32[]{:S(2)}, u32[]{:S(2)}) collective-permute-start(bf16[512,768]{1,0:T(8,128)(2,1)S(1)} %get-tuple-element.37.refs_10_), channel_id=1, source_target_pairs={{0,2},{1,3},{2,4},{3,5},{4,6},{5,7},{6,0},{7,1},{8,10},{9,11},{10,... | collective-permute-start | bytes 2359304 | tf_op jit(solution)/shard_map/ppermute | solution.py:323
  79.1 21.8 %collective-permute-start.17 = (bf16[512,768]{1,0:T(8,128)(2,1)S(1)}, bf16[512,768]{1,0:T(8,128)(2,1)S(1)}, u32[]{:S(2)}, u32[]{:S(2)}) collective-permute-start(bf16[512,768]{1,0:T(8,128)(2,1)S(1)} %get-tuple-element.42), channel_id=1, source_target_pairs={{0,6},{1,7},{2,0},{3,1},{4,2},{5,3},{6,4},{7,5},{8,14},{9,15},{10,... | collective-permute-start | bytes 2359304 | tf_op jit(solution)/shard_map/ppermute | solution.py:324
  79.4 24.9 %collective-permute-start.16 = (bf16[512,768]{1,0:T(8,128)(2,1)S(1)}, bf16[512,768]{1,0:T(8,128)(2,1)S(1)}, u32[]{:S(2)}, u32[]{:S(2)}) collective-permute-start(bf16[512,768]{1,0:T(8,128)(2,1)S(1)} %get-tuple-element.39.refs_8_), channel_id=1, source_target_pairs={{0,2},{1,3},{2,4},{3,5},{4,6},{5,7},{6,0},{7,1},{8,10},{9,11},{10,... | collective-permute-start | bytes 2359304 | tf_op jit(solution)/shard_map/ppermute | solution.py:323
